TPU v7x, 256 devices: a whole 4x4x8 slice. The times are simulated.
256 devices in a mesh: blk: 64 (over y, z, x_hi), split: 4 (over x_lo, core).
Axes of the slice: x: 4 (x_hi: 2, x_lo: 2; x = x_hi * 2 + x_lo), y: 4, z: 8, core: 2. Of those that a mesh axis runs over, the one named last changes fastest.
Arguments:
- points: float32 [32, 262144], P(None, ('blk', 'split')), may hold values from -6 to 6
- vectors: float32 [16, 262144], P(None, ('blk', 'split')), may hold values from -6 to 6
- inv_length: float32 [32], replicated, may hold values from 0.05 to 0.3
- noise: float32 [262144], P(('blk', 'split')), may hold values from 0.5 to 2
Outputs:
- product: float32 [16, 262144], P(None, ('blk', 'split'))
All inputs are finite; a program needn't handle non-finite values.
Results may differ from a plain program's by a relative error of at most 0.0003.
Values sent between devices are 32-bit elements; how exact they have to be, the bound alone decides.
No kernel may reach another device: no remote copies, remote signals or barrier semaphores. Data moves between devices by JAX's collectives and lax.ppermute only.
A program may use at most 64 MiB of HBM per device.

v0:
```python
import functools

import jax
import jax.numpy as jnp
from jax import lax
from jax.experimental import pallas as pl
from jax.experimental.pallas import tpu as pltpu
from jax.sharding import PartitionSpec as P

SIGNAL = 0.03125
ROOT_FIVE = 2.23606797749979
LOG2E = 1.4426950408889634
POINT_SCALE = ROOT_FIVE * LOG2E
OUT_SCALE = SIGNAL / (3.0 * LOG2E * LOG2E)
DIMS = 32
RHS = 16
DEPTH = 256
CHUNK = 512
BF16 = jnp.bfloat16
F32 = jnp.float32


def dot(a, b, ca, cb):
    return lax.dot_general(a, b, (((ca,), (cb,)), ((), ())), preferred_element_type=F32)


def pieces(x):
    hi = x.astype(BF16)
    rest = x - hi.astype(F32)
    mid = rest.astype(BF16)
    lo = (rest - mid.astype(F32)).astype(BF16)
    return hi, mid, lo


def norm_rows(sq, first):
    s1, s2, s3 = (p.astype(F32) for p in pieces(sq))
    row = lax.broadcasted_iota(jnp.int32, (16, sq.shape[1]), 0)
    out = jnp.where(row < 6, 1.0, 0.0)
    for k, s in enumerate((s1, s2, s3)):
        out = jnp.where(row == first + k, s, out)
    return out.astype(BF16)


def features(points, inv_length, rows):
    x = (points * inv_length) * POINT_SCALE
    sq = jnp.sum(x * x, axis=0, keepdims=True)
    hi, mid, lo = pieces(x)
    pad = jnp.zeros((DEPTH - 208, x.shape[1]), BF16)
    if rows:
        two = jnp.asarray(-2.0, BF16)
        hi, mid, lo = hi * two, mid * two, lo * two
        return jnp.concatenate([hi, mid, hi, lo, mid, hi, norm_rows(sq, 0), pad], axis=0)
    return jnp.concatenate([hi, hi, mid, hi, mid, lo, norm_rows(sq, 3), pad], axis=0)


def halves(v):
    hi = v.astype(BF16)
    return jnp.concatenate([hi, (v - hi.astype(F32)).astype(BF16)], axis=0)


def kernel_tile(dist_sq):
    b2 = jnp.maximum(dist_sq, 1e-30)
    b = b2 * lax.rsqrt(b2)
    t = ((b + 3.0 * LOG2E) * b + 3.0 * LOG2E * LOG2E) * jnp.exp2(-b)
    hi = t.astype(BF16)
    return hi, (t - hi.astype(F32)).astype(BF16)


def fold(x):
    return (x[:RHS] + x[RHS:]) * OUT_SCALE


def prep_kernel(count, *refs):
    inv = refs[count][...]
    at_ref, vr_ref = refs[count + 1 :]
    for k in range(count):
        x = refs[k]
        width = x.shape[1]
        f = features(x[:DIMS, :], inv, True)
        at_ref[k * width : (k + 1) * width, :] = f.T
        vr_ref[:, k * width : (k + 1) * width] = halves(x[DIMS:, :])


def tile_kernel(both, at_ref, vr_ref, x_ref, inv_ref, *rest):
    if both:
        fwd_ref, bwd_ref, b_ref, vc_ref, acc_ref = rest
    else:
        bwd_ref, b_ref, vc_ref, acc_ref = rest
    b_ref[...] = features(x_ref[:DIMS, :], inv_ref[...], False)
    vc_ref[...] = halves(x_ref[DIMS:, :])
    acc_ref[...] = jnp.zeros_like(acc_ref)

    def step(i, carry):
        rows = pl.ds(pl.multiple_of(i * CHUNK, CHUNK), CHUNK)
        hi, lo = kernel_tile(dot(at_ref[rows, :], b_ref[...], 1, 0))
        vr = vr_ref[:, rows]
        acc_ref[...] += dot(vr, hi, 1, 0) + dot(vr, lo, 1, 0)
        if both:
            vc = vc_ref[...]
            fwd_ref[:, rows] = fold(dot(vc, hi, 1, 1) + dot(vc, lo, 1, 1))
        return carry

    lax.fori_loop(0, at_ref.shape[0] // CHUNK, step, 0)
    bwd_ref[...] = fold(acc_ref[...])


VMEM = pl.BlockSpec(memory_space=pltpu.VMEM)
PARAMS = pltpu.CompilerParams(vmem_limit_bytes=40 * 2**20)


def prep(xs, inv):
    width = xs[0].shape[1]
    n = len(xs) * width
    return pl.pallas_call(
        functools.partial(prep_kernel, len(xs)),
        out_shape=(
            jax.ShapeDtypeStruct((n, DEPTH), BF16),
            jax.ShapeDtypeStruct((2 * RHS, n), BF16),
        ),
        in_specs=[VMEM] * (len(xs) + 1),
        out_specs=(VMEM, VMEM),
        compiler_params=PARAMS,
        cost_estimate=pl.CostEstimate(flops=n * 2000, bytes_accessed=n * 800, transcendentals=0),
        name="prep",
    )(*xs, inv)


def tiles(at, vr, x, inv, both):
    n, width = at.shape[0], x.shape[1]
    bwd = jax.ShapeDtypeStruct((RHS, width), F32)
    fwd = jax.ShapeDtypeStruct((RHS, n), F32)
    return pl.pallas_call(
        functools.partial(tile_kernel, both),
        out_shape=(fwd, bwd) if both else bwd,
        in_specs=[VMEM] * 4,
        out_specs=(VMEM, VMEM) if both else VMEM,
        scratch_shapes=[
            pltpu.VMEM((DEPTH, width), BF16),
            pltpu.VMEM((2 * RHS, width), BF16),
            pltpu.VMEM((2 * RHS, width), F32),
        ],
        compiler_params=PARAMS,
        cost_estimate=pl.CostEstimate(
            flops=n * width * 2 * DEPTH * (5 if both else 3), bytes_accessed=n * 600, transcendentals=2 * n * width
        ),
        name="both" if both else "own",
    )(at, vr, x, inv)


def shifted(value, steps):
    count = lax.axis_size("blk")
    return lax.ppermute(value, "blk", [(s, (s + steps) % count) for s in range(count)])


def swapped(value, mask):
    count = lax.axis_size("split")
    return lax.ppermute(value, "split", [(s, s ^ mask) for s in range(count)])


def body(points, vectors, inv_length, noise):
    inv = inv_length[:, None]
    own = jnp.concatenate([points, vectors], axis=0)
    far = swapped(own, 2)
    two = shifted(own, 2)
    one = shifted(own, 1)
    at0, vr0 = prep([own], inv)
    total = tiles(at0, vr0, own, inv, False)
    near = swapped(jnp.concatenate([own, far], axis=1), 1)
    width = own.shape[1]
    at2, vr2 = prep([far], inv)
    ata, vra = jnp.concatenate([at0, at2], axis=0), jnp.concatenate([vr0, vr2], axis=1)
    fwd_a2, ret_a2 = tiles(ata, vra, two, inv, True)
    atb, vrb = prep([near], inv)
    fwd_b2, ret_b2 = tiles(atb, vrb, two, inv, True)
    back2 = shifted(ret_a2 + ret_b2, -2)
    fwd_b1, ret_b1 = tiles(atb, vrb, one, inv, True)
    give_near = swapped(fwd_b2 + fwd_b1, 1)
    fwd_a1, ret_a1 = tiles(ata, vra, one, inv, True)
    back1 = shifted(ret_a1 + ret_b1, -1)
    rows = fwd_a2 + fwd_a1 + give_near
    give_far = swapped(rows[:, width:], 2)
    total = total + tiles(atb, vrb, own, inv, False) + tiles(at2, vr2, own, inv, False)
    return total + rows[:, :width] + give_far + back1 + back2 + noise[None, :] * vectors


def solution(mesh):
    placed = (P(None, ("blk", "split")), P(None, ("blk", "split")), P(), P(("blk", "split")))
    return jax.shard_map(
        body, mesh=mesh, in_specs=placed, out_specs=P(None, ("blk", "split")), check_vma=False
    )
```

profile of v0, /device:TPU:1, one launch (start us, length us, event | category | flops | bytes accessed | tf_op | source)
XLA Modules:
  0.0 69.5 jit_solution(16785321490194908924)
XLA Ops:
  0.0 0.9 %constant_dynamic-update-slice_fusion.1 = f32[48,1024]{1,0:T(8,128)S(1)} fusion(f32[32,1024]{1,0:T(8,128)} %param.4), kind=kLoop, calls=%fused_computation.8 | loop fusion | bytes 262144
  1.0 3.7 %collective-permute-start.3 = (f32[48,1024]{1,0:T(8,128)S(1)}, f32[48,1024]{1,0:T(8,128)S(1)}, u32[]{:S(2)}, u32[]{:S(2)}) collective-permute-start(f32[48,1024]{1,0:T(8,128)S(1)} %constant_dynamic-update-slice_fusion.refs_0_.x_ref), channel_id=1, source_target_pairs={{0,4},{4,8},{8,12},{12,16},{16,20},{20,24},{24,28},{28,32},{32,36}... | collective-permute-start | bytes 589832 | tf_op jit(solution)/shard_map/ppermute | solution.py:152
  4.6 1.6 %collective-permute-start.2 = (f32[48,1024]{1,0:T(8,128)S(1)}, f32[48,1024]{1,0:T(8,128)S(1)}, u32[]{:S(2)}, u32[]{:S(2)}) collective-permute-start(f32[48,1024]{1,0:T(8,128)S(1)} %constant_dynamic-update-slice_fusion.refs_0_.x_ref), channel_id=1, source_target_pairs={{0,8},{4,12},{8,16},{12,20},{16,24},{20,28},{24,32},{28,36},{32,40... | collective-permute-start | bytes 589832 | tf_op jit(solution)/shard_map/ppermute | solution.py:152
  6.3 0.3 collective-permute-start
  6.6 0.1 copy.5.refs_1_.inv_ref
  6.7 0.3 prep.3
  7.0 3.0 %own.3 = f32[16,1024]{1,0:T(8,128)S(1)} custom-call(bf16[1024,256]{1,0:T(8,128)(2,1)S(1)} %get-tuple-element.19.at_ref, bf16[32,1024]{1,0:T(8,128)(2,1)S(1)} %get-tuple-element.20.vr_ref, f32[48,1024]{1,0:T(8,128)S(1)} %constant_dynamic-update-slice_fusion.refs_0_.x_ref, f32[32,1]{1,0:T(8,128)S(1)} %copy.5.refs_1_.inv_ref), custom_call_target="tpu_custom_call" | custom-call | flops 1610612736 | bytes 614400 | tf_op jit(solution)/shard_map/own/pallas_call | solution.py:132
  10.0 3.5 %collective-permute-done.refs_0_ = f32[48,1024]{1,0:T(8,128)S(1)} collective-permute-done((f32[48,1024]{1,0:T(8,128)S(1)}, f32[48,1024]{1,0:T(8,128)S(1)}, u32[]{:S(2)}, u32[]{:S(2)}) %collective-permute-start) | collective-permute-done | bytes 196640 | tf_op jit(solution)/shard_map/ppermute | solution.py:157
  13.5 1.6 %collective-permute-start.1 = (f32[48,2048]{1,0:T(8,128)S(1)}, f32[48,2048]{1,0:T(8,128)S(1)}, u32[]{:S(2)}, u32[]{:S(2)}) collective-permute-start(f32[48,2048]{1,0:T(8,128)S(1)} %pad_maximum_fusion), channel_id=1, source_target_pairs={{0,1},{1,0},{2,3},{3,2},{4,5},{5,4},{6,7},{7,6},{8,9},{9,8},{10,11... | collective-permute-start | bytes 1179656 | tf_op jit(solution)/shard_map/ppermute | solution.py:157
  15.1 0.3 prep.5
  15.5 4.2 %collective-permute-done.3.x_ref = f32[48,1024]{1,0:T(8,128)S(1)} collective-permute-done((f32[48,1024]{1,0:T(8,128)S(1)}, f32[48,1024]{1,0:T(8,128)S(1)}, u32[]{:S(2)}, u32[]{:S(2)}) %collective-permute-start.3) | collective-permute-done | bytes 196640 | tf_op jit(solution)/shard_map/ppermute | solution.py:152
  19.7 8.2 %both.5 = (f32[16,2048]{1,0:T(8,128)S(1)}, f32[16,1024]{1,0:T(8,128)S(1)}) custom-call(bf16[2048,256]{1,0:T(8,128)(2,1)S(1)} %constant_dynamic-update-slice_fusion.2.at_ref, bf16[32,2048]{1,0:T(8,128)(2,1)S(1)} %constant_dynamic-update-slice_fusion.4.vr_ref, f32[48,1024]{1,0:T(8,128)S(1)} %collective-permute-done.3.x_ref, f32[32,1]{1,0:T(8,128)S(1)} %copy.5.refs_1_.inv_ref), custom_call_target="tpu_custom_call" | custom-call | flops 5368709120 | bytes 1228800 | tf_op jit(solution)/shard_map/both/pallas_call | solution.py:132
  27.9 0.0 collective-permute-done.2.x_ref
  27.9 8.2 %both.4 = (f32[16,2048]{1,0:T(8,128)S(1)}, f32[16,1024]{1,0:T(8,128)S(1)}) custom-call(bf16[2048,256]{1,0:T(8,128)(2,1)S(1)} %constant_dynamic-update-slice_fusion.2.at_ref, bf16[32,2048]{1,0:T(8,128)(2,1)S(1)} %constant_dynamic-update-slice_fusion.4.vr_ref, f32[48,1024]{1,0:T(8,128)S(1)} %collective-permute-done.2.x_ref, f32[32,1]{1,0:T(8,128)S(1)} %copy.5.refs_1_.inv_ref), custom_call_target="tpu_custom_call" | custom-call | flops 5368709120 | bytes 1228800 | tf_op jit(solution)/shard_map/both/pallas_call | solution.py:132
  36.1 0.4 prep.4
  36.6 8.2 %both.7 = (f32[16,2048]{1,0:T(8,128)S(1)}, f32[16,1024]{1,0:T(8,128)S(1)}) custom-call(bf16[2048,256]{1,0:T(8,128)(2,1)S(1)} %get-tuple-element.21.at_ref, bf16[32,2048]{1,0:T(8,128)(2,1)S(1)} %get-tuple-element.22.vr_ref, f32[48,1024]{1,0:T(8,128)S(1)} %collective-permute-done.3.x_ref, f32[32,1]{1,0:T(8,128)S(1)} %copy.5.refs_1_.inv_ref), custom_call_target="tpu_custom_call" | custom-call | flops 5368709120 | bytes 1228800 | tf_op jit(solution)/shard_map/both/pallas_call | solution.py:132
  44.7 8.2 %both.6 = (f32[16,2048]{1,0:T(8,128)S(1)}, f32[16,1024]{1,0:T(8,128)S(1)}) custom-call(bf16[2048,256]{1,0:T(8,128)(2,1)S(1)} %get-tuple-element.21.at_ref, bf16[32,2048]{1,0:T(8,128)(2,1)S(1)} %get-tuple-element.22.vr_ref, f32[48,1024]{1,0:T(8,128)S(1)} %collective-permute-done.2.x_ref, f32[32,1]{1,0:T(8,128)S(1)} %copy.5.refs_1_.inv_ref), custom_call_target="tpu_custom_call" | custom-call | flops 5368709120 | bytes 1228800 | tf_op jit(solution)/shard_map/both/pallas_call | solution.py:132
  53.0 2.6 %collective-permute-start.4 = (f32[16,2048]{1,0:T(8,128)S(1)}, f32[16,2048]{1,0:T(8,128)S(1)}, u32[]{:S(2)}, u32[]{:S(2)}) collective-permute-start(f32[16,2048]{1,0:T(8,128)S(1)} %add.39), channel_id=1, source_target_pairs={{0,1},{1,0},{2,3},{3,2},{4,5},{5,4},{6,7},{7,6},{8,9},{9,8},{10,11... | collective-permute-start | bytes 393224 | tf_op jit(solution)/shard_map/ppermute | solution.py:157
  55.6 3.0 %own.5 = f32[16,1024]{1,0:T(8,128)S(1)} custom-call(bf16[1024,256]{1,0:T(8,128)(2,1)S(1)} %get-tuple-element.23.at_ref, bf16[32,1024]{1,0:T(8,128)(2,1)S(1)} %get-tuple-element.24.vr_ref, f32[48,1024]{1,0:T(8,128)S(1)} %constant_dynamic-update-slice_fusion.refs_0_.x_ref, f32[32,1]{1,0:T(8,128)S(1)} %copy.5.refs_1_.inv_ref), custom_call_target="tpu_custom_call" | custom-call | flops 1610612736 | bytes 614400 | tf_op jit(solution)/shard_map/own/pallas_call | solution.py:132
  58.6 2.6 %collective-permute-start.6 = (f32[16,1024]{1,0:T(8,128)S(1)}, f32[16,1024]{1,0:T(8,128)S(1)}, u32[]{:S(2)}, u32[]{:S(2)}) collective-permute-start(f32[16,1024]{1,0:T(8,128)S(1)} %add.43), channel_id=1, source_target_pairs={{0,252},{4,0},{8,4},{12,8},{16,12},{20,16},{24,20},{28,24},{32,28}... | collective-permute-start | bytes 196616 | tf_op jit(solution)/shard_map/ppermute | solution.py:152
  61.2 1.7 %collective-permute-start.7 = (f32[16,1024]{1,0:T(8,128)S(1)}, f32[16,1024]{1,0:T(8,128)S(1)}, u32[]{:S(2)}, u32[]{:S(2)}) collective-permute-start(f32[16,1024]{1,0:T(8,128)S(1)} %add.45), channel_id=1, source_target_pairs={{0,248},{4,252},{8,0},{12,4},{16,8},{20,12},{24,16},{28,20},{32,24... | collective-permute-start | bytes 196616 | tf_op jit(solution)/shard_map/ppermute | solution.py:152
  62.9 0.1 collective-permute-start.5
  63.0 5.8 %own.4 = f32[16,1024]{1,0:T(8,128)S(1)} custom-call(bf16[2048,256]{1,0:T(8,128)(2,1)S(1)} %get-tuple-element.21.at_ref, bf16[32,2048]{1,0:T(8,128)(2,1)S(1)} %get-tuple-element.22.vr_ref, f32[48,1024]{1,0:T(8,128)S(1)} %constant_dynamic-update-slice_fusion.refs_0_.x_ref, f32[32,1]{1,0:T(8,128)S(1)} %copy.5.refs_1_.inv_ref), custom_call_target="tpu_custom_call" | custom-call | flops 3221225472 | bytes 1228800 | tf_op jit(solution)/shard_map/own/pallas_call | solution.py:132
  68.8 0.7 fusion.3
  (22 shorter events, 0.2 us)
Async XLA Ops:
  0.0 1.0 %copy-start = (f32[16,1024]{1,0:T(8,128)S(1)}, f32[16,1024]{1,0:T(8,128)}, u32[]{:S(2)}) copy-start(f32[16,1024]{1,0:T(8,128)} %param.5) | copy-start | bytes 196612
  1.0 5.6 %copy-start.2 = (f32[32]{0:T(128)S(1)}, f32[32]{0:T(128)}, u32[]{:S(2)}) copy-start(f32[32]{0:T(128)} %param.6) | copy-start | bytes 388
  1.0 18.7 %collective-permute-start.3 = (f32[48,1024]{1,0:T(8,128)S(1)}, f32[48,1024]{1,0:T(8,128)S(1)}, u32[]{:S(2)}, u32[]{:S(2)}) collective-permute-start(f32[48,1024]{1,0:T(8,128)S(1)} %constant_dynamic-update-slice_fusion.refs_0_.x_ref), channel_id=1, source_target_pairs={{0,4},{4,8},{8,12},{12,16},{16,20},{20,24},{24,28},{28,32},{32,36}... | collective-permute-start | bytes 589832 | tf_op jit(solution)/shard_map/ppermute | solution.py:152
  4.6 23.3 %collective-permute-start.2 = (f32[48,1024]{1,0:T(8,128)S(1)}, f32[48,1024]{1,0:T(8,128)S(1)}, u32[]{:S(2)}, u32[]{:S(2)}) collective-permute-start(f32[48,1024]{1,0:T(8,128)S(1)} %constant_dynamic-update-slice_fusion.refs_0_.x_ref), channel_id=1, source_target_pairs={{0,8},{4,12},{8,16},{12,20},{16,24},{20,28},{24,32},{28,36},{32,40... | collective-permute-start | bytes 589832 | tf_op jit(solution)/shard_map/ppermute | solution.py:152
  6.3 7.2 %collective-permute-start = (f32[48,1024]{1,0:T(8,128)S(1)}, f32[48,1024]{1,0:T(8,128)S(1)}, u32[]{:S(2)}, u32[]{:S(2)}) collective-permute-start(f32[48,1024]{1,0:T(8,128)S(1)} %constant_dynamic-update-slice_fusion.refs_0_.x_ref), channel_id=1, source_target_pairs={{0,2},{1,3},{2,0},{3,1},{4,6},{5,7},{6,4},{7,5},{8,10},{9,11},{10,... | collective-permute-start | bytes 589832 | tf_op jit(solution)/shard_map/ppermute | solution.py:157
  13.5 22.6 %collective-permute-start.1 = (f32[48,2048]{1,0:T(8,128)S(1)}, f32[48,2048]{1,0:T(8,128)S(1)}, u32[]{:S(2)}, u32[]{:S(2)}) collective-permute-start(f32[48,2048]{1,0:T(8,128)S(1)} %pad_maximum_fusion), channel_id=1, source_target_pairs={{0,1},{1,0},{2,3},{3,2},{4,5},{5,4},{6,7},{7,6},{8,9},{9,8},{10,11... | collective-permute-start | bytes 1179656 | tf_op jit(solution)/shard_map/ppermute | solution.py:157
  53.0 9.9 %collective-permute-start.4 = (f32[16,2048]{1,0:T(8,128)S(1)}, f32[16,2048]{1,0:T(8,128)S(1)}, u32[]{:S(2)}, u32[]{:S(2)}) collective-permute-start(f32[16,2048]{1,0:T(8,128)S(1)} %add.39), channel_id=1, source_target_pairs={{0,1},{1,0},{2,3},{3,2},{4,5},{5,4},{6,7},{7,6},{8,9},{9,8},{10,11... | collective-permute-start | bytes 393224 | tf_op jit(solution)/shard_map/ppermute | solution.py:157
  58.6 10.2 %collective-permute-start.6 = (f32[16,1024]{1,0:T(8,128)S(1)}, f32[16,1024]{1,0:T(8,128)S(1)}, u32[]{:S(2)}, u32[]{:S(2)}) collective-permute-start(f32[16,1024]{1,0:T(8,128)S(1)} %add.43), channel_id=1, source_target_pairs={{0,252},{4,0},{8,4},{12,8},{16,12},{20,16},{24,20},{28,24},{32,28}... | collective-permute-start | bytes 196616 | tf_op jit(solution)/shard_map/ppermute | solution.py:152
  61.2 7.6 %collective-permute-start.7 = (f32[16,1024]{1,0:T(8,128)S(1)}, f32[16,1024]{1,0:T(8,128)S(1)}, u32[]{:S(2)}, u32[]{:S(2)}) collective-permute-start(f32[16,1024]{1,0:T(8,128)S(1)} %add.45), channel_id=1, source_target_pairs={{0,248},{4,252},{8,0},{12,4},{16,8},{20,12},{24,16},{28,20},{32,24... | collective-permute-start | bytes 196616 | tf_op jit(solution)/shard_map/ppermute | solution.py:152
  62.9 5.9 %copy-start.1 = (f32[1024]{0:T(1024)S(1)}, f32[1024]{0:T(1024)}, u32[]{:S(2)}) copy-start(f32[1024]{0:T(1024)} %param.7) | copy-start | bytes 12292
  62.9 5.9 %collective-permute-start.5 = (f32[16,1024]{1,0:T(8,128)S(1)}, f32[16,1024]{1,0:T(8,128)S(1)}, u32[]{:S(2)}, u32[]{:S(2)}) collective-permute-start(f32[16,1024]{1,0:T(8,128)S(1)} %slice.9), channel_id=1, source_target_pairs={{0,2},{1,3},{2,0},{3,1},{4,6},{5,7},{6,4},{7,5},{8,10},{9,11},{10,... | collective-permute-start | bytes 196616 | tf_op jit(solution)/shard_map/ppermute | solution.py:157
where the time goes:
time: 69.7 us; the launch traced here: 69.5 us
  Pallas kernels  45.4 us (65%)
  starting transfers between devices  14.2 us (20%)
  waiting for transfers between devices  7.76 us (11%)
  local copies, waits for them, and re-layouts  1.15 us (2%)
  other arithmetic  0.76 us (1%)
    pallas_call x7, Pallas kernels, tiles(): pl.pallas_call(functools.partial(tile_kernel, both), out_shape=(fwd, bwd)...  44.5 us
    ppermute x4, starting transfers between devices, shifted(): lax.ppermute(value, 'blk', [(s, (s + steps) % count) for s in range(count)])  9.52 us
    ppermute x4, starting transfers between devices, swapped(): return lax.ppermute(value, 'split', [(s, s ^ mask) for s in range(count)])  4.66 us
    ppermute x4, waiting for transfers between devices, shifted(): lax.ppermute(value, 'blk', [(s, (s + steps) % count) for s in range(count)])  4.27 us
    ppermute x4, waiting for transfers between devices, swapped(): return lax.ppermute(value, 'split', [(s, s ^ mask) for s in range(count)])  3.5 us
  transfers between devices with their start and end apart: 8, of which 2 were waited for; matrix products, arithmetic and copies ran while one was open for 0% of the time, Pallas kernels for 41%

commit v1 on v0

v1 whole, which is shorter than its diff:
```python
import functools

import jax
import jax.numpy as jnp
from jax import lax
from jax.experimental import pallas as pl
from jax.experimental.pallas import tpu as pltpu
from jax.sharding import PartitionSpec as P

SIGNAL = 0.03125
ROOT_FIVE = 2.23606797749979
LOG2E = 1.4426950408889634
POINT_SCALE = ROOT_FIVE * LOG2E
SHIFT = 1.5 * LOG2E
FLOOR = 0.75 * LOG2E * LOG2E
OUT_SCALE = SIGNAL / (3.0 * LOG2E * LOG2E) * 2.0**SHIFT
DIMS = 32
RHS = 16
DEPTH = 256
TILE = 256
STEP_TILES = 16
BF16 = jnp.bfloat16
F32 = jnp.float32
LOW = jnp.bfloat16


def dot(a, b, ca, cb):
    return lax.dot_general(a, b, (((ca,), (cb,)), ((), ())), preferred_element_type=F32)


def pieces(x):
    hi = x.astype(BF16)
    rest = x - hi.astype(F32)
    mid = rest.astype(BF16)
    lo = (rest - mid.astype(F32)).astype(BF16)
    return hi, mid, lo


def norm_rows(sq, first):
    s1, s2, s3 = (p.astype(F32) for p in pieces(sq))
    row = lax.broadcasted_iota(jnp.int32, (16, sq.shape[1]), 0)
    out = jnp.where(row < 6, 1.0, 0.0)
    for k, s in enumerate((s1, s2, s3)):
        out = jnp.where(row == first + k, s, out)
    return out.astype(BF16)


def features(points, inv_length, rows):
    x = (points * inv_length) * POINT_SCALE
    sq = jnp.sum(x * x, axis=0, keepdims=True)
    hi, mid, lo = pieces(x)
    pad = jnp.zeros((DEPTH - 208, x.shape[1]), BF16)
    if rows:
        two = jnp.asarray(-2.0, BF16)
        hi, mid, lo = hi * two, mid * two, lo * two
        return jnp.concatenate([hi, mid, hi, lo, mid, hi, norm_rows(sq, 0), pad], axis=0)
    return jnp.concatenate([hi, hi, mid, hi, mid, lo, norm_rows(sq, 3), pad], axis=0)


def halves(v, kind):
    hi = v.astype(kind)
    return jnp.concatenate([hi, (v - hi.astype(F32)).astype(kind)], axis=0)


def kernel_tile(dist_sq):
    b2 = jnp.maximum(dist_sq, 1e-30)
    w = -SHIFT - b2 * lax.rsqrt(b2)
    t = (w * w + FLOOR) * jnp.exp2(w)
    hi = t.astype(BF16)
    return hi, (t - hi.astype(F32)).astype(LOW)


def fold(x):
    return (x[:RHS] + x[RHS:]) * OUT_SCALE


def prep_kernel(count, *refs):
    inv = refs[count][...]
    at_ref, v_ref = refs[count + 1 : count + 3]
    for k in range(count):
        x = refs[k]
        width = x.shape[1]
        at_ref[k * width : (k + 1) * width, :] = features(x[:DIMS, :], inv, True).T
        v_ref[:, k * width : (k + 1) * width] = x[DIMS:, :]


def first_kernel(points_ref, vectors_ref, inv_ref, x_ref, at_ref):
    points = points_ref[...]
    x_ref[:DIMS, :] = points
    x_ref[DIMS:, :] = vectors_ref[...]
    at_ref[...] = features(points, inv_ref[...], True).T


def tile_kernel(both, count, at_ref, v_ref, inv_ref, *rest):
    xs = rest[:count]
    if both:
        fwd_ref, bwd_ref, b_ref, vr_ref, vc_ref, facc_ref, acc_ref, d_ref, hi_ref, lo_ref = rest[count:]
    else:
        bwd_ref, b_ref, vr_ref, acc_ref, d_ref, hi_ref, lo_ref = rest[count:]
    rows = at_ref.shape[0]
    for k, x in enumerate(xs):
        width = x.shape[1]
        cols = slice(k * width, (k + 1) * width)
        b_ref[:, cols] = features(x[:DIMS, :], inv_ref[...], False)
        if both:
            vc_ref[:, cols] = halves(x[DIMS:, :], BF16)
    vr_ref[...] = halves(v_ref[...], BF16)
    acc_ref[...] = jnp.zeros_like(acc_ref)
    if both:
        facc_ref[...] = jnp.zeros_like(facc_ref)
    across = count * width // TILE
    down = STEP_TILES // across
    chunks = rows // TILE

    def span(i):
        return pl.ds(pl.multiple_of(i * TILE, TILE), TILE)

    def distances(i, j):
        return dot(at_ref[span(i), :], b_ref[:, j * TILE : (j + 1) * TILE], 1, 0)

    def products(hi, lo, i, j):
        cols = slice(j * TILE, (j + 1) * TILE)
        vr = vr_ref[:, span(i)]
        acc_ref[:, cols] += dot(vr, hi, 1, 0) + dot(vr, lo, 1, 0)
        if both:
            vc = vc_ref[:, cols]
            facc_ref[:, span(i)] += dot(vc, hi, 1, 1) + dot(vc, lo, 1, 1)

    hi_ref[...] = jnp.zeros_like(hi_ref)
    lo_ref[...] = jnp.zeros_like(lo_ref)
    d_ref[...] = distances(0, 0)

    def step(k, carry):
        now, hi, lo = d_ref[...], hi_ref[...], lo_ref[...]
        i, j = jnp.maximum(k * down - 1, 0), across - 1
        for t in range(STEP_TILES):
            ahead = k * down + (t + 1) // across
            if t == STEP_TILES - 1:
                ahead = jnp.where(ahead < chunks, ahead, 0)
            later = distances(ahead, (t + 1) % across)
            products(hi, lo, i, j)
            hi, lo = kernel_tile(now)
            now, i, j = later, k * down + t // across, t % across
        d_ref[...], hi_ref[...], lo_ref[...] = now, hi, lo
        return carry

    lax.fori_loop(0, chunks // down, step, 0)
    products(hi_ref[...], lo_ref[...], chunks - 1, across - 1)
    bwd_ref[...] = fold(acc_ref[...])
    if both:
        fwd_ref[...] = fold(facc_ref[...])


VMEM = pl.BlockSpec(memory_space=pltpu.VMEM)
PARAMS = pltpu.CompilerParams(vmem_limit_bytes=40 * 2**20)


def first(points, vectors, inv):
    width = points.shape[1]
    return pl.pallas_call(
        first_kernel,
        out_shape=(
            jax.ShapeDtypeStruct((DIMS + RHS, width), F32),
            jax.ShapeDtypeStruct((width, DEPTH), BF16),
        ),
        in_specs=[VMEM] * 3,
        out_specs=(VMEM, VMEM),
        compiler_params=PARAMS,
        cost_estimate=pl.CostEstimate(flops=width * 2000, bytes_accessed=width * 800, transcendentals=0),
        name="first",
    )(points, vectors, inv)


def prep(xs, inv):
    width = xs[0].shape[1]
    n = len(xs) * width
    return pl.pallas_call(
        functools.partial(prep_kernel, len(xs)),
        out_shape=(
            jax.ShapeDtypeStruct((n, DEPTH), BF16),
            jax.ShapeDtypeStruct((RHS, n), F32),
        ),
        in_specs=[VMEM] * (len(xs) + 1),
        out_specs=(VMEM, VMEM),
        compiler_params=PARAMS,
        cost_estimate=pl.CostEstimate(flops=n * 2000, bytes_accessed=n * 800, transcendentals=0),
        name="prep",
    )(*xs, inv)


def tiles(at, v, inv, xs, both):
    n, width = at.shape[0], len(xs) * xs[0].shape[1]
    bwd = jax.ShapeDtypeStruct((RHS, width), F32)
    fwd = jax.ShapeDtypeStruct((RHS, n), F32)
    across = [pltpu.VMEM((2 * RHS, width), BF16)] if both else []
    total = [pltpu.VMEM((2 * RHS, n), F32)] if both else []
    return pl.pallas_call(
        functools.partial(tile_kernel, both, len(xs)),
        out_shape=(fwd, bwd) if both else bwd,
        in_specs=[VMEM] * (3 + len(xs)),
        out_specs=(VMEM, VMEM) if both else VMEM,
        scratch_shapes=[pltpu.VMEM((DEPTH, width), BF16), pltpu.VMEM((2 * RHS, n), BF16)]
        + across
        + total
        + [
            pltpu.VMEM((2 * RHS, width), F32),
            pltpu.VMEM((TILE, TILE), F32),
            pltpu.VMEM((TILE, TILE), BF16),
            pltpu.VMEM((TILE, TILE), LOW),
        ],
        compiler_params=PARAMS,
        cost_estimate=pl.CostEstimate(
            flops=n * width * 2 * DEPTH * (5 if both else 3), bytes_accessed=n * 600, transcendentals=2 * n * width
        ),
        name="both" if both else "own",
    )(at, v, inv, *xs)


def shifted(value, steps):
    count = lax.axis_size("blk")
    return lax.ppermute(value, "blk", [(s, (s + steps) % count) for s in range(count)])


def swapped(value, mask):
    count = lax.axis_size("split")
    return lax.ppermute(value, "split", [(s, s ^ mask) for s in range(count)])


def body(points, vectors, inv_length, noise):
    inv = inv_length[:, None]
    own, at0 = first(points, vectors, inv)
    far = swapped(own, 2)
    two = shifted(own, 2)
    one = shifted(own, 1)
    total = tiles(at0, vectors, inv, [own], False)
    near = swapped(jnp.concatenate([own, far], axis=1), 1)
    width = own.shape[1]
    at2, v2 = prep([far], inv)
    ata, va = jnp.concatenate([at0, at2], axis=0), jnp.concatenate([vectors, v2], axis=1)
    fwd_a, ret_a = tiles(ata, va, inv, [two, one], True)
    atb, vb = prep([near], inv)
    fwd_b, ret_b = tiles(atb, vb, inv, [two, one], True)
    give_near = swapped(fwd_b, 1)
    ret = ret_a + ret_b
    back2 = shifted(ret[:, :width], -2)
    back1 = shifted(ret[:, width:], -1)
    rows = fwd_a + give_near
    give_far = swapped(rows[:, width:], 2)
    total = total + tiles(atb, vb, inv, [own], False) + tiles(at2, v2, inv, [own], False)
    return total + rows[:, :width] + give_far + back1 + back2 + noise[None, :] * vectors


def solution(mesh):
    placed = (P(None, ("blk", "split")), P(None, ("blk", "split")), P(), P(("blk", "split")))
    return jax.shard_map(
        body, mesh=mesh, in_specs=placed, out_specs=P(None, ("blk", "split")), check_vma=False
    )
```

time: 69.7 us -> 58.7 us (0.84)
  Pallas kernels: 45.4 us -> 32.2 us
  local copies, waits for them, and re-layouts: 1.15 us -> 3.35 us
    pallas_call x7 -> x6, Pallas kernels: 44.5 us -> 31.5 us  [the longest x5 31.2 us: tiles(): pl.pallas_call(functools.partial(tile_kernel, both, len(xs)), out_shape=(...]
    ppermute x4, waiting for transfers between devices: 4.27 us -> 7.76 us  [shifted(): lax.ppermute(value, 'blk', [(s, (s + steps) % count) for s in range(count)])]
    ppermute x4, waiting for transfers between devices: 3.5 us -> 0.01 us  [swapped(): return lax.ppermute(value, 'split', [(s, s ^ mask) for s in range(count)])]
    ppermute x4, starting transfers between devices: 9.52 us -> 6.63 us  [shifted(): lax.ppermute(value, 'blk', [(s, (s + steps) % count) for s in range(count)])]
    ppermute x4, starting transfers between devices: 4.66 us -> 7.55 us  [swapped(): return lax.ppermute(value, 'split', [(s, s ^ mask) for s in range(count)])]
    unnamed x9 -> x10, local copies, waits for them, and re-layouts: 1 us -> 2.59 us
  transfers between devices with their start and end apart: 8 -> 8, of which waited for: 2 -> 2; matrix products, arithmetic and copies ran while one was open for 0% -> 0% of each run, Pallas kernels for 41% -> 35%
where the time goes in v1:
time: 58.7 us; the launch traced here: 58.4 us
  Pallas kernels  32.2 us (55%)
  starting transfers between devices  14.2 us (24%)
  waiting for transfers between devices  7.77 us (13%)
  local copies, waits for them, and re-layouts  3.35 us (6%)
  other arithmetic  0.8 us (1%)
    pallas_call x5, Pallas kernels, tiles(): pl.pallas_call(functools.partial(tile_kernel, both, len(xs)), out_shape=(...  31.2 us
    ppermute x4, waiting for transfers between devices, shifted(): lax.ppermute(value, 'blk', [(s, (s + steps) % count) for s in range(count)])  7.76 us
    ppermute x4, starting transfers between devices, swapped(): return lax.ppermute(value, 'split', [(s, s ^ mask) for s in range(count)])  7.55 us
    ppermute x4, starting transfers between devices, shifted(): lax.ppermute(value, 'blk', [(s, (s + steps) % count) for s in range(count)])  6.63 us
    unnamed x10, local copies, waits for them, and re-layouts  2.59 us
  transfers between devices with their start and end apart: 8, of which 2 were waited for; matrix products, arithmetic and copies ran while one was open for 0% of the time, Pallas kernels for 35%

profile of v1, /device:TPU:1, one launch (start us, length us, event | category | flops | bytes accessed | tf_op | source)
XLA Modules:
  0.0 58.4 jit_solution(3308602197240372249)
XLA Ops:
  0.0 0.7 %copy.5.inv_ref.refs_1_ = f32[32,1]{1,0:T(8,128)S(1)} copy(f32[32,1]{0,1:T(1,128)} %bitcast.1) | data formatting | bytes 256 | tf_op jit(solution)/shard_map/broadcast_in_dim | solution.py:230
  0.7 0.8 %copy-done = f32[16,1024]{1,0:T(8,128)S(1)} copy-done((f32[16,1024]{1,0:T(8,128)S(1)}, f32[16,1024]{1,0:T(8,128)}, u32[]{:S(2)}) %copy-start) | copy-done | bytes 65560
  1.6 0.9 %copy-done.3 = f32[32,1024]{1,0:T(8,128)S(1)} copy-done((f32[32,1024]{1,0:T(8,128)S(1)}, f32[32,1024]{1,0:T(8,128)}, u32[]{:S(2)}) %copy-start.3) | copy-done | bytes 131096
  2.5 0.3 first.1
  2.8 2.1 %collective-permute-start = (f32[48,1024]{1,0:T(8,128)S(1)}, f32[48,1024]{1,0:T(8,128)S(1)}, u32[]{:S(2)}, u32[]{:S(2)}) collective-permute-start(f32[48,1024]{1,0:T(8,128)S(1)} %get-tuple-element.16.rest_0_), channel_id=1, source_target_pairs={{0,2},{1,3},{2,0},{3,1},{4,6},{5,7},{6,4},{7,5},{8,10},{9,11},{10,... | collective-permute-start | bytes 589832 | tf_op jit(solution)/shard_map/ppermute | solution.py:226
  4.9 2.5 %collective-permute-start.3 = (f32[48,1024]{1,0:T(8,128)S(1)}, f32[48,1024]{1,0:T(8,128)S(1)}, u32[]{:S(2)}, u32[]{:S(2)}) collective-permute-start(f32[48,1024]{1,0:T(8,128)S(1)} %get-tuple-element.16.rest_0_), channel_id=1, source_target_pairs={{0,4},{4,8},{8,12},{12,16},{16,20},{20,24},{24,28},{28,32},{32,36}... | collective-permute-start | bytes 589832 | tf_op jit(solution)/shard_map/ppermute | solution.py:221
  7.3 1.6 %collective-permute-start.2 = (f32[48,1024]{1,0:T(8,128)S(1)}, f32[48,1024]{1,0:T(8,128)S(1)}, u32[]{:S(2)}, u32[]{:S(2)}) collective-permute-start(f32[48,1024]{1,0:T(8,128)S(1)} %get-tuple-element.16.rest_0_), channel_id=1, source_target_pairs={{0,8},{4,12},{8,16},{12,20},{16,24},{20,28},{24,32},{28,36},{32,40... | collective-permute-start | bytes 589832 | tf_op jit(solution)/shard_map/ppermute | solution.py:221
  9.0 0.8 %copy-done.1 = f32[16,1024]{1,0:T(8,128)S(1)} copy-done((f32[16,1024]{1,0:T(8,128)S(1)}, f32[16,1024]{1,0:T(8,128)}, u32[]{:S(2)}) %copy-start.1) | copy-done | bytes 65560
  9.8 2.1 %own.3 = f32[16,1024]{1,0:T(8,128)S(1)} custom-call(bf16[1024,256]{1,0:T(8,128)(2,1)S(1)} %get-tuple-element.15.at_ref, f32[16,1024]{1,0:T(8,128)S(1)} %copy-done.1, f32[32,1]{1,0:T(8,128)S(1)} %copy.5.inv_ref.refs_1_, f32[48,1024]{1,0:T(8,128)S(1)} %get-tuple-element.16.rest_0_), custom_call_target="tpu_custom_call" | custom-call | flops 1610612736 | bytes 614400 | tf_op jit(solution)/shard_map/own/pallas_call | solution.py:197
  12.0 0.3 prep.3
  12.3 0.1 pad_maximum_fusion.at_ref
  12.4 1.8 %collective-permute-start.1 = (f32[48,2048]{1,0:T(8,128)S(1)}, f32[48,2048]{1,0:T(8,128)S(1)}, u32[]{:S(2)}, u32[]{:S(2)}) collective-permute-start(f32[48,2048]{1,0:T(8,128)S(1)} %pad_maximum_fusion.1), channel_id=1, source_target_pairs={{0,1},{1,0},{2,3},{3,2},{4,5},{5,4},{6,7},{7,6},{8,9},{9,8},{10,11... | collective-permute-start | bytes 1179656 | tf_op jit(solution)/shard_map/ppermute | solution.py:226
  14.2 7.6 %collective-permute-done.3.rest_1_ = f32[48,1024]{1,0:T(8,128)S(1)} collective-permute-done((f32[48,1024]{1,0:T(8,128)S(1)}, f32[48,1024]{1,0:T(8,128)S(1)}, u32[]{:S(2)}, u32[]{:S(2)}) %collective-permute-start.3) | collective-permute-done | bytes 196640 | tf_op jit(solution)/shard_map/ppermute | solution.py:221
  21.7 0.2 collective-permute-done.2.rest_0_
  21.9 11.2 %both.2 = (f32[16,2048]{1,0:T(8,128)S(1)}, f32[16,2048]{1,0:T(8,128)S(1)}) custom-call(bf16[2048,256]{1,0:T(8,128)(2,1)S(1)} %pad_maximum_fusion.at_ref, f32[16,2048]{1,0:T(8,128)S(1)} %pad_maximum_fusion.2.v_ref, f32[32,1]{1,0:T(8,128)S(1)} %copy.5.inv_ref.refs_1_, f32[48,1024]{1,0:T(8,128)S(1)} %collective-permute-done.2.rest_0_, ...), custom_call_target="tpu_custom_call" | custom-call | flops 10737418240 | bytes 1228800 | tf_op jit(solution)/shard_map/both/pallas_call | solution.py:197
  33.2 2.1 %own.5 = f32[16,1024]{1,0:T(8,128)S(1)} custom-call(bf16[1024,256]{1,0:T(8,128)(2,1)S(1)} %get-tuple-element.19.at_ref, f32[16,1024]{1,0:T(8,128)S(1)} %get-tuple-element.20.v_ref, f32[32,1]{1,0:T(8,128)S(1)} %copy.5.inv_ref.refs_1_, f32[48,1024]{1,0:T(8,128)S(1)} %get-tuple-element.16.rest_0_), custom_call_target="tpu_custom_call" | custom-call | flops 1610612736 | bytes 614400 | tf_op jit(solution)/shard_map/own/pallas_call | solution.py:197
  35.3 0.4 prep.2
  35.7 11.2 %both.3 = (f32[16,2048]{1,0:T(8,128)S(1)}, f32[16,2048]{1,0:T(8,128)S(1)}) custom-call(bf16[2048,256]{1,0:T(8,128)(2,1)S(1)} %get-tuple-element.17.at_ref, f32[16,2048]{1,0:T(8,128)S(1)} %get-tuple-element.18.v_ref, f32[32,1]{1,0:T(8,128)S(1)} %copy.5.inv_ref.refs_1_, f32[48,1024]{1,0:T(8,128)S(1)} %collective-permute-done.2.rest_0_, ...), custom_call_target="tpu_custom_call" | custom-call | flops 10737418240 | bytes 1228800 | tf_op jit(solution)/shard_map/both/pallas_call | solution.py:197
  47.0 3.3 %collective-permute-start.4 = (f32[16,2048]{1,0:T(8,128)S(1)}, f32[16,2048]{1,0:T(8,128)S(1)}, u32[]{:S(2)}, u32[]{:S(2)}) collective-permute-start(f32[16,2048]{1,0:T(8,128)S(1)} %get-tuple-element.22), channel_id=1, source_target_pairs={{0,1},{1,0},{2,3},{3,2},{4,5},{5,4},{6,7},{7,6},{8,9},{9,8},{10,11... | collective-permute-start | bytes 393224 | tf_op jit(solution)/shard_map/ppermute | solution.py:226
  50.3 1.8 %collective-permute-start.6 = (f32[16,1024]{1,0:T(8,128)S(1)}, f32[16,1024]{1,0:T(8,128)S(1)}, u32[]{:S(2)}, u32[]{:S(2)}) collective-permute-start(f32[16,1024]{1,0:T(8,128)S(1)} %get-tuple-element.25), channel_id=1, source_target_pairs={{0,252},{4,0},{8,4},{12,8},{16,12},{20,16},{24,20},{28,24},{32,28}... | collective-permute-start | bytes 196616 | tf_op jit(solution)/shard_map/ppermute | solution.py:221
  52.1 0.7 %collective-permute-start.7 = (f32[16,1024]{1,0:T(8,128)S(1)}, f32[16,1024]{1,0:T(8,128)S(1)}, u32[]{:S(2)}, u32[]{:S(2)}) collective-permute-start(f32[16,1024]{1,0:T(8,128)S(1)} %get-tuple-element.26), channel_id=1, source_target_pairs={{0,248},{4,252},{8,0},{12,4},{16,8},{20,12},{24,16},{28,20},{32,24... | collective-permute-start | bytes 196616 | tf_op jit(solution)/shard_map/ppermute | solution.py:221
  52.9 0.4 collective-permute-start.5
  53.2 4.5 %own.4 = f32[16,1024]{1,0:T(8,128)S(1)} custom-call(bf16[2048,256]{1,0:T(8,128)(2,1)S(1)} %get-tuple-element.17.at_ref, f32[16,2048]{1,0:T(8,128)S(1)} %get-tuple-element.18.v_ref, f32[32,1]{1,0:T(8,128)S(1)} %copy.5.inv_ref.refs_1_, f32[48,1024]{1,0:T(8,128)S(1)} %get-tuple-element.16.rest_0_), custom_call_target="tpu_custom_call" | custom-call | flops 3221225472 | bytes 1228800 | tf_op jit(solution)/shard_map/own/pallas_call | solution.py:197
  57.8 0.7 %fusion.3 = f32[16,1024]{1,0:T(8,128)} fusion(f32[16,1024]{1,0:T(8,128)S(1)} %collective-permute-done.7, f32[16,1024]{1,0:T(8,128)S(1)} %collective-permute-done.6, f32[16,1024]{1,0:T(8,128)S(1)} %collective-permute-done.5, f32[16,2048]{1,0:T(8,128)S(1)} %add.29, f32[16,1024]{1,0:T(8,128)S(1)} %copy-done.2, f32[16,1024]{1,0:T(8,128)S(1)} %own.5, ...), kind=kLoop, calls=%fused_computation.7 | loop fusion | flops 131072 | bytes 593920 | tf_op jit(solution)/shard_map/add | solution.py:250
  (19 shorter events, 0.1 us)
Async XLA Ops:
  0.7 0.8 %copy-start = (f32[16,1024]{1,0:T(8,128)S(1)}, f32[16,1024]{1,0:T(8,128)}, u32[]{:S(2)}) copy-start(f32[16,1024]{1,0:T(8,128)} %v_ref.1) | copy-start | bytes 196612
  1.6 0.9 %copy-start.3 = (f32[32,1024]{1,0:T(8,128)S(1)}, f32[32,1024]{1,0:T(8,128)}, u32[]{:S(2)}) copy-start(f32[32,1024]{1,0:T(8,128)} %points_ref.1) | copy-start | bytes 393220
  2.8 9.2 %collective-permute-start = (f32[48,1024]{1,0:T(8,128)S(1)}, f32[48,1024]{1,0:T(8,128)S(1)}, u32[]{:S(2)}, u32[]{:S(2)}) collective-permute-start(f32[48,1024]{1,0:T(8,128)S(1)} %get-tuple-element.16.rest_0_), channel_id=1, source_target_pairs={{0,2},{1,3},{2,0},{3,1},{4,6},{5,7},{6,4},{7,5},{8,10},{9,11},{10,... | collective-permute-start | bytes 589832 | tf_op jit(solution)/shard_map/ppermute | solution.py:226
  4.9 16.8 %collective-permute-start.3 = (f32[48,1024]{1,0:T(8,128)S(1)}, f32[48,1024]{1,0:T(8,128)S(1)}, u32[]{:S(2)}, u32[]{:S(2)}) collective-permute-start(f32[48,1024]{1,0:T(8,128)S(1)} %get-tuple-element.16.rest_0_), channel_id=1, source_target_pairs={{0,4},{4,8},{8,12},{12,16},{16,20},{20,24},{24,28},{28,32},{32,36}... | collective-permute-start | bytes 589832 | tf_op jit(solution)/shard_map/ppermute | solution.py:221
  7.3 14.6 %collective-permute-start.2 = (f32[48,1024]{1,0:T(8,128)S(1)}, f32[48,1024]{1,0:T(8,128)S(1)}, u32[]{:S(2)}, u32[]{:S(2)}) collective-permute-start(f32[48,1024]{1,0:T(8,128)S(1)} %get-tuple-element.16.rest_0_), channel_id=1, source_target_pairs={{0,8},{4,12},{8,16},{12,20},{16,24},{20,28},{24,32},{28,36},{32,40... | collective-permute-start | bytes 589832 | tf_op jit(solution)/shard_map/ppermute | solution.py:221
  9.0 0.8 %copy-start.1 = (f32[16,1024]{1,0:T(8,128)S(1)}, f32[16,1024]{1,0:T(8,128)}, u32[]{:S(2)}) copy-start(f32[16,1024]{1,0:T(8,128)} %v_ref.1) | copy-start | bytes 196612
  12.2 1.9 %copy-start.2 = (f32[16,1024]{1,0:T(8,128)S(1)}, f32[16,1024]{1,0:T(8,128)}, u32[]{:S(2)}) copy-start(f32[16,1024]{1,0:T(8,128)} %v_ref.1) | copy-start | bytes 196612
  12.4 22.9 %collective-permute-start.1 = (f32[48,2048]{1,0:T(8,128)S(1)}, f32[48,2048]{1,0:T(8,128)S(1)}, u32[]{:S(2)}, u32[]{:S(2)}) collective-permute-start(f32[48,2048]{1,0:T(8,128)S(1)} %pad_maximum_fusion.1), channel_id=1, source_target_pairs={{0,1},{1,0},{2,3},{3,2},{4,5},{5,4},{6,7},{7,6},{8,9},{9,8},{10,11... | collective-permute-start | bytes 1179656 | tf_op jit(solution)/shard_map/ppermute | solution.py:226
  47.0 5.9 %collective-permute-start.4 = (f32[16,2048]{1,0:T(8,128)S(1)}, f32[16,2048]{1,0:T(8,128)S(1)}, u32[]{:S(2)}, u32[]{:S(2)}) collective-permute-start(f32[16,2048]{1,0:T(8,128)S(1)} %get-tuple-element.22), channel_id=1, source_target_pairs={{0,1},{1,0},{2,3},{3,2},{4,5},{5,4},{6,7},{7,6},{8,9},{9,8},{10,11... | collective-permute-start | bytes 393224 | tf_op jit(solution)/shard_map/ppermute | solution.py:226
  50.3 7.4 %collective-permute-start.6 = (f32[16,1024]{1,0:T(8,128)S(1)}, f32[16,1024]{1,0:T(8,128)S(1)}, u32[]{:S(2)}, u32[]{:S(2)}) collective-permute-start(f32[16,1024]{1,0:T(8,128)S(1)} %get-tuple-element.25), channel_id=1, source_target_pairs={{0,252},{4,0},{8,4},{12,8},{16,12},{20,16},{24,20},{28,24},{32,28}... | collective-permute-start | bytes 196616 | tf_op jit(solution)/shard_map/ppermute | solution.py:221
  52.1 5.6 %collective-permute-start.7 = (f32[16,1024]{1,0:T(8,128)S(1)}, f32[16,1024]{1,0:T(8,128)S(1)}, u32[]{:S(2)}, u32[]{:S(2)}) collective-permute-start(f32[16,1024]{1,0:T(8,128)S(1)} %get-tuple-element.26), channel_id=1, source_target_pairs={{0,248},{4,252},{8,0},{12,4},{16,8},{20,12},{24,16},{28,20},{32,24... | collective-permute-start | bytes 196616 | tf_op jit(solution)/shard_map/ppermute | solution.py:221
  52.9 4.9 %copy-start.4 = (f32[1024]{0:T(1024)S(1)}, f32[1024]{0:T(1024)}, u32[]{:S(2)}) copy-start(f32[1024]{0:T(1024)} %param.7) | copy-start | bytes 12292
  52.9 4.9 %collective-permute-start.5 = (f32[16,1024]{1,0:T(8,128)S(1)}, f32[16,1024]{1,0:T(8,128)S(1)}, u32[]{:S(2)}, u32[]{:S(2)}) collective-permute-start(f32[16,1024]{1,0:T(8,128)S(1)} %slice.17), channel_id=1, source_target_pairs={{0,2},{1,3},{2,0},{3,1},{4,6},{5,7},{6,4},{7,5},{8,10},{9,11},{10,... | collective-permute-start | bytes 196616 | tf_op jit(solution)/shard_map/ppermute | solution.py:226

commit v2 on v0

v2 whole, which is shorter than its diff:
```python
import functools

import jax
import jax.numpy as jnp
from jax import lax
from jax.experimental import pallas as pl
from jax.experimental.pallas import tpu as pltpu
from jax.sharding import PartitionSpec as P

SIGNAL = 0.03125
ROOT_FIVE = 2.23606797749979
LOG2E = 1.4426950408889634
POINT_SCALE = ROOT_FIVE * LOG2E
SHIFT = 1.5 * LOG2E
FLOOR = 0.75 * LOG2E * LOG2E
OUT_SCALE = SIGNAL / (3.0 * LOG2E * LOG2E) * 2.0**SHIFT
DIMS = 32
RHS = 16
DEPTH = 256
TILE = 256
GROUP = 2
STEP_TILES = 32
BF16 = jnp.bfloat16
F32 = jnp.float32
LOW = jnp.bfloat16


def dot(a, b, ca, cb):
    return lax.dot_general(a, b, (((ca,), (cb,)), ((), ())), preferred_element_type=F32)


def pieces(x):
    hi = x.astype(BF16)
    rest = x - hi.astype(F32)
    mid = rest.astype(BF16)
    lo = (rest - mid.astype(F32)).astype(BF16)
    return hi, mid, lo


def norm_rows(sq, first):
    s1, s2, s3 = (p.astype(F32) for p in pieces(sq))
    row = lax.broadcasted_iota(jnp.int32, (16, sq.shape[1]), 0)
    out = jnp.where(row < 6, 1.0, 0.0)
    for k, s in enumerate((s1, s2, s3)):
        out = jnp.where(row == first + k, s, out)
    return out.astype(BF16)


def features(x, rows):
    sq = jnp.sum(x * x, axis=0, keepdims=True)
    hi, mid, lo = pieces(x)
    pad = jnp.zeros((DEPTH - 208, x.shape[1]), BF16)
    if rows:
        two = jnp.asarray(-2.0, BF16)
        hi, mid, lo = hi * two, mid * two, lo * two
        return jnp.concatenate([hi, mid, hi, lo, mid, hi, norm_rows(sq, 0), pad], axis=0)
    return jnp.concatenate([hi, hi, mid, hi, mid, lo, norm_rows(sq, 3), pad], axis=0)


def halves(v, kind):
    hi = v.astype(kind)
    return jnp.concatenate([hi, (v - hi.astype(F32)).astype(kind)], axis=0)


def kernel_tile(b2):
    w = -SHIFT - b2 * lax.rsqrt(b2)
    t = (w * w + FLOOR) * jnp.exp2(w)
    hi = t.astype(BF16)
    return hi, (t - hi.astype(F32)).astype(LOW)


def fold(x):
    return (x[:RHS] + x[RHS:]) * OUT_SCALE


def first_kernel(x_ref, at_ref, b_ref):
    x = x_ref[:DIMS, :]
    at_ref[...] = features(x, True).T
    b_ref[...] = features(x, False)


def rows_kernel(x_ref, at_ref):
    at_ref[...] = features(x_ref[:DIMS, :], True).T


def cols_kernel(x_ref, b_ref):
    b_ref[...] = features(x_ref[:DIMS, :], False)


def tile_kernel(both, at_ref, v_ref, b_ref, *rest):
    if both:
        x_ref, fwd_ref, bwd_ref, vc_ref, facc_ref = rest[:5]
    else:
        bwd_ref = rest[0]
    vr_ref, acc_ref, even_ref, odd_ref, hi_ref, lo_ref, slot_ref = rest[5 if both else 1 :]
    across, groups = b_ref.shape[1] // TILE, at_ref.shape[0] // (TILE * GROUP)
    down = min(STEP_TILES // (GROUP * across), groups)
    slot_ref[0] = 0
    slot = slot_ref[0]
    if both:
        vc_ref[...] = halves(x_ref[DIMS:, :], BF16)
        facc_ref[...] = jnp.zeros_like(facc_ref)
    vr_ref[...] = halves(v_ref[DIMS:, :], BF16)
    acc_ref[...] = jnp.zeros_like(acc_ref)

    def distances(ref, i, j):
        rows = pl.ds(pl.multiple_of(i * TILE * GROUP, TILE * GROUP), TILE * GROUP)
        d2 = dot(at_ref[rows, :], b_ref[:, j * TILE : (j + 1) * TILE], 1, 0)
        ref[0] = jnp.maximum(d2, 1e-30)

    def products(hi, lo, i, j):
        cols = slice(j * TILE, (j + 1) * TILE)
        rows = pl.ds(pl.multiple_of(i * TILE, TILE), TILE)
        vr = vr_ref[:, rows]
        acc_ref[:, cols] += dot(vr, hi, 1, 0) + dot(vr, lo, 1, 0)
        if both:
            vc = vc_ref[:, cols]
            facc_ref[:, rows] += dot(vc, hi, 1, 1) + dot(vc, lo, 1, 1)

    hi_ref[...] = jnp.zeros_like(hi_ref)
    lo_ref[...] = jnp.zeros_like(lo_ref)
    distances(even_ref, 0, 0)

    def step(k, carry):
        hi, lo = hi_ref[...], lo_ref[...]
        i, j = jnp.maximum(k * down * GROUP - 1, 0), across - 1
        for t in range(down * across):
            now, later = (even_ref, odd_ref) if t % 2 == 0 else (odd_ref, even_ref)
            ahead = k * down + (t + 1) // across
            if t == down * across - 1:
                ahead = jnp.where(ahead < groups, ahead, 0)
            distances(later, ahead, (t + 1) % across)
            for g in range(GROUP):
                products(hi, lo, i, j)
                hi, lo = kernel_tile(now[slot, g * TILE : (g + 1) * TILE, :])
                i, j = (k * down + t // across) * GROUP + g, t % across
        hi_ref[...], lo_ref[...] = hi, lo
        return carry

    lax.fori_loop(0, groups // down, step, 0)
    products(hi_ref[...], lo_ref[...], groups * GROUP - 1, across - 1)
    bwd_ref[...] = fold(acc_ref[...])
    if both:
        fwd_ref[...] = fold(facc_ref[...])


VMEM = pl.BlockSpec(memory_space=pltpu.VMEM)
PARAMS = pltpu.CompilerParams(vmem_limit_bytes=40 * 2**20)


def first(x):
    n = x.shape[1]
    return pl.pallas_call(
        first_kernel,
        out_shape=(jax.ShapeDtypeStruct((n, DEPTH), BF16), jax.ShapeDtypeStruct((DEPTH, n), BF16)),
        in_specs=[VMEM],
        out_specs=(VMEM, VMEM),
        compiler_params=PARAMS,
        cost_estimate=pl.CostEstimate(flops=n * 64, bytes_accessed=n * 16, transcendentals=0),
        name="first",
    )(x)


def prep(x, rows):
    n = x.shape[1]
    return pl.pallas_call(
        rows_kernel if rows else cols_kernel,
        out_shape=jax.ShapeDtypeStruct((n, DEPTH) if rows else (DEPTH, n), BF16),
        in_specs=[VMEM],
        out_specs=VMEM,
        compiler_params=PARAMS,
        cost_estimate=pl.CostEstimate(flops=n * 64, bytes_accessed=n * 16, transcendentals=0),
        name="rows" if rows else "cols",
    )(x)


def tiles(at, v, b, x=None):
    n, width = at.shape[0], b.shape[1]
    both = x is not None
    bwd = jax.ShapeDtypeStruct((RHS, width), F32)
    fwd = jax.ShapeDtypeStruct((RHS, n), F32)
    more = [pltpu.VMEM((2 * RHS, width), BF16), pltpu.VMEM((2 * RHS, n), F32)] if both else []
    return pl.pallas_call(
        functools.partial(tile_kernel, both),
        out_shape=(fwd, bwd) if both else bwd,
        in_specs=[VMEM] * (4 if both else 3),
        out_specs=(VMEM, VMEM) if both else VMEM,
        scratch_shapes=more
        + [
            pltpu.VMEM((2 * RHS, n), BF16),
            pltpu.VMEM((2 * RHS, width), F32),
            pltpu.VMEM((1, TILE * GROUP, TILE), F32),
            pltpu.VMEM((1, TILE * GROUP, TILE), F32),
            pltpu.VMEM((TILE, TILE), BF16),
            pltpu.VMEM((TILE, TILE), LOW),
            pltpu.SMEM((1,), jnp.int32),
        ],
        compiler_params=PARAMS,
        cost_estimate=pl.CostEstimate(
            flops=n * width * 8, bytes_accessed=n * 16, transcendentals=0
        ),
        name="both" if both else "own",
    )(at, v, b, *([x] if both else []))


def shifted(value, steps):
    count = lax.axis_size("blk")
    return lax.ppermute(value, "blk", [(s, (s + steps) % count) for s in range(count)])


def swapped(value, mask):
    count = lax.axis_size("split")
    return lax.ppermute(value, "split", [(s, s ^ mask) for s in range(count)])


def after(value, *others):
    return lax.optimization_barrier((value, *others))[0]


def body(points, vectors, inv_length, noise):
    own = jnp.concatenate([points * inv_length[:, None] * POINT_SCALE, vectors], axis=0)
    width = own.shape[1]
    far = swapped(own, 2)
    two = shifted(own, 2)
    at0, b0 = first(own)
    total = tiles(at0, own, b0)
    far = after(far, total)
    pair = jnp.concatenate([own, far], axis=1)
    other = swapped(pair, 1)
    one = shifted(after(own, far), 1)
    at1 = prep(far, True)
    total = total + tiles(at1, far, b0)
    other = after(other, total)
    at_other = prep(other, True)
    total = total + tiles(at_other, other, b0)
    block = jnp.concatenate([pair, other], axis=1)
    at_pair = jnp.concatenate([at0, at1], axis=0)
    at = jnp.concatenate([at_pair, at_other], axis=0)
    two = after(two, total)
    fwd2, ret2 = tiles(at, block, prep(two, False), two)
    back2 = shifted(ret2, -2)
    one = after(one, ret2)
    b1 = prep(one, False)
    fwd_other, ret_other = tiles(at_other, other, b1, one)
    give_near = swapped(fwd_other + fwd2[:, 2 * width :], 1)
    fwd_pair, ret_pair = tiles(at_pair, after(pair, ret_other), b1, one)
    back1 = shifted(ret_other + ret_pair, -1)
    rows = fwd_pair + fwd2[:, : 2 * width] + give_near
    give_far = swapped(rows[:, width:], 2)
    return total + rows[:, :width] + give_far + back1 + back2 + noise[None, :] * vectors


def solution(mesh):
    placed = (P(None, ("blk", "split")), P(None, ("blk", "split")), P(), P(("blk", "split")))
    return jax.shard_map(
        body, mesh=mesh, in_specs=placed, out_specs=P(None, ("blk", "split")), check_vma=False
    )
```

time: 69.7 us -> 55.4 us (0.79)
  Pallas kernels: 45.4 us -> 29.1 us
  starting transfers between devices: 14.2 us -> 17.1 us
  other arithmetic: 0.76 us -> 2.94 us
  waiting for transfers between devices: 7.76 us -> 5.95 us
  local copies, waits for them, and re-layouts: 1.15 us -> 0.02 us
    pallas_call x7 -> x6, Pallas kernels: 44.5 us -> 28.2 us  [tiles(): pl.pallas_call(functools.partial(tile_kernel, both), out_shape=(fwd, bwd)...]
    ppermute x4, starting transfers between devices: 4.66 us -> 7.79 us  [swapped(): return lax.ppermute(value, 'split', [(s, s ^ mask) for s in range(count)])]
    ppermute x4, waiting for transfers between devices: 3.5 us -> 1.73 us  [swapped(): return lax.ppermute(value, 'split', [(s, s ^ mask) for s in range(count)])]
    concatenate x1 -> x5, other arithmetic: 0.03 us -> 1.14 us  [the longest x1 0.86 us: body(): jnp.concatenate([points * inv_length[:, None] * POINT_SCALE, vectors], ax...]
    mul x0 -> x1, other arithmetic: none -> 1.02 us  [body(): points * inv_length[:, None] * POINT_SCALE]
    unnamed x9 -> x4, local copies, waits for them, and re-layouts: 1 us -> 0.01 us
  transfers between devices with their start and end apart: 8 -> 8, of which waited for: 2 -> 4; matrix products, arithmetic and copies ran while one was open for 0% -> 1% of each run, Pallas kernels for 41% -> 44%
where the time goes in v2:
time: 55.4 us; the launch traced here: 55.2 us
  Pallas kernels  29.1 us (53%)
  starting transfers between devices  17.1 us (31%)
  waiting for transfers between devices  5.95 us (11%)
  other arithmetic  2.94 us (5%)
    pallas_call x6, Pallas kernels, tiles(): pl.pallas_call(functools.partial(tile_kernel, both), out_shape=(fwd, bwd)...  28.2 us
    ppermute x4, starting transfers between devices, shifted(): lax.ppermute(value, 'blk', [(s, (s + steps) % count) for s in range(count)])  9.3 us
    ppermute x4, starting transfers between devices, swapped(): return lax.ppermute(value, 'split', [(s, s ^ mask) for s in range(count)])  7.79 us
    ppermute x4, waiting for transfers between devices, shifted(): lax.ppermute(value, 'blk', [(s, (s + steps) % count) for s in range(count)])  4.22 us
    ppermute x4, waiting for transfers between devices, swapped(): return lax.ppermute(value, 'split', [(s, s ^ mask) for s in range(count)])  1.73 us
  transfers between devices with their start and end apart: 8, of which 4 were waited for; matrix products, arithmetic and copies ran while one was open for 1% of the time, Pallas kernels for 44%

profile of v2, /device:TPU:1, one launch (start us, length us, event | category | flops | bytes accessed | tf_op | source)
XLA Modules:
  0.0 55.2 jit_solution(8004812389387621751)
XLA Ops:
  0.0 1.0 %multiply_multiply_fusion = f32[32,1024]{1,0:T(8,128)S(1)} fusion(f32[32,1024]{1,0:T(8,128)} %param.4, f32[32]{0:T(128)} %param.6), kind=kLoop, calls=%fused_computation.7 | loop fusion | flops 65536 | bytes 262272 | tf_op jit(solution)/shard_map/mul | solution.py:221
  1.0 0.9 %pad_maximum_fusion.4.x_ref.v_ref = f32[48,1024]{1,0:T(8,128)S(1)} fusion(f32[16,1024]{1,0:T(8,128)} %param.5, f32[32,1024]{1,0:T(8,128)S(1)} %multiply_multiply_fusion), kind=kLoop, calls=%fused_computation.4 | loop fusion | flops 49152 | bytes 393216 | tf_op jit(solution)/shard_map/concatenate | solution.py:221
  1.9 2.1 %collective-permute-start = (f32[48,1024]{1,0:T(8,128)S(1)}, f32[48,1024]{1,0:T(8,128)S(1)}, u32[]{:S(2)}, u32[]{:S(2)}) collective-permute-start(f32[48,1024]{1,0:T(8,128)S(1)} %pad_maximum_fusion.4.x_ref.v_ref), channel_id=1, source_target_pairs={{0,2},{1,3},{2,0},{3,1},{4,6},{5,7},{6,4},{7,5},{8,10},{9,11},{10,... | collective-permute-start | bytes 589832 | tf_op jit(solution)/shard_map/ppermute | solution.py:213
  4.0 0.2 first.1
  4.2 2.0 %own.3 = f32[16,1024]{1,0:T(8,128)S(1)} custom-call(bf16[1024,256]{1,0:T(8,128)(2,1)S(1)} %get-tuple-element.19.at_ref, f32[48,1024]{1,0:T(8,128)S(1)} %pad_maximum_fusion.4.x_ref.v_ref, bf16[256,1024]{1,0:T(8,128)(2,1)S(1)} %get-tuple-element.20.b_ref), custom_call_target="tpu_custom_call" | custom-call | flops 8388608 | bytes 16384 | tf_op jit(solution)/shard_map/own/pallas_call | solution.py:183
  6.3 1.0 %collective-permute-done.x_ref.v_ref = f32[48,1024]{1,0:T(8,128)S(1)} collective-permute-done((f32[48,1024]{1,0:T(8,128)S(1)}, f32[48,1024]{1,0:T(8,128)S(1)}, u32[]{:S(2)}, u32[]{:S(2)}) %collective-permute-start) | collective-permute-done | bytes 196640 | tf_op jit(solution)/shard_map/ppermute | solution.py:213
  7.3 3.7 %collective-permute-start.1 = (f32[48,2048]{1,0:T(8,128)S(1)}, f32[48,2048]{1,0:T(8,128)S(1)}, u32[]{:S(2)}, u32[]{:S(2)}) collective-permute-start(f32[48,2048]{1,0:T(8,128)S(1)} %pad_maximum_fusion.3.v_ref), channel_id=1, source_target_pairs={{0,1},{1,0},{2,3},{3,2},{4,5},{5,4},{6,7},{7,6},{8,9},{9,8},{10,11... | collective-permute-start | bytes 1179656 | tf_op jit(solution)/shard_map/ppermute | solution.py:213
  11.0 0.9 %collective-permute-start.3 = (f32[48,1024]{1,0:T(8,128)S(1)}, f32[48,1024]{1,0:T(8,128)S(1)}, u32[]{:S(2)}, u32[]{:S(2)}) collective-permute-start(f32[48,1024]{1,0:T(8,128)S(1)} %pad_maximum_fusion.4.x_ref.v_ref), channel_id=1, source_target_pairs={{0,8},{4,12},{8,16},{12,20},{16,24},{20,28},{24,32},{28,36},{32,40... | collective-permute-start | bytes 589832 | tf_op jit(solution)/shard_map/ppermute | solution.py:208
  11.9 0.2 rows.2.at_ref
  12.1 2.0 %own.4 = f32[16,1024]{1,0:T(8,128)S(1)} custom-call(bf16[1024,256]{1,0:T(8,128)(2,1)S(1)} %rows.2.at_ref, f32[48,1024]{1,0:T(8,128)S(1)} %collective-permute-done.x_ref.v_ref, bf16[256,1024]{1,0:T(8,128)(2,1)S(1)} %get-tuple-element.20.b_ref), custom_call_target="tpu_custom_call" | custom-call | flops 8388608 | bytes 16384 | tf_op jit(solution)/shard_map/own/pallas_call | solution.py:183
  14.2 2.8 %collective-permute-start.2 = (f32[48,1024]{1,0:T(8,128)S(1)}, f32[48,1024]{1,0:T(8,128)S(1)}, u32[]{:S(2)}, u32[]{:S(2)}) collective-permute-start(f32[48,1024]{1,0:T(8,128)S(1)} %pad_maximum_fusion.4.x_ref.v_ref), channel_id=1, source_target_pairs={{0,4},{4,8},{8,12},{12,16},{16,20},{20,24},{24,28},{28,32},{32,36}... | collective-permute-start | bytes 589832 | tf_op jit(solution)/shard_map/ppermute | solution.py:208
  17.0 0.3 rows.3.at_ref
  17.5 3.8 %own.5 = f32[16,1024]{1,0:T(8,128)S(1)} custom-call(bf16[2048,256]{1,0:T(8,128)(2,1)S(1)} %rows.3.at_ref, f32[48,2048]{1,0:T(8,128)S(1)} %collective-permute-done.1.x_ref.v_ref, bf16[256,1024]{1,0:T(8,128)(2,1)S(1)} %get-tuple-element.20.b_ref), custom_call_target="tpu_custom_call" | custom-call | flops 16777216 | bytes 32768 | tf_op jit(solution)/shard_map/own/pallas_call | solution.py:183
  21.4 2.1 %collective-permute-done.3.x_ref.rest_0_ = f32[48,1024]{1,0:T(8,128)S(1)} collective-permute-done((f32[48,1024]{1,0:T(8,128)S(1)}, f32[48,1024]{1,0:T(8,128)S(1)}, u32[]{:S(2)}, u32[]{:S(2)}) %collective-permute-start.3) | collective-permute-done | bytes 196640 | tf_op jit(solution)/shard_map/ppermute | solution.py:208
  23.5 10.4 %both.3 = (f32[16,4096]{1,0:T(8,128)S(1)}, f32[16,1024]{1,0:T(8,128)S(1)}) custom-call(bf16[4096,256]{1,0:T(8,128)(2,1)S(1)} %pad_maximum_fusion.at_ref, f32[48,4096]{1,0:T(8,128)S(1)} %pad_maximum_fusion.2.v_ref, bf16[256,1024]{1,0:T(8,128)(2,1)S(1)} %cols.2.b_ref, f32[48,1024]{1,0:T(8,128)S(1)} %collective-permute-done.3.x_ref.rest_0_), custom_call_target="tpu_custom_call" | custom-call | flops 33554432 | bytes 65536 | tf_op jit(solution)/shard_map/both/pallas_call | solution.py:183
  34.0 5.0 %both.4 = (f32[16,2048]{1,0:T(8,128)S(1)}, f32[16,1024]{1,0:T(8,128)S(1)}) custom-call(bf16[2048,256]{1,0:T(8,128)(2,1)S(1)} %rows.3.at_ref, f32[48,2048]{1,0:T(8,128)S(1)} %collective-permute-done.1.x_ref.v_ref, bf16[256,1024]{1,0:T(8,128)(2,1)S(1)} %cols.3.b_ref, f32[48,1024]{1,0:T(8,128)S(1)} %collective-permute-done.2.x_ref.rest_0_), custom_call_target="tpu_custom_call" | custom-call | flops 16777216 | bytes 32768 | tf_op jit(solution)/shard_map/both/pallas_call | solution.py:183
  39.0 0.8 %collective-permute-start.4 = (f32[16,2048]{1,0:T(8,128)S(1)}, f32[16,2048]{1,0:T(8,128)S(1)}, u32[]{:S(2)}, u32[]{:S(2)}) collective-permute-start(f32[16,2048]{1,0:T(8,128)S(1)} %slice_add_fusion), channel_id=1, source_target_pairs={{0,1},{1,0},{2,3},{3,2},{4,5},{5,4},{6,7},{7,6},{8,9},{9,8},{10,11... | collective-permute-start | bytes 393224 | tf_op jit(solution)/shard_map/ppermute | solution.py:213
  39.9 4.3 %collective-permute-start.7 = (f32[16,1024]{1,0:T(8,128)S(1)}, f32[16,1024]{1,0:T(8,128)S(1)}, u32[]{:S(2)}, u32[]{:S(2)}) collective-permute-start(f32[16,1024]{1,0:T(8,128)S(1)} %get-tuple-element.25), channel_id=1, source_target_pairs={{0,248},{4,252},{8,0},{12,4},{16,8},{20,12},{24,16},{28,20},{32,24... | collective-permute-start | bytes 196616 | tf_op jit(solution)/shard_map/ppermute | solution.py:208
  44.2 5.0 %both.5 = (f32[16,2048]{1,0:T(8,128)S(1)}, f32[16,1024]{1,0:T(8,128)S(1)}) custom-call(bf16[2048,256]{1,0:T(8,128)(2,1)S(1)} %pad_maximum_fusion.1.at_ref, f32[48,2048]{1,0:T(8,128)S(1)} %pad_maximum_fusion.3.v_ref, bf16[256,1024]{1,0:T(8,128)(2,1)S(1)} %cols.3.b_ref, f32[48,1024]{1,0:T(8,128)S(1)} %collective-permute-done.2.x_ref.rest_0_), custom_call_target="tpu_custom_call" | custom-call | flops 16777216 | bytes 32768 | tf_op jit(solution)/shard_map/both/pallas_call | solution.py:183
  49.2 1.3 %collective-permute-start.6 = (f32[16,1024]{1,0:T(8,128)S(1)}, f32[16,1024]{1,0:T(8,128)S(1)}, u32[]{:S(2)}, u32[]{:S(2)}) collective-permute-start(f32[16,1024]{1,0:T(8,128)S(1)} %add.40), channel_id=1, source_target_pairs={{0,252},{4,0},{8,4},{12,8},{16,12},{20,16},{24,20},{28,24},{32,28}... | collective-permute-start | bytes 196616 | tf_op jit(solution)/shard_map/ppermute | solution.py:208
  50.5 1.2 %collective-permute-start.5 = (f32[16,1024]{1,0:T(8,128)S(1)}, f32[16,1024]{1,0:T(8,128)S(1)}, u32[]{:S(2)}, u32[]{:S(2)}) collective-permute-start(f32[16,1024]{1,0:T(8,128)S(1)} %slice.17), channel_id=1, source_target_pairs={{0,2},{1,3},{2,0},{3,1},{4,6},{5,7},{6,4},{7,5},{8,10},{9,11},{10,... | collective-permute-start | bytes 196616 | tf_op jit(solution)/shard_map/ppermute | solution.py:213
  51.7 2.2 %collective-permute-done.6 = f32[16,1024]{1,0:T(8,128)S(1)} collective-permute-done((f32[16,1024]{1,0:T(8,128)S(1)}, f32[16,1024]{1,0:T(8,128)S(1)}, u32[]{:S(2)}, u32[]{:S(2)}) %collective-permute-start.6) | collective-permute-done | bytes 65568 | tf_op jit(solution)/shard_map/ppermute | solution.py:208
  53.9 0.7 %collective-permute-done.5 = f32[16,1024]{1,0:T(8,128)S(1)} collective-permute-done((f32[16,1024]{1,0:T(8,128)S(1)}, f32[16,1024]{1,0:T(8,128)S(1)}, u32[]{:S(2)}, u32[]{:S(2)}) %collective-permute-start.5) | collective-permute-done | bytes 65568 | tf_op jit(solution)/shard_map/ppermute | solution.py:213
  54.6 0.7 %fusion.3 = f32[16,1024]{1,0:T(8,128)} fusion(f32[16,1024]{1,0:T(8,128)S(1)} %collective-permute-done.7, f32[16,1024]{1,0:T(8,128)S(1)} %collective-permute-done.6, f32[16,1024]{1,0:T(8,128)S(1)} %collective-permute-done.5, f32[16,1024]{1,0:T(8,128)S(1)} %add.34, f32[16,2048]{1,0:T(8,128)S(1)} %add_add_fusion, f32[16,1024]{1,0:T(8,128)S(1)} %copy-done, ...), kind=kLoop, calls=%fused_computation.12 | loop fusion | flops 98304 | bytes 462848 | tf_op jit(solution)/shard_map/add | solution.py:250
  (20 shorter events, 0.6 us)
Async XLA Ops:
  0.0 7.3 %copy-start = (f32[16,1024]{1,0:T(8,128)S(1)}, f32[16,1024]{1,0:T(8,128)}, u32[]{:S(2)}) copy-start(f32[16,1024]{1,0:T(8,128)} %param.5) | copy-start | bytes 196612
  1.9 5.4 %collective-permute-start = (f32[48,1024]{1,0:T(8,128)S(1)}, f32[48,1024]{1,0:T(8,128)S(1)}, u32[]{:S(2)}, u32[]{:S(2)}) collective-permute-start(f32[48,1024]{1,0:T(8,128)S(1)} %pad_maximum_fusion.4.x_ref.v_ref), channel_id=1, source_target_pairs={{0,2},{1,3},{2,0},{3,1},{4,6},{5,7},{6,4},{7,5},{8,10},{9,11},{10,... | collective-permute-start | bytes 589832 | tf_op jit(solution)/shard_map/ppermute | solution.py:213
  7.3 9.7 %collective-permute-start.1 = (f32[48,2048]{1,0:T(8,128)S(1)}, f32[48,2048]{1,0:T(8,128)S(1)}, u32[]{:S(2)}, u32[]{:S(2)}) collective-permute-start(f32[48,2048]{1,0:T(8,128)S(1)} %pad_maximum_fusion.3.v_ref), channel_id=1, source_target_pairs={{0,1},{1,0},{2,3},{3,2},{4,5},{5,4},{6,7},{7,6},{8,9},{9,8},{10,11... | collective-permute-start | bytes 1179656 | tf_op jit(solution)/shard_map/ppermute | solution.py:213
  11.0 12.4 %collective-permute-start.3 = (f32[48,1024]{1,0:T(8,128)S(1)}, f32[48,1024]{1,0:T(8,128)S(1)}, u32[]{:S(2)}, u32[]{:S(2)}) collective-permute-start(f32[48,1024]{1,0:T(8,128)S(1)} %pad_maximum_fusion.4.x_ref.v_ref), channel_id=1, source_target_pairs={{0,8},{4,12},{8,16},{12,20},{16,24},{20,28},{24,32},{28,36},{32,40... | collective-permute-start | bytes 589832 | tf_op jit(solution)/shard_map/ppermute | solution.py:208
  14.2 19.8 %collective-permute-start.2 = (f32[48,1024]{1,0:T(8,128)S(1)}, f32[48,1024]{1,0:T(8,128)S(1)}, u32[]{:S(2)}, u32[]{:S(2)}) collective-permute-start(f32[48,1024]{1,0:T(8,128)S(1)} %pad_maximum_fusion.4.x_ref.v_ref), channel_id=1, source_target_pairs={{0,4},{4,8},{8,12},{12,16},{16,20},{20,24},{24,28},{28,32},{32,36}... | collective-permute-start | bytes 589832 | tf_op jit(solution)/shard_map/ppermute | solution.py:208
  39.0 15.6 %copy-start.1 = (f32[1024]{0:T(1024)S(1)}, f32[1024]{0:T(1024)}, u32[]{:S(2)}) copy-start(f32[1024]{0:T(1024)} %param.7) | copy-start | bytes 12292
  39.0 11.4 %collective-permute-start.4 = (f32[16,2048]{1,0:T(8,128)S(1)}, f32[16,2048]{1,0:T(8,128)S(1)}, u32[]{:S(2)}, u32[]{:S(2)}) collective-permute-start(f32[16,2048]{1,0:T(8,128)S(1)} %slice_add_fusion), channel_id=1, source_target_pairs={{0,1},{1,0},{2,3},{3,2},{4,5},{5,4},{6,7},{7,6},{8,9},{9,8},{10,11... | collective-permute-start | bytes 393224 | tf_op jit(solution)/shard_map/ppermute | solution.py:213
  39.9 14.0 %collective-permute-start.7 = (f32[16,1024]{1,0:T(8,128)S(1)}, f32[16,1024]{1,0:T(8,128)S(1)}, u32[]{:S(2)}, u32[]{:S(2)}) collective-permute-start(f32[16,1024]{1,0:T(8,128)S(1)} %get-tuple-element.25), channel_id=1, source_target_pairs={{0,248},{4,252},{8,0},{12,4},{16,8},{20,12},{24,16},{28,20},{32,24... | collective-permute-start | bytes 196616 | tf_op jit(solution)/shard_map/ppermute | solution.py:208
  49.2 4.7 %collective-permute-start.6 = (f32[16,1024]{1,0:T(8,128)S(1)}, f32[16,1024]{1,0:T(8,128)S(1)}, u32[]{:S(2)}, u32[]{:S(2)}) collective-permute-start(f32[16,1024]{1,0:T(8,128)S(1)} %add.40), channel_id=1, source_target_pairs={{0,252},{4,0},{8,4},{12,8},{16,12},{20,16},{24,20},{28,24},{32,28}... | collective-permute-start | bytes 196616 | tf_op jit(solution)/shard_map/ppermute | solution.py:208
  50.5 4.1 %collective-permute-start.5 = (f32[16,1024]{1,0:T(8,128)S(1)}, f32[16,1024]{1,0:T(8,128)S(1)}, u32[]{:S(2)}, u32[]{:S(2)}) collective-permute-start(f32[16,1024]{1,0:T(8,128)S(1)} %slice.17), channel_id=1, source_target_pairs={{0,2},{1,3},{2,0},{3,1},{4,6},{5,7},{6,4},{7,5},{8,10},{9,11},{10,... | collective-permute-start | bytes 196616 | tf_op jit(solution)/shard_map/ppermute | solution.py:213

commit v3 on v2

--- a/solution.py
+++ b/solution.py
@@ -87,24 +87,24 @@
     b_ref[...] = features(x_ref[:DIMS, :], False)
 
 
-def tile_kernel(both, at_ref, v_ref, b_ref, *rest):
+def tile_kernel(both, start, count, at_ref, v_ref, b_ref, *rest):
     if both:
         x_ref, fwd_ref, bwd_ref, vc_ref, facc_ref = rest[:5]
     else:
         bwd_ref = rest[0]
     vr_ref, acc_ref, even_ref, odd_ref, hi_ref, lo_ref, slot_ref = rest[5 if both else 1 :]
-    across, groups = b_ref.shape[1] // TILE, at_ref.shape[0] // (TILE * GROUP)
+    across, groups = b_ref.shape[1] // TILE, count // (TILE * GROUP)
     down = min(STEP_TILES // (GROUP * across), groups)
     slot_ref[0] = 0
     slot = slot_ref[0]
     if both:
         vc_ref[...] = halves(x_ref[DIMS:, :], BF16)
         facc_ref[...] = jnp.zeros_like(facc_ref)
-    vr_ref[...] = halves(v_ref[DIMS:, :], BF16)
+    vr_ref[...] = halves(v_ref[DIMS:, start : start + count], BF16)
     acc_ref[...] = jnp.zeros_like(acc_ref)
 
     def distances(ref, i, j):
-        rows = pl.ds(pl.multiple_of(i * TILE * GROUP, TILE * GROUP), TILE * GROUP)
+        rows = pl.ds(pl.multiple_of(start + i * TILE * GROUP, TILE * GROUP), TILE * GROUP)
         d2 = dot(at_ref[rows, :], b_ref[:, j * TILE : (j + 1) * TILE], 1, 0)
         ref[0] = jnp.maximum(d2, 1e-30)
 
@@ -174,14 +174,14 @@
     )(x)
 
 
-def tiles(at, v, b, x=None):
-    n, width = at.shape[0], b.shape[1]
+def tiles(at, v, b, x=None, start=0, n=None):
+    n, width = n or at.shape[0], b.shape[1]
     both = x is not None
     bwd = jax.ShapeDtypeStruct((RHS, width), F32)
     fwd = jax.ShapeDtypeStruct((RHS, n), F32)
     more = [pltpu.VMEM((2 * RHS, width), BF16), pltpu.VMEM((2 * RHS, n), F32)] if both else []
     return pl.pallas_call(
-        functools.partial(tile_kernel, both),
+        functools.partial(tile_kernel, both, start, n),
         out_shape=(fwd, bwd) if both else bwd,
         in_specs=[VMEM] * (4 if both else 3),
         out_specs=(VMEM, VMEM) if both else VMEM,
@@ -218,36 +218,43 @@
 
 
 def body(points, vectors, inv_length, noise):
-    own = jnp.concatenate([points * inv_length[:, None] * POINT_SCALE, vectors], axis=0)
+    scaled = points * inv_length[:, None] * POINT_SCALE
+    row = lax.broadcasted_iota(jnp.int32, (DIMS + RHS, points.shape[1]), 0)
+    own = jnp.where(
+        row < DIMS, jnp.pad(scaled, ((0, RHS), (0, 0))), jnp.pad(vectors, ((DIMS, 0), (0, 0)))
+    )
     width = own.shape[1]
+    near = swapped(own, 1)
     far = swapped(own, 2)
     two = shifted(own, 2)
     at0, b0 = first(own)
     total = tiles(at0, own, b0)
+    near = after(near, total)
+    at_near = prep(near, True)
+    total = total + tiles(at_near, near, b0)
     far = after(far, total)
-    pair = jnp.concatenate([own, far], axis=1)
-    other = swapped(pair, 1)
+    cross = swapped(far, 1)
     one = shifted(after(own, far), 1)
-    at1 = prep(far, True)
-    total = total + tiles(at1, far, b0)
-    other = after(other, total)
-    at_other = prep(other, True)
-    total = total + tiles(at_other, other, b0)
-    block = jnp.concatenate([pair, other], axis=1)
-    at_pair = jnp.concatenate([at0, at1], axis=0)
-    at = jnp.concatenate([at_pair, at_other], axis=0)
-    two = after(two, total)
-    fwd2, ret2 = tiles(at, block, prep(two, False), two)
+    at_far = prep(far, True)
+    b2 = prep(after(two, total), False)
+    cross = after(cross, b2)
+    at_cross = prep(cross, True)
+    block = jnp.concatenate([own, far, cross, near], axis=1)
+    at = jnp.concatenate([at0, at_far, at_cross, at_near], axis=0)
+    fwd2, ret2 = tiles(at, block, b2, two)
     back2 = shifted(ret2, -2)
     one = after(one, ret2)
     b1 = prep(one, False)
-    fwd_other, ret_other = tiles(at_other, other, b1, one)
+    fwd_other, ret_other = tiles(at, block, b1, one, 2 * width, 2 * width)
     give_near = swapped(fwd_other + fwd2[:, 2 * width :], 1)
-    fwd_pair, ret_pair = tiles(at_pair, after(pair, ret_other), b1, one)
+    fwd_pair, ret_pair = tiles(at, after(block, ret_other), b1, one, 0, 2 * width)
     back1 = shifted(ret_other + ret_pair, -1)
-    rows = fwd_pair + fwd2[:, : 2 * width] + give_near
-    give_far = swapped(rows[:, width:], 2)
-    return total + rows[:, :width] + give_far + back1 + back2 + noise[None, :] * vectors
+    rows = fwd_pair + fwd2[:, : 2 * width]
+    rows_far = rows[:, width:] + give_near[:, :width]
+    give_far = swapped(rows_far, 2)
+    total = total + tiles(at, after(block, rows_far), b0, None, width, 2 * width)
+    total = total + rows[:, :width] + give_near[:, width:]
+    return total + give_far + back1 + back2 + noise[None, :] * vectors
 
 
 def solution(mesh):

time: 55.4 us -> 53.5 us (0.966)
  starting transfers between devices: 17.1 us -> 14.7 us
  waiting for transfers between devices: 5.95 us -> 6.69 us
    ppermute x4 -> x5, starting transfers between devices: 7.79 us -> 6.01 us  [swapped(): return lax.ppermute(value, 'split', [(s, s ^ mask) for s in range(count)])]
    concatenate x5 -> x2, other arithmetic: 1.14 us -> 0.19 us  [the longest x1 0.14 us: body(): at = jnp.concatenate([at0, at_far, at_cross, at_near], axis=0)]
    select_n x0 -> x1, other arithmetic: none -> 0.93 us  [body(): jnp.where(row < DIMS, jnp.pad(scaled, ((0, RHS), (0, 0))), jnp.pad(vector...]
    ppermute x4, waiting for transfers between devices: 4.22 us -> 4.99 us  [shifted(): lax.ppermute(value, 'blk', [(s, (s + steps) % count) for s in range(count)])]
    ppermute x4, starting transfers between devices: 9.3 us -> 8.68 us  [shifted(): lax.ppermute(value, 'blk', [(s, (s + steps) % count) for s in range(count)])]
    ppermute x4 -> x5, waiting for transfers between devices: 1.73 us -> 1.7 us  [swapped(): return lax.ppermute(value, 'split', [(s, s ^ mask) for s in range(count)])]
  transfers between devices with their start and end apart: 8 -> 9, of which waited for: 4 -> 3; matrix products, arithmetic and copies ran while one was open for 1% -> 0% of each run, Pallas kernels for 44% -> 36%
where the time goes in v3:
time: 53.5 us; the launch traced here: 53.4 us
  Pallas kernels  29 us (54%)
  starting transfers between devices  14.7 us (27%)
  waiting for transfers between devices  6.69 us (13%)
  other arithmetic  2.85 us (5%)
    pallas_call x6, Pallas kernels, tiles(): pl.pallas_call(functools.partial(tile_kernel, both, start, n), out_shape=...  28.1 us
    ppermute x4, starting transfers between devices, shifted(): lax.ppermute(value, 'blk', [(s, (s + steps) % count) for s in range(count)])  8.68 us
    ppermute x5, starting transfers between devices, swapped(): return lax.ppermute(value, 'split', [(s, s ^ mask) for s in range(count)])  6.01 us
    ppermute x4, waiting for transfers between devices, shifted(): lax.ppermute(value, 'blk', [(s, (s + steps) % count) for s in range(count)])  4.99 us
    ppermute x5, waiting for transfers between devices, swapped(): return lax.ppermute(value, 'split', [(s, s ^ mask) for s in range(count)])  1.7 us
  transfers between devices with their start and end apart: 9, of which 3 were waited for; matrix products, arithmetic and copies ran while one was open for 0% of the time, Pallas kernels for 36%

profile of v3, /device:TPU:1, one launch (start us, length us, event | category | flops | bytes accessed | tf_op | source)
XLA Modules:
  0.0 53.4 jit_solution(1910586496297003625)
XLA Ops:
  0.0 1.0 %multiply_multiply_fusion = f32[32,1024]{1,0:T(8,128)S(1)} fusion(f32[32,1024]{1,0:T(8,128)} %param.4, f32[32]{0:T(128)} %param.6), kind=kLoop, calls=%fused_computation.5 | loop fusion | flops 65536 | bytes 262272 | tf_op jit(solution)/shard_map/mul | solution.py:221
  1.0 0.9 %pad_select_fusion.x_ref.v_ref = f32[48,1024]{1,0:T(8,128)S(1)} fusion(f32[16,1024]{1,0:T(8,128)} %param.5, f32[32,1024]{1,0:T(8,128)S(1)} %multiply_multiply_fusion, pred[48]{0:T(512)(128)(4,1)S(1)} %iota_compare_fusion), kind=kLoop, calls=%fused_computation.2 | loop fusion | flops 49152 | bytes 393264 | tf_op jit(solution)/shard_map/jit(_where)/select_n | solution.py:223
  1.9 3.3 %collective-permute-start = (f32[48,1024]{1,0:T(8,128)S(1)}, f32[48,1024]{1,0:T(8,128)S(1)}, u32[]{:S(2)}, u32[]{:S(2)}) collective-permute-start(f32[48,1024]{1,0:T(8,128)S(1)} %pad_select_fusion.x_ref.v_ref), channel_id=1, source_target_pairs={{0,1},{1,0},{2,3},{3,2},{4,5},{5,4},{6,7},{7,6},{8,9},{9,8},{10,11... | collective-permute-start | bytes 589832 | tf_op jit(solution)/shard_map/ppermute | solution.py:213
  5.3 1.1 %collective-permute-start.3 = (f32[48,1024]{1,0:T(8,128)S(1)}, f32[48,1024]{1,0:T(8,128)S(1)}, u32[]{:S(2)}, u32[]{:S(2)}) collective-permute-start(f32[48,1024]{1,0:T(8,128)S(1)} %pad_select_fusion.x_ref.v_ref), channel_id=1, source_target_pairs={{0,8},{4,12},{8,16},{12,20},{16,24},{20,28},{24,32},{28,36},{32,40... | collective-permute-start | bytes 589832 | tf_op jit(solution)/shard_map/ppermute | solution.py:208
  6.4 0.2 first.1
  6.6 2.0 %own.3 = f32[16,1024]{1,0:T(8,128)S(1)} custom-call(bf16[1024,256]{1,0:T(8,128)(2,1)S(1)} %get-tuple-element.21.at_ref, f32[48,1024]{1,0:T(8,128)S(1)} %pad_select_fusion.x_ref.v_ref, bf16[256,1024]{1,0:T(8,128)(2,1)S(1)} %get-tuple-element.22.b_ref), custom_call_target="tpu_custom_call" | custom-call | flops 8388608 | bytes 16384 | tf_op jit(solution)/shard_map/own/pallas_call | solution.py:183
  8.6 0.2 rows.3.at_ref
  8.9 2.0 %own.4 = f32[16,1024]{1,0:T(8,128)S(1)} custom-call(bf16[1024,256]{1,0:T(8,128)(2,1)S(1)} %rows.3.at_ref, f32[48,1024]{1,0:T(8,128)S(1)} %collective-permute-done.x_ref.v_ref, bf16[256,1024]{1,0:T(8,128)(2,1)S(1)} %get-tuple-element.22.b_ref), custom_call_target="tpu_custom_call" | custom-call | flops 8388608 | bytes 16384 | tf_op jit(solution)/shard_map/own/pallas_call | solution.py:183
  10.9 0.8 %collective-permute-done.1.x_ref = f32[48,1024]{1,0:T(8,128)S(1)} collective-permute-done((f32[48,1024]{1,0:T(8,128)S(1)}, f32[48,1024]{1,0:T(8,128)S(1)}, u32[]{:S(2)}, u32[]{:S(2)}) %collective-permute-start.1) | collective-permute-done | bytes 196640 | tf_op jit(solution)/shard_map/ppermute | solution.py:213
  11.7 0.9 %collective-permute-start.2 = (f32[48,1024]{1,0:T(8,128)S(1)}, f32[48,1024]{1,0:T(8,128)S(1)}, u32[]{:S(2)}, u32[]{:S(2)}) collective-permute-start(f32[48,1024]{1,0:T(8,128)S(1)} %collective-permute-done.1.x_ref), channel_id=1, source_target_pairs={{0,1},{1,0},{2,3},{3,2},{4,5},{5,4},{6,7},{7,6},{8,9},{9,8},{10,11... | collective-permute-start | bytes 589832 | tf_op jit(solution)/shard_map/ppermute | solution.py:213
  12.6 0.2 rows.4
  12.8 5.0 %collective-permute-done.3.x_ref.rest_0_ = f32[48,1024]{1,0:T(8,128)S(1)} collective-permute-done((f32[48,1024]{1,0:T(8,128)S(1)}, f32[48,1024]{1,0:T(8,128)S(1)}, u32[]{:S(2)}, u32[]{:S(2)}) %collective-permute-start.3) | collective-permute-done | bytes 196640 | tf_op jit(solution)/shard_map/ppermute | solution.py:208
  17.8 2.7 %collective-permute-start.4 = (f32[48,1024]{1,0:T(8,128)S(1)}, f32[48,1024]{1,0:T(8,128)S(1)}, u32[]{:S(2)}, u32[]{:S(2)}) collective-permute-start(f32[48,1024]{1,0:T(8,128)S(1)} %pad_select_fusion.x_ref.v_ref), channel_id=1, source_target_pairs={{0,4},{4,8},{8,12},{12,16},{16,20},{20,24},{24,28},{28,32},{32,36}... | collective-permute-start | bytes 589832 | tf_op jit(solution)/shard_map/ppermute | solution.py:208
  20.5 0.2 rows.5
  20.9 10.2 %both.3 = (f32[16,4096]{1,0:T(8,128)S(1)}, f32[16,1024]{1,0:T(8,128)S(1)}) custom-call(bf16[4096,256]{1,0:T(8,128)(2,1)S(1)} %pad_maximum_fusion.at_ref, f32[48,4096]{1,0:T(8,128)S(1)} %pad_maximum_fusion.1.v_ref, bf16[256,1024]{1,0:T(8,128)(2,1)S(1)} %cols.2.b_ref, f32[48,1024]{1,0:T(8,128)S(1)} %collective-permute-done.3.x_ref.rest_0_), custom_call_target="tpu_custom_call" | custom-call | flops 33554432 | bytes 65536 | tf_op jit(solution)/shard_map/both/pallas_call | solution.py:183
  31.3 5.0 %both.4 = (f32[16,2048]{1,0:T(8,128)S(1)}, f32[16,1024]{1,0:T(8,128)S(1)}) custom-call(bf16[4096,256]{1,0:T(8,128)(2,1)S(1)} %pad_maximum_fusion.at_ref, f32[48,4096]{1,0:T(8,128)S(1)} %pad_maximum_fusion.1.v_ref, bf16[256,1024]{1,0:T(8,128)(2,1)S(1)} %cols.3.b_ref, f32[48,1024]{1,0:T(8,128)S(1)} %collective-permute-done.4.x_ref.rest_0_), custom_call_target="tpu_custom_call" | custom-call | flops 16777216 | bytes 32768 | tf_op jit(solution)/shard_map/both/pallas_call | solution.py:183
  36.2 5.0 %both.5 = (f32[16,2048]{1,0:T(8,128)S(1)}, f32[16,1024]{1,0:T(8,128)S(1)}) custom-call(bf16[4096,256]{1,0:T(8,128)(2,1)S(1)} %pad_maximum_fusion.at_ref, f32[48,4096]{1,0:T(8,128)S(1)} %pad_maximum_fusion.1.v_ref, bf16[256,1024]{1,0:T(8,128)(2,1)S(1)} %cols.3.b_ref, f32[48,1024]{1,0:T(8,128)S(1)} %collective-permute-done.4.x_ref.rest_0_), custom_call_target="tpu_custom_call" | custom-call | flops 16777216 | bytes 32768 | tf_op jit(solution)/shard_map/both/pallas_call | solution.py:183
  41.3 1.2 %collective-permute-start.5 = (f32[16,2048]{1,0:T(8,128)S(1)}, f32[16,2048]{1,0:T(8,128)S(1)}, u32[]{:S(2)}, u32[]{:S(2)}) collective-permute-start(f32[16,2048]{1,0:T(8,128)S(1)} %get-tuple-element.38), channel_id=1, source_target_pairs={{0,1},{1,0},{2,3},{3,2},{4,5},{5,4},{6,7},{7,6},{8,9},{9,8},{10,11... | collective-permute-start | bytes 393224 | tf_op jit(solution)/shard_map/ppermute | solution.py:213
  42.5 1.5 %collective-permute-start.8 = (f32[16,1024]{1,0:T(8,128)S(1)}, f32[16,1024]{1,0:T(8,128)S(1)}, u32[]{:S(2)}, u32[]{:S(2)}) collective-permute-start(f32[16,1024]{1,0:T(8,128)S(1)} %get-tuple-element.28), channel_id=1, source_target_pairs={{0,248},{4,252},{8,0},{12,4},{16,8},{20,12},{24,16},{28,20},{32,24... | collective-permute-start | bytes 196616 | tf_op jit(solution)/shard_map/ppermute | solution.py:208
  44.0 3.4 %collective-permute-start.7 = (f32[16,1024]{1,0:T(8,128)S(1)}, f32[16,1024]{1,0:T(8,128)S(1)}, u32[]{:S(2)}, u32[]{:S(2)}) collective-permute-start(f32[16,1024]{1,0:T(8,128)S(1)} %add.48), channel_id=1, source_target_pairs={{0,252},{4,0},{8,4},{12,8},{16,12},{20,16},{24,20},{28,24},{32,28}... | collective-permute-start | bytes 196616 | tf_op jit(solution)/shard_map/ppermute | solution.py:208
  47.4 0.6 %collective-permute-start.6 = (f32[16,1024]{1,0:T(8,128)S(1)}, f32[16,1024]{1,0:T(8,128)S(1)}, u32[]{:S(2)}, u32[]{:S(2)}) collective-permute-start(f32[16,1024]{1,0:T(8,128)S(1)} %slice_add_fusion.4), channel_id=1, source_target_pairs={{0,2},{1,3},{2,0},{3,1},{4,6},{5,7},{6,4},{7,5},{8,10},{9,11},{10,... | collective-permute-start | bytes 196616 | tf_op jit(solution)/shard_map/ppermute | solution.py:213
  48.0 3.8 %own.5 = f32[16,1024]{1,0:T(8,128)S(1)} custom-call(bf16[4096,256]{1,0:T(8,128)(2,1)S(1)} %pad_maximum_fusion.at_ref, f32[48,4096]{1,0:T(8,128)S(1)} %pad_maximum_fusion.1.v_ref, bf16[256,1024]{1,0:T(8,128)(2,1)S(1)} %get-tuple-element.22.b_ref), custom_call_target="tpu_custom_call" | custom-call | flops 16777216 | bytes 32768 | tf_op jit(solution)/shard_map/own/pallas_call | solution.py:183
  51.8 0.9 %collective-permute-done.6 = f32[16,1024]{1,0:T(8,128)S(1)} collective-permute-done((f32[16,1024]{1,0:T(8,128)S(1)}, f32[16,1024]{1,0:T(8,128)S(1)}, u32[]{:S(2)}, u32[]{:S(2)}) %collective-permute-start.6) | collective-permute-done | bytes 65568 | tf_op jit(solution)/shard_map/ppermute | solution.py:213
  52.7 0.7 %fusion.3 = f32[16,1024]{1,0:T(8,128)} fusion(f32[16,1024]{1,0:T(8,128)S(1)} %collective-permute-done.8, f32[16,1024]{1,0:T(8,128)S(1)} %collective-permute-done.7, f32[16,1024]{1,0:T(8,128)S(1)} %collective-permute-done.6, f32[16,2048]{1,0:T(8,128)S(1)} %collective-permute-done.5, f32[16,2048]{1,0:T(8,128)S(1)} %get-tuple-element.37, ...), kind=kLoop, calls=%fused_computation.10 | loop fusion | flops 131072 | bytes 593920 | tf_op jit(solution)/shard_map/add | solution.py:257
  (20 shorter events, 0.5 us)
Async XLA Ops:
  1.9 6.7 %collective-permute-start = (f32[48,1024]{1,0:T(8,128)S(1)}, f32[48,1024]{1,0:T(8,128)S(1)}, u32[]{:S(2)}, u32[]{:S(2)}) collective-permute-start(f32[48,1024]{1,0:T(8,128)S(1)} %pad_select_fusion.x_ref.v_ref), channel_id=1, source_target_pairs={{0,1},{1,0},{2,3},{3,2},{4,5},{5,4},{6,7},{7,6},{8,9},{9,8},{10,11... | collective-permute-start | bytes 589832 | tf_op jit(solution)/shard_map/ppermute | solution.py:213
  5.3 6.5 %collective-permute-start.1 = (f32[48,1024]{1,0:T(8,128)S(1)}, f32[48,1024]{1,0:T(8,128)S(1)}, u32[]{:S(2)}, u32[]{:S(2)}) collective-permute-start(f32[48,1024]{1,0:T(8,128)S(1)} %pad_select_fusion.x_ref.v_ref), channel_id=1, source_target_pairs={{0,2},{1,3},{2,0},{3,1},{4,6},{5,7},{6,4},{7,5},{8,10},{9,11},{10,... | collective-permute-start | bytes 589832 | tf_op jit(solution)/shard_map/ppermute | solution.py:213
  5.3 12.5 %collective-permute-start.3 = (f32[48,1024]{1,0:T(8,128)S(1)}, f32[48,1024]{1,0:T(8,128)S(1)}, u32[]{:S(2)}, u32[]{:S(2)}) collective-permute-start(f32[48,1024]{1,0:T(8,128)S(1)} %pad_select_fusion.x_ref.v_ref), channel_id=1, source_target_pairs={{0,8},{4,12},{8,16},{12,20},{16,24},{20,28},{24,32},{28,36},{32,40... | collective-permute-start | bytes 589832 | tf_op jit(solution)/shard_map/ppermute | solution.py:208
  11.7 8.8 %collective-permute-start.2 = (f32[48,1024]{1,0:T(8,128)S(1)}, f32[48,1024]{1,0:T(8,128)S(1)}, u32[]{:S(2)}, u32[]{:S(2)}) collective-permute-start(f32[48,1024]{1,0:T(8,128)S(1)} %collective-permute-done.1.x_ref), channel_id=1, source_target_pairs={{0,1},{1,0},{2,3},{3,2},{4,5},{5,4},{6,7},{7,6},{8,9},{9,8},{10,11... | collective-permute-start | bytes 589832 | tf_op jit(solution)/shard_map/ppermute | solution.py:213
  17.8 13.4 %collective-permute-start.4 = (f32[48,1024]{1,0:T(8,128)S(1)}, f32[48,1024]{1,0:T(8,128)S(1)}, u32[]{:S(2)}, u32[]{:S(2)}) collective-permute-start(f32[48,1024]{1,0:T(8,128)S(1)} %pad_select_fusion.x_ref.v_ref), channel_id=1, source_target_pairs={{0,4},{4,8},{8,12},{12,16},{16,20},{20,24},{24,28},{28,32},{32,36}... | collective-permute-start | bytes 589832 | tf_op jit(solution)/shard_map/ppermute | solution.py:208
  41.3 11.5 %copy-start = (f32[16,1024]{1,0:T(8,128)S(1)}, f32[16,1024]{1,0:T(8,128)}, u32[]{:S(2)}) copy-start(f32[16,1024]{1,0:T(8,128)} %param.5) | copy-start | bytes 196612
  41.3 11.4 %copy-start.1 = (f32[1024]{0:T(1024)S(1)}, f32[1024]{0:T(1024)}, u32[]{:S(2)}) copy-start(f32[1024]{0:T(1024)} %param.7) | copy-start | bytes 12292
  41.3 6.1 %collective-permute-start.5 = (f32[16,2048]{1,0:T(8,128)S(1)}, f32[16,2048]{1,0:T(8,128)S(1)}, u32[]{:S(2)}, u32[]{:S(2)}) collective-permute-start(f32[16,2048]{1,0:T(8,128)S(1)} %get-tuple-element.38), channel_id=1, source_target_pairs={{0,1},{1,0},{2,3},{3,2},{4,5},{5,4},{6,7},{7,6},{8,9},{9,8},{10,11... | collective-permute-start | bytes 393224 | tf_op jit(solution)/shard_map/ppermute | solution.py:213
  42.5 9.3 %collective-permute-start.8 = (f32[16,1024]{1,0:T(8,128)S(1)}, f32[16,1024]{1,0:T(8,128)S(1)}, u32[]{:S(2)}, u32[]{:S(2)}) collective-permute-start(f32[16,1024]{1,0:T(8,128)S(1)} %get-tuple-element.28), channel_id=1, source_target_pairs={{0,248},{4,252},{8,0},{12,4},{16,8},{20,12},{24,16},{28,20},{32,24... | collective-permute-start | bytes 196616 | tf_op jit(solution)/shard_map/ppermute | solution.py:208
  44.0 7.8 %collective-permute-start.7 = (f32[16,1024]{1,0:T(8,128)S(1)}, f32[16,1024]{1,0:T(8,128)S(1)}, u32[]{:S(2)}, u32[]{:S(2)}) collective-permute-start(f32[16,1024]{1,0:T(8,128)S(1)} %add.48), channel_id=1, source_target_pairs={{0,252},{4,0},{8,4},{12,8},{16,12},{20,16},{24,20},{28,24},{32,28}... | collective-permute-start | bytes 196616 | tf_op jit(solution)/shard_map/ppermute | solution.py:208
  47.4 5.3 %collective-permute-start.6 = (f32[16,1024]{1,0:T(8,128)S(1)}, f32[16,1024]{1,0:T(8,128)S(1)}, u32[]{:S(2)}, u32[]{:S(2)}) collective-permute-start(f32[16,1024]{1,0:T(8,128)S(1)} %slice_add_fusion.4), channel_id=1, source_target_pairs={{0,2},{1,3},{2,0},{3,1},{4,6},{5,7},{6,4},{7,5},{8,10},{9,11},{10,... | collective-permute-start | bytes 196616 | tf_op jit(solution)/shard_map/ppermute | solution.py:213

commit v4 on v3

--- a/solution.py
+++ b/solution.py
@@ -11,9 +11,10 @@
 ROOT_FIVE = 2.23606797749979
 LOG2E = 1.4426950408889634
 POINT_SCALE = ROOT_FIVE * LOG2E
+OUT_SCALE = SIGNAL / (3.0 * LOG2E * LOG2E)
 SHIFT = 1.5 * LOG2E
 FLOOR = 0.75 * LOG2E * LOG2E
-OUT_SCALE = SIGNAL / (3.0 * LOG2E * LOG2E) * 2.0**SHIFT
+LIFT = 14.0
 DIMS = 32
 RHS = 16
 DEPTH = 256
@@ -22,7 +23,8 @@
 STEP_TILES = 32
 BF16 = jnp.bfloat16
 F32 = jnp.float32
-LOW = jnp.bfloat16
+F8 = jnp.float8_e4m3fn
+PEAK = 128.0
 
 
 def dot(a, b, ca, cb):
@@ -62,45 +64,68 @@
     return jnp.concatenate([hi, (v - hi.astype(F32)).astype(kind)], axis=0)
 
 
-def kernel_tile(b2):
-    w = -SHIFT - b2 * lax.rsqrt(b2)
-    t = (w * w + FLOOR) * jnp.exp2(w)
+def kernel_tile(b2, low):
+    if low == BF16:
+        w = -SHIFT - b2 * lax.rsqrt(b2)
+        t = (w * w + FLOOR) * jnp.exp2(w)
+    else:
+        b = b2 * lax.rsqrt(b2)
+        t = ((b + 3.0 * LOG2E) * b + 3.0 * LOG2E * LOG2E) * jnp.exp2(LIFT - b)
     hi = t.astype(BF16)
-    return hi, (t - hi.astype(F32)).astype(LOW)
-
-
-def fold(x):
-    return (x[:RHS] + x[RHS:]) * OUT_SCALE
-
-
-def first_kernel(x_ref, at_ref, b_ref):
-    x = x_ref[:DIMS, :]
+    return hi, (t - hi.astype(F32)).astype(low)
+
+
+def leveled(v, low):
+    if low == BF16:
+        return v, OUT_SCALE * 2.0**SHIFT
+    top = jnp.maximum(jnp.max(jnp.abs(v), axis=1, keepdims=True), 1e-30)
+    return v * (PEAK / top), top * (OUT_SCALE * 2.0**-LIFT / PEAK)
+
+
+def fold(x, undo):
+    return (x[:RHS] + x[RHS:]) * undo
+
+
+def scaled(x_ref, inv):
+    return (x_ref[:DIMS, :] * inv) * POINT_SCALE
+
+
+def first_kernel(x_ref, inv_ref, at_ref, b_ref, inv_col_ref):
+    row = lax.broadcasted_iota(jnp.int32, (DIMS, DIMS), 0)
+    col = lax.broadcasted_iota(jnp.int32, (DIMS, DIMS), 1)
+    inv = jnp.sum(jnp.where(row == col, inv_ref[...], 0.0), axis=1, keepdims=True)
+    inv_col_ref[...] = jnp.broadcast_to(inv, inv_col_ref.shape)
+    x = scaled(x_ref, inv)
     at_ref[...] = features(x, True).T
     b_ref[...] = features(x, False)
 
 
-def rows_kernel(x_ref, at_ref):
-    at_ref[...] = features(x_ref[:DIMS, :], True).T
-
-
-def cols_kernel(x_ref, b_ref):
-    b_ref[...] = features(x_ref[:DIMS, :], False)
-
-
-def tile_kernel(both, start, count, at_ref, v_ref, b_ref, *rest):
+def rows_kernel(x_ref, inv_ref, at_ref):
+    at_ref[...] = features(scaled(x_ref, inv_ref[:, :1]), True).T
+
+
+def cols_kernel(x_ref, inv_ref, b_ref):
+    b_ref[...] = features(scaled(x_ref, inv_ref[:, :1]), False)
+
+
+def tile_kernel(both, low, start, count, at_ref, v_ref, b_ref, *rest):
     if both:
-        x_ref, fwd_ref, bwd_ref, vc_ref, facc_ref = rest[:5]
+        x_ref, fwd_ref, bwd_ref, vc_ref, vc_low_ref, facc_ref = rest[:6]
     else:
         bwd_ref = rest[0]
-    vr_ref, acc_ref, even_ref, odd_ref, hi_ref, lo_ref, slot_ref = rest[5 if both else 1 :]
+    vr_ref, vr_low_ref, acc_ref, even_ref, odd_ref, hi_ref, lo_ref, slot_ref = rest[6 if both else 1 :]
     across, groups = b_ref.shape[1] // TILE, count // (TILE * GROUP)
     down = min(STEP_TILES // (GROUP * across), groups)
     slot_ref[0] = 0
     slot = slot_ref[0]
     if both:
-        vc_ref[...] = halves(x_ref[DIMS:, :], BF16)
+        vc, undo_c = leveled(x_ref[DIMS:, :], low)
+        vc_ref[...] = halves(vc, BF16)
+        vc_low_ref[...] = halves(vc, low)
         facc_ref[...] = jnp.zeros_like(facc_ref)
-    vr_ref[...] = halves(v_ref[DIMS:, start : start + count], BF16)
+    vr, undo_r = leveled(v_ref[DIMS:, start : start + count], low)
+    vr_ref[...] = halves(vr, BF16)
+    vr_low_ref[...] = halves(vr, low)
     acc_ref[...] = jnp.zeros_like(acc_ref)
 
     def distances(ref, i, j):
@@ -111,11 +136,9 @@
     def products(hi, lo, i, j):
         cols = slice(j * TILE, (j + 1) * TILE)
         rows = pl.ds(pl.multiple_of(i * TILE, TILE), TILE)
-        vr = vr_ref[:, rows]
-        acc_ref[:, cols] += dot(vr, hi, 1, 0) + dot(vr, lo, 1, 0)
+        acc_ref[:, cols] += dot(vr_ref[:, rows], hi, 1, 0) + dot(vr_low_ref[:, rows], lo, 1, 0)
         if both:
-            vc = vc_ref[:, cols]
-            facc_ref[:, rows] += dot(vc, hi, 1, 1) + dot(vc, lo, 1, 1)
+            facc_ref[:, rows] += dot(vc_ref[:, cols], hi, 1, 1) + dot(vc_low_ref[:, cols], lo, 1, 1)
 
     hi_ref[...] = jnp.zeros_like(hi_ref)
     lo_ref[...] = jnp.zeros_like(lo_ref)
@@ -132,67 +155,77 @@
             distances(later, ahead, (t + 1) % across)
             for g in range(GROUP):
                 products(hi, lo, i, j)
-                hi, lo = kernel_tile(now[slot, g * TILE : (g + 1) * TILE, :])
+                hi, lo = kernel_tile(now[slot, g * TILE : (g + 1) * TILE, :], low)
                 i, j = (k * down + t // across) * GROUP + g, t % across
         hi_ref[...], lo_ref[...] = hi, lo
         return carry
 
     lax.fori_loop(0, groups // down, step, 0)
     products(hi_ref[...], lo_ref[...], groups * GROUP - 1, across - 1)
-    bwd_ref[...] = fold(acc_ref[...])
+    bwd_ref[...] = fold(acc_ref[...], undo_r)
     if both:
-        fwd_ref[...] = fold(facc_ref[...])
+        fwd_ref[...] = fold(facc_ref[...], undo_c)
 
 
 VMEM = pl.BlockSpec(memory_space=pltpu.VMEM)
 PARAMS = pltpu.CompilerParams(vmem_limit_bytes=40 * 2**20)
 
 
-def first(x):
+def first(x, inv):
     n = x.shape[1]
     return pl.pallas_call(
         first_kernel,
-        out_shape=(jax.ShapeDtypeStruct((n, DEPTH), BF16), jax.ShapeDtypeStruct((DEPTH, n), BF16)),
-        in_specs=[VMEM],
-        out_specs=(VMEM, VMEM),
+        out_shape=(
+            jax.ShapeDtypeStruct((n, DEPTH), BF16),
+            jax.ShapeDtypeStruct((DEPTH, n), BF16),
+            jax.ShapeDtypeStruct((DIMS, 128), F32),
+        ),
+        in_specs=[VMEM, VMEM],
+        out_specs=(VMEM, VMEM, VMEM),
         compiler_params=PARAMS,
         cost_estimate=pl.CostEstimate(flops=n * 64, bytes_accessed=n * 16, transcendentals=0),
         name="first",
-    )(x)
-
-
-def prep(x, rows):
+    )(x, inv)
+
+
+def prep(x, inv, rows):
     n = x.shape[1]
     return pl.pallas_call(
         rows_kernel if rows else cols_kernel,
         out_shape=jax.ShapeDtypeStruct((n, DEPTH) if rows else (DEPTH, n), BF16),
-        in_specs=[VMEM],
+        in_specs=[VMEM, VMEM],
         out_specs=VMEM,
         compiler_params=PARAMS,
         cost_estimate=pl.CostEstimate(flops=n * 64, bytes_accessed=n * 16, transcendentals=0),
         name="rows" if rows else "cols",
-    )(x)
+    )(x, inv)
 
 
 def tiles(at, v, b, x=None, start=0, n=None):
     n, width = n or at.shape[0], b.shape[1]
     both = x is not None
+    low = F8 if both else BF16
     bwd = jax.ShapeDtypeStruct((RHS, width), F32)
     fwd = jax.ShapeDtypeStruct((RHS, n), F32)
-    more = [pltpu.VMEM((2 * RHS, width), BF16), pltpu.VMEM((2 * RHS, n), F32)] if both else []
+    more = [
+        pltpu.VMEM((2 * RHS, width), BF16),
+        pltpu.VMEM((2 * RHS, width), low),
+        pltpu.VMEM((2 * RHS, n), F32),
+    ]
     return pl.pallas_call(
-        functools.partial(tile_kernel, both, start, n),
+        functools.partial(tile_kernel, both, low, start, n),
         out_shape=(fwd, bwd) if both else bwd,
         in_specs=[VMEM] * (4 if both else 3),
         out_specs=(VMEM, VMEM) if both else VMEM,
-        scratch_shapes=more
+        scratch_shapes=(more if both else [])
         + [
             pltpu.VMEM((2 * RHS, n), BF16),
+            pltpu.VMEM((2 * RHS, n), low),
             pltpu.VMEM((2 * RHS, width), F32),
             pltpu.VMEM((1, TILE * GROUP, TILE), F32),
             pltpu.VMEM((1, TILE * GROUP, TILE), F32),
             pltpu.VMEM((TILE, TILE), BF16),
-            pltpu.VMEM((TILE, TILE), LOW),
+            pltpu.VMEM((TILE, TILE), low),
             pltpu.SMEM((1,), jnp.int32),
         ],
         compiler_params=PARAMS,
@@ -218,33 +251,30 @@
 
 
 def body(points, vectors, inv_length, noise):
-    scaled = points * inv_length[:, None] * POINT_SCALE
     row = lax.broadcasted_iota(jnp.int32, (DIMS + RHS, points.shape[1]), 0)
-    own = jnp.where(
-        row < DIMS, jnp.pad(scaled, ((0, RHS), (0, 0))), jnp.pad(vectors, ((DIMS, 0), (0, 0)))
-    )
+    own = jnp.where(row < DIMS, jnp.pad(points, ((0, RHS), (0, 0))), jnp.pad(vectors, ((DIMS, 0), (0, 0))))
     width = own.shape[1]
     near = swapped(own, 1)
     far = swapped(own, 2)
     two = shifted(own, 2)
-    at0, b0 = first(own)
+    at0, b0, inv = first(own, inv_length.reshape(1, DIMS))
     total = tiles(at0, own, b0)
     near = after(near, total)
-    at_near = prep(near, True)
+    at_near = prep(near, inv, True)
     total = total + tiles(at_near, near, b0)
     far = after(far, total)
     cross = swapped(far, 1)
     one = shifted(after(own, far), 1)
-    at_far = prep(far, True)
-    b2 = prep(after(two, total), False)
+    at_far = prep(far, inv, True)
+    b2 = prep(after(two, total), inv, False)
     cross = after(cross, b2)
-    at_cross = prep(cross, True)
+    at_cross = prep(cross, inv, True)
     block = jnp.concatenate([own, far, cross, near], axis=1)
     at = jnp.concatenate([at0, at_far, at_cross, at_near], axis=0)
     fwd2, ret2 = tiles(at, block, b2, two)
     back2 = shifted(ret2, -2)
     one = after(one, ret2)
-    b1 = prep(one, False)
+    b1 = prep(one, inv, False)
     fwd_other, ret_other = tiles(at, block, b1, one, 2 * width, 2 * width)
     give_near = swapped(fwd_other + fwd2[:, 2 * width :], 1)
     fwd_pair, ret_pair = tiles(at, after(block, ret_other), b1, one, 0, 2 * width)

time: 53.5 us -> 51.3 us (0.959)
  Pallas kernels: 29 us -> 27.9 us
  waiting for transfers between devices: 6.69 us -> 5.78 us
  other arithmetic: 2.85 us -> 1.95 us
  local copies, waits for them, and re-layouts: 0.01 us -> 0.67 us
    pallas_call x6, Pallas kernels: 28.1 us -> 26.5 us  [tiles(): pl.pallas_call(functools.partial(tile_kernel, both, low, start, n), out_s...]
    mul x1 -> x0, other arithmetic: 0.98 us -> none  [body(): scaled = points * inv_length[:, None] * POINT_SCALE]
    ppermute x5, waiting for transfers between devices: 1.7 us -> 0.87 us  [swapped(): return lax.ppermute(value, 'split', [(s, s ^ mask) for s in range(count)])]
    unnamed x4 -> x6, local copies, waits for them, and re-layouts: 0.01 us -> 0.67 us
  transfers between devices with their start and end apart: 9 -> 9, of which waited for: 3 -> 2; matrix products, arithmetic and copies ran while one was open for 0% -> 0% of each run, Pallas kernels for 36% -> 37%
where the time goes in v4:
time: 51.3 us; the launch traced here: 51.2 us
  Pallas kernels  27.9 us (54%)
  starting transfers between devices  14.7 us (29%)
  waiting for transfers between devices  5.78 us (11%)
  other arithmetic  1.95 us (4%)
  local copies, waits for them, and re-layouts  0.67 us (1%)
    pallas_call x6, Pallas kernels, tiles(): pl.pallas_call(functools.partial(tile_kernel, both, low, start, n), out_s...  26.5 us
    ppermute x4, starting transfers between devices, shifted(): lax.ppermute(value, 'blk', [(s, (s + steps) % count) for s in range(count)])  8.68 us
    ppermute x5, starting transfers between devices, swapped(): return lax.ppermute(value, 'split', [(s, s ^ mask) for s in range(count)])  6.01 us
    ppermute x4, waiting for transfers between devices, shifted(): lax.ppermute(value, 'blk', [(s, (s + steps) % count) for s in range(count)])  4.91 us
    pallas_call x5, Pallas kernels, prep(): pl.pallas_call(rows_kernel if rows else cols_kernel, out_shape=jax.ShapeD...  1.14 us
    select_n x1, other arithmetic, body(): jnp.where(row < DIMS, jnp.pad(points, ((0, RHS), (0, 0))), jnp.pad(vector...  1.03 us
  transfers between devices with their start and end apart: 9, of which 2 were waited for; matrix products, arithmetic and copies ran while one was open for 0% of the time, Pallas kernels for 37%

profile of v4, /device:TPU:1, one launch (start us, length us, event | category | flops | bytes accessed | tf_op | source)
XLA Modules:
  0.0 51.2 jit_solution(6590155173083046302)
XLA Ops:
  0.0 1.0 %pad_select_fusion.x_ref.v_ref = f32[48,1024]{1,0:T(8,128)S(1)} fusion(f32[16,1024]{1,0:T(8,128)} %param.5, f32[32,1024]{1,0:T(8,128)} %param.4, pred[48]{0:T(512)(128)(4,1)S(1)} %iota_compare_fusion), kind=kLoop, calls=%fused_computation.2 | loop fusion | flops 49152 | bytes 393264 | tf_op jit(solution)/shard_map/jit(_where)/select_n | solution.py:255
  1.0 3.3 %collective-permute-start = (f32[48,1024]{1,0:T(8,128)S(1)}, f32[48,1024]{1,0:T(8,128)S(1)}, u32[]{:S(2)}, u32[]{:S(2)}) collective-permute-start(f32[48,1024]{1,0:T(8,128)S(1)} %pad_select_fusion.x_ref.v_ref), channel_id=1, source_target_pairs={{0,1},{1,0},{2,3},{3,2},{4,5},{5,4},{6,7},{7,6},{8,9},{9,8},{10,11... | collective-permute-start | bytes 589832 | tf_op jit(solution)/shard_map/ppermute | solution.py:246
  4.4 1.1 %collective-permute-start.3 = (f32[48,1024]{1,0:T(8,128)S(1)}, f32[48,1024]{1,0:T(8,128)S(1)}, u32[]{:S(2)}, u32[]{:S(2)}) collective-permute-start(f32[48,1024]{1,0:T(8,128)S(1)} %pad_select_fusion.x_ref.v_ref), channel_id=1, source_target_pairs={{0,8},{4,12},{8,16},{12,20},{16,24},{20,28},{24,32},{28,36},{32,40... | collective-permute-start | bytes 589832 | tf_op jit(solution)/shard_map/ppermute | solution.py:241
  5.5 0.7 %copy-done = f32[32]{0:T(128)S(1)} copy-done((f32[32]{0:T(128)S(1)}, f32[32]{0:T(128)}, u32[]{:S(2)}) %copy-start) | copy-done | bytes 152
  6.2 0.3 first.1
  6.5 2.0 %own.3 = f32[16,1024]{1,0:T(8,128)S(1)} custom-call(bf16[1024,256]{1,0:T(8,128)(2,1)S(1)} %get-tuple-element.22.at_ref, f32[48,1024]{1,0:T(8,128)S(1)} %pad_select_fusion.x_ref.v_ref, bf16[256,1024]{1,0:T(8,128)(2,1)S(1)} %get-tuple-element.23.b_ref), custom_call_target="tpu_custom_call" | custom-call | flops 8388608 | bytes 16384 | tf_op jit(solution)/shard_map/own/pallas_call | solution.py:215
  8.5 0.3 rows.3.at_ref
  8.8 2.0 %own.4 = f32[16,1024]{1,0:T(8,128)S(1)} custom-call(bf16[1024,256]{1,0:T(8,128)(2,1)S(1)} %rows.3.at_ref, f32[48,1024]{1,0:T(8,128)S(1)} %collective-permute-done.x_ref.v_ref, bf16[256,1024]{1,0:T(8,128)(2,1)S(1)} %get-tuple-element.23.b_ref), custom_call_target="tpu_custom_call" | custom-call | flops 8388608 | bytes 16384 | tf_op jit(solution)/shard_map/own/pallas_call | solution.py:215
  10.9 0.8 %collective-permute-start.2 = (f32[48,1024]{1,0:T(8,128)S(1)}, f32[48,1024]{1,0:T(8,128)S(1)}, u32[]{:S(2)}, u32[]{:S(2)}) collective-permute-start(f32[48,1024]{1,0:T(8,128)S(1)} %collective-permute-done.1.x_ref), channel_id=1, source_target_pairs={{0,1},{1,0},{2,3},{3,2},{4,5},{5,4},{6,7},{7,6},{8,9},{9,8},{10,11... | collective-permute-start | bytes 589832 | tf_op jit(solution)/shard_map/ppermute | solution.py:246
  11.7 0.3 rows.4
  12.0 4.9 %collective-permute-done.3.x_ref.rest_0_ = f32[48,1024]{1,0:T(8,128)S(1)} collective-permute-done((f32[48,1024]{1,0:T(8,128)S(1)}, f32[48,1024]{1,0:T(8,128)S(1)}, u32[]{:S(2)}, u32[]{:S(2)}) %collective-permute-start.3) | collective-permute-done | bytes 196640 | tf_op jit(solution)/shard_map/ppermute | solution.py:241
  17.0 2.7 %collective-permute-start.4 = (f32[48,1024]{1,0:T(8,128)S(1)}, f32[48,1024]{1,0:T(8,128)S(1)}, u32[]{:S(2)}, u32[]{:S(2)}) collective-permute-start(f32[48,1024]{1,0:T(8,128)S(1)} %pad_select_fusion.x_ref.v_ref), channel_id=1, source_target_pairs={{0,4},{4,8},{8,12},{12,16},{16,20},{20,24},{24,28},{28,32},{32,36}... | collective-permute-start | bytes 589832 | tf_op jit(solution)/shard_map/ppermute | solution.py:241
  19.7 0.3 rows.5
  20.2 9.5 %both.3 = (f32[16,4096]{1,0:T(8,128)S(1)}, f32[16,1024]{1,0:T(8,128)S(1)}) custom-call(bf16[4096,256]{1,0:T(8,128)(2,1)S(1)} %pad_maximum_fusion.at_ref, f32[48,4096]{1,0:T(8,128)S(1)} %pad_maximum_fusion.1.v_ref, bf16[256,1024]{1,0:T(8,128)(2,1)S(1)} %cols.2.b_ref, f32[48,1024]{1,0:T(8,128)S(1)} %collective-permute-done.3.x_ref.rest_0_), custom_call_target="tpu_custom_call" | custom-call | flops 33554432 | bytes 65536 | tf_op jit(solution)/shard_map/both/pallas_call | solution.py:215
  29.8 0.2 cols.3.b_ref
  29.9 4.5 %both.4 = (f32[16,2048]{1,0:T(8,128)S(1)}, f32[16,1024]{1,0:T(8,128)S(1)}) custom-call(bf16[4096,256]{1,0:T(8,128)(2,1)S(1)} %pad_maximum_fusion.at_ref, f32[48,4096]{1,0:T(8,128)S(1)} %pad_maximum_fusion.1.v_ref, bf16[256,1024]{1,0:T(8,128)(2,1)S(1)} %cols.3.b_ref, f32[48,1024]{1,0:T(8,128)S(1)} %collective-permute-done.4.x_ref.rest_0_), custom_call_target="tpu_custom_call" | custom-call | flops 16777216 | bytes 32768 | tf_op jit(solution)/shard_map/both/pallas_call | solution.py:215
  34.5 4.5 %both.5 = (f32[16,2048]{1,0:T(8,128)S(1)}, f32[16,1024]{1,0:T(8,128)S(1)}) custom-call(bf16[4096,256]{1,0:T(8,128)(2,1)S(1)} %pad_maximum_fusion.at_ref, f32[48,4096]{1,0:T(8,128)S(1)} %pad_maximum_fusion.1.v_ref, bf16[256,1024]{1,0:T(8,128)(2,1)S(1)} %cols.3.b_ref, f32[48,1024]{1,0:T(8,128)S(1)} %collective-permute-done.4.x_ref.rest_0_), custom_call_target="tpu_custom_call" | custom-call | flops 16777216 | bytes 32768 | tf_op jit(solution)/shard_map/both/pallas_call | solution.py:215
  39.1 1.2 %collective-permute-start.5 = (f32[16,2048]{1,0:T(8,128)S(1)}, f32[16,2048]{1,0:T(8,128)S(1)}, u32[]{:S(2)}, u32[]{:S(2)}) collective-permute-start(f32[16,2048]{1,0:T(8,128)S(1)} %get-tuple-element.40), channel_id=1, source_target_pairs={{0,1},{1,0},{2,3},{3,2},{4,5},{5,4},{6,7},{7,6},{8,9},{9,8},{10,11... | collective-permute-start | bytes 393224 | tf_op jit(solution)/shard_map/ppermute | solution.py:246
  40.3 1.5 %collective-permute-start.8 = (f32[16,1024]{1,0:T(8,128)S(1)}, f32[16,1024]{1,0:T(8,128)S(1)}, u32[]{:S(2)}, u32[]{:S(2)}) collective-permute-start(f32[16,1024]{1,0:T(8,128)S(1)} %get-tuple-element.30), channel_id=1, source_target_pairs={{0,248},{4,252},{8,0},{12,4},{16,8},{20,12},{24,16},{28,20},{32,24... | collective-permute-start | bytes 196616 | tf_op jit(solution)/shard_map/ppermute | solution.py:241
  41.8 3.4 %collective-permute-start.7 = (f32[16,1024]{1,0:T(8,128)S(1)}, f32[16,1024]{1,0:T(8,128)S(1)}, u32[]{:S(2)}, u32[]{:S(2)}) collective-permute-start(f32[16,1024]{1,0:T(8,128)S(1)} %add.48), channel_id=1, source_target_pairs={{0,252},{4,0},{8,4},{12,8},{16,12},{20,16},{24,20},{28,24},{32,28}... | collective-permute-start | bytes 196616 | tf_op jit(solution)/shard_map/ppermute | solution.py:241
  45.2 0.6 %collective-permute-start.6 = (f32[16,1024]{1,0:T(8,128)S(1)}, f32[16,1024]{1,0:T(8,128)S(1)}, u32[]{:S(2)}, u32[]{:S(2)}) collective-permute-start(f32[16,1024]{1,0:T(8,128)S(1)} %slice_add_fusion.4), channel_id=1, source_target_pairs={{0,2},{1,3},{2,0},{3,1},{4,6},{5,7},{6,4},{7,5},{8,10},{9,11},{10,... | collective-permute-start | bytes 196616 | tf_op jit(solution)/shard_map/ppermute | solution.py:246
  45.8 3.8 %own.5 = f32[16,1024]{1,0:T(8,128)S(1)} custom-call(bf16[4096,256]{1,0:T(8,128)(2,1)S(1)} %pad_maximum_fusion.at_ref, f32[48,4096]{1,0:T(8,128)S(1)} %pad_maximum_fusion.1.v_ref, bf16[256,1024]{1,0:T(8,128)(2,1)S(1)} %get-tuple-element.23.b_ref), custom_call_target="tpu_custom_call" | custom-call | flops 16777216 | bytes 32768 | tf_op jit(solution)/shard_map/own/pallas_call | solution.py:215
  49.7 0.9 %collective-permute-done.6 = f32[16,1024]{1,0:T(8,128)S(1)} collective-permute-done((f32[16,1024]{1,0:T(8,128)S(1)}, f32[16,1024]{1,0:T(8,128)S(1)}, u32[]{:S(2)}, u32[]{:S(2)}) %collective-permute-start.6) | collective-permute-done | bytes 65568 | tf_op jit(solution)/shard_map/ppermute | solution.py:246
  50.5 0.7 %fusion.3 = f32[16,1024]{1,0:T(8,128)} fusion(f32[16,1024]{1,0:T(8,128)S(1)} %collective-permute-done.8, f32[16,1024]{1,0:T(8,128)S(1)} %collective-permute-done.7, f32[16,1024]{1,0:T(8,128)S(1)} %collective-permute-done.6, f32[16,2048]{1,0:T(8,128)S(1)} %collective-permute-done.5, f32[16,2048]{1,0:T(8,128)S(1)} %get-tuple-element.39, ...), kind=kLoop, calls=%fused_computation.9 | loop fusion | flops 131072 | bytes 593920 | tf_op jit(solution)/shard_map/add | solution.py:287
  (21 shorter events, 0.5 us)
Async XLA Ops:
  1.0 7.5 %collective-permute-start = (f32[48,1024]{1,0:T(8,128)S(1)}, f32[48,1024]{1,0:T(8,128)S(1)}, u32[]{:S(2)}, u32[]{:S(2)}) collective-permute-start(f32[48,1024]{1,0:T(8,128)S(1)} %pad_select_fusion.x_ref.v_ref), channel_id=1, source_target_pairs={{0,1},{1,0},{2,3},{3,2},{4,5},{5,4},{6,7},{7,6},{8,9},{9,8},{10,11... | collective-permute-start | bytes 589832 | tf_op jit(solution)/shard_map/ppermute | solution.py:246
  4.4 6.5 %collective-permute-start.1 = (f32[48,1024]{1,0:T(8,128)S(1)}, f32[48,1024]{1,0:T(8,128)S(1)}, u32[]{:S(2)}, u32[]{:S(2)}) collective-permute-start(f32[48,1024]{1,0:T(8,128)S(1)} %pad_select_fusion.x_ref.v_ref), channel_id=1, source_target_pairs={{0,2},{1,3},{2,0},{3,1},{4,6},{5,7},{6,4},{7,5},{8,10},{9,11},{10,... | collective-permute-start | bytes 589832 | tf_op jit(solution)/shard_map/ppermute | solution.py:246
  4.4 12.5 %collective-permute-start.3 = (f32[48,1024]{1,0:T(8,128)S(1)}, f32[48,1024]{1,0:T(8,128)S(1)}, u32[]{:S(2)}, u32[]{:S(2)}) collective-permute-start(f32[48,1024]{1,0:T(8,128)S(1)} %pad_select_fusion.x_ref.v_ref), channel_id=1, source_target_pairs={{0,8},{4,12},{8,16},{12,20},{16,24},{20,28},{24,32},{28,36},{32,40... | collective-permute-start | bytes 589832 | tf_op jit(solution)/shard_map/ppermute | solution.py:241
  5.5 0.7 %copy-start = (f32[32]{0:T(128)S(1)}, f32[32]{0:T(128)}, u32[]{:S(2)}) copy-start(f32[32]{0:T(128)} %param.6) | copy-start | bytes 388
  10.9 8.9 %collective-permute-start.2 = (f32[48,1024]{1,0:T(8,128)S(1)}, f32[48,1024]{1,0:T(8,128)S(1)}, u32[]{:S(2)}, u32[]{:S(2)}) collective-permute-start(f32[48,1024]{1,0:T(8,128)S(1)} %collective-permute-done.1.x_ref), channel_id=1, source_target_pairs={{0,1},{1,0},{2,3},{3,2},{4,5},{5,4},{6,7},{7,6},{8,9},{9,8},{10,11... | collective-permute-start | bytes 589832 | tf_op jit(solution)/shard_map/ppermute | solution.py:246
  17.0 12.7 %collective-permute-start.4 = (f32[48,1024]{1,0:T(8,128)S(1)}, f32[48,1024]{1,0:T(8,128)S(1)}, u32[]{:S(2)}, u32[]{:S(2)}) collective-permute-start(f32[48,1024]{1,0:T(8,128)S(1)} %pad_select_fusion.x_ref.v_ref), channel_id=1, source_target_pairs={{0,4},{4,8},{8,12},{12,16},{16,20},{20,24},{24,28},{28,32},{32,36}... | collective-permute-start | bytes 589832 | tf_op jit(solution)/shard_map/ppermute | solution.py:241
  39.1 11.4 %copy-start.1 = (f32[16,1024]{1,0:T(8,128)S(1)}, f32[16,1024]{1,0:T(8,128)}, u32[]{:S(2)}) copy-start(f32[16,1024]{1,0:T(8,128)} %param.5) | copy-start | bytes 196612
  39.1 11.4 %copy-start.2 = (f32[1024]{0:T(1024)S(1)}, f32[1024]{0:T(1024)}, u32[]{:S(2)}) copy-start(f32[1024]{0:T(1024)} %param.7) | copy-start | bytes 12292
  39.1 6.1 %collective-permute-start.5 = (f32[16,2048]{1,0:T(8,128)S(1)}, f32[16,2048]{1,0:T(8,128)S(1)}, u32[]{:S(2)}, u32[]{:S(2)}) collective-permute-start(f32[16,2048]{1,0:T(8,128)S(1)} %get-tuple-element.40), channel_id=1, source_target_pairs={{0,1},{1,0},{2,3},{3,2},{4,5},{5,4},{6,7},{7,6},{8,9},{9,8},{10,11... | collective-permute-start | bytes 393224 | tf_op jit(solution)/shard_map/ppermute | solution.py:246
  40.3 9.3 %collective-permute-start.8 = (f32[16,1024]{1,0:T(8,128)S(1)}, f32[16,1024]{1,0:T(8,128)S(1)}, u32[]{:S(2)}, u32[]{:S(2)}) collective-permute-start(f32[16,1024]{1,0:T(8,128)S(1)} %get-tuple-element.30), channel_id=1, source_target_pairs={{0,248},{4,252},{8,0},{12,4},{16,8},{20,12},{24,16},{28,20},{32,24... | collective-permute-start | bytes 196616 | tf_op jit(solution)/shard_map/ppermute | solution.py:241
  41.8 7.8 %collective-permute-start.7 = (f32[16,1024]{1,0:T(8,128)S(1)}, f32[16,1024]{1,0:T(8,128)S(1)}, u32[]{:S(2)}, u32[]{:S(2)}) collective-permute-start(f32[16,1024]{1,0:T(8,128)S(1)} %add.48), channel_id=1, source_target_pairs={{0,252},{4,0},{8,4},{12,8},{16,12},{20,16},{24,20},{28,24},{32,28}... | collective-permute-start | bytes 196616 | tf_op jit(solution)/shard_map/ppermute | solution.py:241
  45.2 5.3 %collective-permute-start.6 = (f32[16,1024]{1,0:T(8,128)S(1)}, f32[16,1024]{1,0:T(8,128)S(1)}, u32[]{:S(2)}, u32[]{:S(2)}) collective-permute-start(f32[16,1024]{1,0:T(8,128)S(1)} %slice_add_fusion.4), channel_id=1, source_target_pairs={{0,2},{1,3},{2,0},{3,1},{4,6},{5,7},{6,4},{7,5},{8,10},{9,11},{10,... | collective-permute-start | bytes 196616 | tf_op jit(solution)/shard_map/ppermute | solution.py:246

commit v5 on v4

--- a/solution.py
+++ b/solution.py
@@ -20,7 +20,6 @@
 DEPTH = 256
 TILE = 256
 GROUP = 2
-STEP_TILES = 32
 BF16 = jnp.bfloat16
 F32 = jnp.float32
 F8 = jnp.float8_e4m3fn
@@ -108,14 +107,15 @@
     b_ref[...] = features(scaled(x_ref, inv_ref[:, :1]), False)
 
 
-def tile_kernel(both, low, start, count, at_ref, v_ref, b_ref, *rest):
+def tile_kernel(both, low, count, *refs):
+    ats, vs, b_ref, rest = refs[:count], refs[count : 2 * count], refs[2 * count], refs[2 * count + 1 :]
     if both:
         x_ref, fwd_ref, bwd_ref, vc_ref, vc_low_ref, facc_ref = rest[:6]
     else:
         bwd_ref = rest[0]
-    vr_ref, vr_low_ref, acc_ref, even_ref, odd_ref, hi_ref, lo_ref, slot_ref = rest[6 if both else 1 :]
-    across, groups = b_ref.shape[1] // TILE, count // (TILE * GROUP)
-    down = min(STEP_TILES // (GROUP * across), groups)
+    vr_ref, vr_low_ref, acc_ref, even_ref, odd_ref, slot_ref = rest[6 if both else 1 :]
+    part = ats[0].shape[0]
+    across, per_part = b_ref.shape[1] // TILE, part // (TILE * GROUP)
     slot_ref[0] = 0
     slot = slot_ref[0]
     if both:
@@ -123,45 +123,35 @@
         vc_ref[...] = halves(vc, BF16)
         vc_low_ref[...] = halves(vc, low)
         facc_ref[...] = jnp.zeros_like(facc_ref)
-    vr, undo_r = leveled(v_ref[DIMS:, start : start + count], low)
+    vr, undo_r = leveled(jnp.concatenate([v[DIMS:, :] for v in vs], axis=1), low)
     vr_ref[...] = halves(vr, BF16)
     vr_low_ref[...] = halves(vr, low)
     acc_ref[...] = jnp.zeros_like(acc_ref)
 
-    def distances(ref, i, j):
-        rows = pl.ds(pl.multiple_of(start + i * TILE * GROUP, TILE * GROUP), TILE * GROUP)
-        d2 = dot(at_ref[rows, :], b_ref[:, j * TILE : (j + 1) * TILE], 1, 0)
-        ref[0] = jnp.maximum(d2, 1e-30)
+    def distances(ref, group, j):
+        first = group % per_part * TILE * GROUP
+        rows = ats[group // per_part][first : first + TILE * GROUP, :]
+        ref[0] = jnp.maximum(dot(rows, b_ref[:, j * TILE : (j + 1) * TILE], 1, 0), 1e-30)
 
     def products(hi, lo, i, j):
-        cols = slice(j * TILE, (j + 1) * TILE)
-        rows = pl.ds(pl.multiple_of(i * TILE, TILE), TILE)
+        rows, cols = slice(i * TILE, (i + 1) * TILE), slice(j * TILE, (j + 1) * TILE)
         acc_ref[:, cols] += dot(vr_ref[:, rows], hi, 1, 0) + dot(vr_low_ref[:, rows], lo, 1, 0)
         if both:
             facc_ref[:, rows] += dot(vc_ref[:, cols], hi, 1, 1) + dot(vc_low_ref[:, cols], lo, 1, 1)
 
-    hi_ref[...] = jnp.zeros_like(hi_ref)
-    lo_ref[...] = jnp.zeros_like(lo_ref)
+    behind = None
+    groups = [(i, j) for i in range(count * per_part) for j in range(across)]
     distances(even_ref, 0, 0)
-
-    def step(k, carry):
-        hi, lo = hi_ref[...], lo_ref[...]
-        i, j = jnp.maximum(k * down * GROUP - 1, 0), across - 1
-        for t in range(down * across):
-            now, later = (even_ref, odd_ref) if t % 2 == 0 else (odd_ref, even_ref)
-            ahead = k * down + (t + 1) // across
-            if t == down * across - 1:
-                ahead = jnp.where(ahead < groups, ahead, 0)
-            distances(later, ahead, (t + 1) % across)
-            for g in range(GROUP):
-                products(hi, lo, i, j)
-                hi, lo = kernel_tile(now[slot, g * TILE : (g + 1) * TILE, :], low)
-                i, j = (k * down + t // across) * GROUP + g, t % across
-        hi_ref[...], lo_ref[...] = hi, lo
-        return carry
-
-    lax.fori_loop(0, groups // down, step, 0)
-    products(hi_ref[...], lo_ref[...], groups * GROUP - 1, across - 1)
+    for t, (i, j) in enumerate(groups):
+        now, later = (even_ref, odd_ref) if t % 2 == 0 else (odd_ref, even_ref)
+        if t + 1 < len(groups):
+            distances(later, *groups[t + 1])
+        for g in range(GROUP):
+            if behind is not None:
+                products(*behind)
+            hi, lo = kernel_tile(now[slot, g * TILE : (g + 1) * TILE, :], low)
+            behind = hi, lo, i * GROUP + g, j
+    products(*behind)
     bwd_ref[...] = fold(acc_ref[...], undo_r)
     if both:
         fwd_ref[...] = fold(facc_ref[...], undo_c)
@@ -201,8 +191,8 @@
     )(x, inv)
 
 
-def tiles(at, v, b, x=None, start=0, n=None):
-    n, width = n or at.shape[0], b.shape[1]
+def tiles(ats, vs, b, x=None):
+    n, width = len(ats) * ats[0].shape[0], b.shape[1]
     both = x is not None
     low = F8 if both else BF16
     bwd = jax.ShapeDtypeStruct((RHS, width), F32)
@@ -213,9 +203,9 @@
         pltpu.VMEM((2 * RHS, n), F32),
     ]
     return pl.pallas_call(
-        functools.partial(tile_kernel, both, low, start, n),
+        functools.partial(tile_kernel, both, low, len(ats)),
         out_shape=(fwd, bwd) if both else bwd,
-        in_specs=[VMEM] * (4 if both else 3),
+        in_specs=[VMEM] * (2 * len(ats) + (2 if both else 1)),
         out_specs=(VMEM, VMEM) if both else VMEM,
         scratch_shapes=(more if both else [])
         + [
@@ -224,8 +214,6 @@
             pltpu.VMEM((2 * RHS, width), F32),
             pltpu.VMEM((1, TILE * GROUP, TILE), F32),
             pltpu.VMEM((1, TILE * GROUP, TILE), F32),
-            pltpu.VMEM((TILE, TILE), BF16),
-            pltpu.VMEM((TILE, TILE), low),
             pltpu.SMEM((1,), jnp.int32),
         ],
         compiler_params=PARAMS,
@@ -233,7 +221,7 @@
             flops=n * width * 8, bytes_accessed=n * 16, transcendentals=0
         ),
         name="both" if both else "own",
-    )(at, v, b, *([x] if both else []))
+    )(*ats, *vs, b, *([x] if both else []))
 
 
 def shifted(value, steps):
@@ -258,10 +246,10 @@
     far = swapped(own, 2)
     two = shifted(own, 2)
     at0, b0, inv = first(own, inv_length.reshape(1, DIMS))
-    total = tiles(at0, own, b0)
+    total = tiles([at0], [own], b0)
     near = after(near, total)
     at_near = prep(near, inv, True)
-    total = total + tiles(at_near, near, b0)
+    total = total + tiles([at_near], [near], b0)
     far = after(far, total)
     cross = swapped(far, 1)
     one = shifted(after(own, far), 1)
@@ -269,20 +257,18 @@
     b2 = prep(after(two, total), inv, False)
     cross = after(cross, b2)
     at_cross = prep(cross, inv, True)
-    block = jnp.concatenate([own, far, cross, near], axis=1)
-    at = jnp.concatenate([at0, at_far, at_cross, at_near], axis=0)
-    fwd2, ret2 = tiles(at, block, b2, two)
+    fwd2, ret2 = tiles([at0, at_far, at_cross, at_near], [own, far, cross, near], b2, two)
     back2 = shifted(ret2, -2)
     one = after(one, ret2)
     b1 = prep(one, inv, False)
-    fwd_other, ret_other = tiles(at, block, b1, one, 2 * width, 2 * width)
+    fwd_other, ret_other = tiles([at_cross, at_near], [cross, near], b1, one)
     give_near = swapped(fwd_other + fwd2[:, 2 * width :], 1)
-    fwd_pair, ret_pair = tiles(at, after(block, ret_other), b1, one, 0, 2 * width)
+    fwd_pair, ret_pair = tiles([at0, after(at_far, ret_other)], [own, far], b1, one)
     back1 = shifted(ret_other + ret_pair, -1)
     rows = fwd_pair + fwd2[:, : 2 * width]
     rows_far = rows[:, width:] + give_near[:, :width]
     give_far = swapped(rows_far, 2)
-    total = total + tiles(at, after(block, rows_far), b0, None, width, 2 * width)
+    total = total + tiles([at_far, after(at_cross, rows_far)], [far, cross], b0)
     total = total + rows[:, :width] + give_near[:, width:]
     return total + give_far + back1 + back2 + noise[None, :] * vectors
 

time: 51.3 us -> 47.3 us (0.922)
  waiting for transfers between devices: 5.78 us -> 4.25 us
  Pallas kernels: 27.9 us -> 26.9 us
  local copies, waits for them, and re-layouts: 0.67 us -> 0.02 us
  starting transfers between devices: 14.7 us -> 14.1 us
    ppermute x4, waiting for transfers between devices: 4.91 us -> 3.42 us  [shifted(): lax.ppermute(value, 'blk', [(s, (s + steps) % count) for s in range(count)])]
    ppermute x4, starting transfers between devices: 8.68 us -> 7.4 us  [shifted(): lax.ppermute(value, 'blk', [(s, (s + steps) % count) for s in range(count)])]
    pallas_call x6, Pallas kernels: 26.5 us -> 25.4 us  [tiles(): pl.pallas_call(functools.partial(tile_kernel, both, low, len(ats)), out_s...]
    ppermute x5, starting transfers between devices: 6.01 us -> 6.71 us  [swapped(): return lax.ppermute(value, 'split', [(s, s ^ mask) for s in range(count)])]
    unnamed x6, local copies, waits for them, and re-layouts: 0.67 us -> 0.02 us
where the time goes in v5:
time: 47.3 us; the launch traced here: 47.2 us
  Pallas kernels  26.9 us (57%)
  starting transfers between devices  14.1 us (30%)
  waiting for transfers between devices  4.25 us (9%)
  other arithmetic  1.77 us (4%)
    pallas_call x6, Pallas kernels, tiles(): pl.pallas_call(functools.partial(tile_kernel, both, low, len(ats)), out_s...  25.4 us
    ppermute x4, starting transfers between devices, shifted(): lax.ppermute(value, 'blk', [(s, (s + steps) % count) for s in range(count)])  7.4 us
    ppermute x5, starting transfers between devices, swapped(): return lax.ppermute(value, 'split', [(s, s ^ mask) for s in range(count)])  6.71 us
    ppermute x4, waiting for transfers between devices, shifted(): lax.ppermute(value, 'blk', [(s, (s + steps) % count) for s in range(count)])  3.42 us
    pallas_call x5, Pallas kernels, prep(): pl.pallas_call(rows_kernel if rows else cols_kernel, out_shape=jax.ShapeD...  1.15 us
    select_n x1, other arithmetic, body(): jnp.where(row < DIMS, jnp.pad(points, ((0, RHS), (0, 0))), jnp.pad(vector...  1.03 us
  transfers between devices with their start and end apart: 9, of which 2 were waited for; matrix products, arithmetic and copies ran while one was open for 0% of the time, Pallas kernels for 37%

profile of v5, /device:TPU:1, one launch (start us, length us, event | category | flops | bytes accessed | tf_op | source)
XLA Modules:
  0.0 47.2 jit_solution(11006902187462762025)
XLA Ops:
  0.0 1.0 %pad_select_fusion.x_ref.refs_1_.refs_4_.refs_2_ = f32[48,1024]{1,0:T(8,128)S(1)} fusion(f32[16,1024]{1,0:T(8,128)} %param.5, f32[32,1024]{1,0:T(8,128)} %param.4, pred[48]{0:T(512)(128)(4,1)S(1)} %iota_compare_fusion), kind=kLoop, calls=%fused_computation | loop fusion | flops 49152 | bytes 393264 | tf_op jit(solution)/shard_map/jit(_where)/select_n | solution.py:243
  1.0 3.3 %collective-permute-start = (f32[48,1024]{1,0:T(8,128)S(1)}, f32[48,1024]{1,0:T(8,128)S(1)}, u32[]{:S(2)}, u32[]{:S(2)}) collective-permute-start(f32[48,1024]{1,0:T(8,128)S(1)} %pad_select_fusion.x_ref.refs_1_.refs_4_.refs_2_), channel_id=1, source_target_pairs={{0,1},{1,0},{2,3},{3,2},{4,5},{5,4},{6,7},{7,6},{8,9},{9,8},{10,11... | collective-permute-start | bytes 589832 | tf_op jit(solution)/shard_map/ppermute | solution.py:234
  4.4 1.1 %collective-permute-start.3 = (f32[48,1024]{1,0:T(8,128)S(1)}, f32[48,1024]{1,0:T(8,128)S(1)}, u32[]{:S(2)}, u32[]{:S(2)}) collective-permute-start(f32[48,1024]{1,0:T(8,128)S(1)} %pad_select_fusion.x_ref.refs_1_.refs_4_.refs_2_), channel_id=1, source_target_pairs={{0,8},{4,12},{8,16},{12,20},{16,24},{20,28},{24,32},{28,36},{32,40... | collective-permute-start | bytes 589832 | tf_op jit(solution)/shard_map/ppermute | solution.py:229
  5.5 0.3 first.1
  5.8 1.9 %own.3 = f32[16,1024]{1,0:T(8,128)S(1)} custom-call(bf16[1024,256]{1,0:T(8,128)(2,1)S(1)} %get-tuple-element.22.refs_0_, f32[48,1024]{1,0:T(8,128)S(1)} %pad_select_fusion.x_ref.refs_1_.refs_4_.refs_2_, bf16[256,1024]{1,0:T(8,128)(2,1)S(1)} %get-tuple-element.23.refs_2_.refs_4_), custom_call_target="tpu_custom_call" | custom-call | flops 8388608 | bytes 16384 | tf_op jit(solution)/shard_map/own/pallas_call | solution.py:205
  7.8 0.3 rows.3.refs_0_.refs_3_.refs_1_
  8.1 1.9 %own.4 = f32[16,1024]{1,0:T(8,128)S(1)} custom-call(bf16[1024,256]{1,0:T(8,128)(2,1)S(1)} %rows.3.refs_0_.refs_3_.refs_1_, f32[48,1024]{1,0:T(8,128)S(1)} %collective-permute-done.x_ref.refs_1_.refs_7_.refs_3_, bf16[256,1024]{1,0:T(8,128)(2,1)S(1)} %get-tuple-element.23.refs_2_.refs_4_), custom_call_target="tpu_custom_call" | custom-call | flops 8388608 | bytes 16384 | tf_op jit(solution)/shard_map/own/pallas_call | solution.py:205
  10.0 0.8 %collective-permute-done.1.x_ref.refs_5_.refs_3_.refs_2_ = f32[48,1024]{1,0:T(8,128)S(1)} collective-permute-done((f32[48,1024]{1,0:T(8,128)S(1)}, f32[48,1024]{1,0:T(8,128)S(1)}, u32[]{:S(2)}, u32[]{:S(2)}) %collective-permute-start.1) | collective-permute-done | bytes 196640 | tf_op jit(solution)/shard_map/ppermute | solution.py:234
  10.8 0.9 %collective-permute-start.2 = (f32[48,1024]{1,0:T(8,128)S(1)}, f32[48,1024]{1,0:T(8,128)S(1)}, u32[]{:S(2)}, u32[]{:S(2)}) collective-permute-start(f32[48,1024]{1,0:T(8,128)S(1)} %collective-permute-done.1.x_ref.refs_5_.refs_3_.refs_2_), channel_id=1, source_target_pairs={{0,1},{1,0},{2,3},{3,2},{4,5},{5,4},{6,7},{7,6},{8,9},{9,8},{10,11... | collective-permute-start | bytes 589832 | tf_op jit(solution)/shard_map/ppermute | solution.py:234
  11.7 1.5 %collective-permute-start.4 = (f32[48,1024]{1,0:T(8,128)S(1)}, f32[48,1024]{1,0:T(8,128)S(1)}, u32[]{:S(2)}, u32[]{:S(2)}) collective-permute-start(f32[48,1024]{1,0:T(8,128)S(1)} %pad_select_fusion.x_ref.refs_1_.refs_4_.refs_2_), channel_id=1, source_target_pairs={{0,4},{4,8},{8,12},{12,16},{16,20},{20,24},{24,28},{28,32},{32,36}... | collective-permute-start | bytes 589832 | tf_op jit(solution)/shard_map/ppermute | solution.py:229
  13.2 0.3 rows.4.refs_1_.refs_0_
  13.5 3.4 %collective-permute-done.3.x_ref.refs_9_ = f32[48,1024]{1,0:T(8,128)S(1)} collective-permute-done((f32[48,1024]{1,0:T(8,128)S(1)}, f32[48,1024]{1,0:T(8,128)S(1)}, u32[]{:S(2)}, u32[]{:S(2)}) %collective-permute-start.3) | collective-permute-done | bytes 196640 | tf_op jit(solution)/shard_map/ppermute | solution.py:229
  16.9 0.2 cols.2.refs_8_
  17.1 0.3 rows.5.refs_2_.refs_0_.refs_1_
  17.3 8.6 %both.3 = (f32[16,4096]{1,0:T(8,128)S(1)}, f32[16,1024]{1,0:T(8,128)S(1)}) custom-call(bf16[1024,256]{1,0:T(8,128)(2,1)S(1)} %get-tuple-element.22.refs_0_, bf16[1024,256]{1,0:T(8,128)(2,1)S(1)} %rows.4.refs_1_.refs_0_, bf16[1024,256]{1,0:T(8,128)(2,1)S(1)} %rows.5.refs_2_.refs_0_.refs_1_, bf16[1024,256]{1,0:T(8,128)(2,1)S(1)} %rows.3.refs_0_.refs_3_.refs_1_, ...), custom_call_target="tpu_custom_call" | custom-call | flops 33554432 | bytes 65536 | tf_op jit(solution)/shard_map/both/pallas_call | solution.py:205
  26.0 0.2 cols.3.refs_4_
  26.2 4.8 %both.4 = (f32[16,2048]{1,0:T(8,128)S(1)}, f32[16,1024]{1,0:T(8,128)S(1)}) custom-call(bf16[1024,256]{1,0:T(8,128)(2,1)S(1)} %rows.5.refs_2_.refs_0_.refs_1_, bf16[1024,256]{1,0:T(8,128)(2,1)S(1)} %rows.3.refs_0_.refs_3_.refs_1_, f32[48,1024]{1,0:T(8,128)S(1)} %collective-permute-done.2.x_ref.refs_6_.refs_2_.refs_3_, ...), custom_call_target="tpu_custom_call" | custom-call | flops 16777216 | bytes 32768 | tf_op jit(solution)/shard_map/both/pallas_call | solution.py:205
  30.9 4.6 %both.5 = (f32[16,2048]{1,0:T(8,128)S(1)}, f32[16,1024]{1,0:T(8,128)S(1)}) custom-call(bf16[1024,256]{1,0:T(8,128)(2,1)S(1)} %get-tuple-element.22.refs_0_, bf16[1024,256]{1,0:T(8,128)(2,1)S(1)} %rows.4.refs_1_.refs_0_, f32[48,1024]{1,0:T(8,128)S(1)} %pad_select_fusion.x_ref.refs_1_.refs_4_.refs_2_, ...), custom_call_target="tpu_custom_call" | custom-call | flops 16777216 | bytes 32768 | tf_op jit(solution)/shard_map/both/pallas_call | solution.py:205
  35.5 1.0 %collective-permute-start.5 = (f32[16,2048]{1,0:T(8,128)S(1)}, f32[16,2048]{1,0:T(8,128)S(1)}, u32[]{:S(2)}, u32[]{:S(2)}) collective-permute-start(f32[16,2048]{1,0:T(8,128)S(1)} %get-tuple-element.40), channel_id=1, source_target_pairs={{0,1},{1,0},{2,3},{3,2},{4,5},{5,4},{6,7},{7,6},{8,9},{9,8},{10,11... | collective-permute-start | bytes 393224 | tf_op jit(solution)/shard_map/ppermute | solution.py:234
  36.5 3.6 %collective-permute-start.8 = (f32[16,1024]{1,0:T(8,128)S(1)}, f32[16,1024]{1,0:T(8,128)S(1)}, u32[]{:S(2)}, u32[]{:S(2)}) collective-permute-start(f32[16,1024]{1,0:T(8,128)S(1)} %get-tuple-element.30), channel_id=1, source_target_pairs={{0,248},{4,252},{8,0},{12,4},{16,8},{20,12},{24,16},{28,20},{32,24... | collective-permute-start | bytes 196616 | tf_op jit(solution)/shard_map/ppermute | solution.py:229
  40.1 1.2 %collective-permute-start.7 = (f32[16,1024]{1,0:T(8,128)S(1)}, f32[16,1024]{1,0:T(8,128)S(1)}, u32[]{:S(2)}, u32[]{:S(2)}) collective-permute-start(f32[16,1024]{1,0:T(8,128)S(1)} %add.48), channel_id=1, source_target_pairs={{0,252},{4,0},{8,4},{12,8},{16,12},{20,16},{24,20},{28,24},{32,28}... | collective-permute-start | bytes 196616 | tf_op jit(solution)/shard_map/ppermute | solution.py:229
  41.3 1.5 %collective-permute-start.6 = (f32[16,1024]{1,0:T(8,128)S(1)}, f32[16,1024]{1,0:T(8,128)S(1)}, u32[]{:S(2)}, u32[]{:S(2)}) collective-permute-start(f32[16,1024]{1,0:T(8,128)S(1)} %slice_add_fusion.4), channel_id=1, source_target_pairs={{0,2},{1,3},{2,0},{3,1},{4,6},{5,7},{6,4},{7,5},{8,10},{9,11},{10,... | collective-permute-start | bytes 196616 | tf_op jit(solution)/shard_map/ppermute | solution.py:234
  42.9 3.6 %own.5 = f32[16,1024]{1,0:T(8,128)S(1)} custom-call(bf16[1024,256]{1,0:T(8,128)(2,1)S(1)} %rows.4.refs_1_.refs_0_, bf16[1024,256]{1,0:T(8,128)(2,1)S(1)} %rows.5.refs_2_.refs_0_.refs_1_, f32[48,1024]{1,0:T(8,128)S(1)} %collective-permute-done.1.x_ref.refs_5_.refs_3_.refs_2_, f32[48,1024]{1,0:T(8,128)S(1)} %collective-permute-done.2.x_ref.refs_6_.refs_2_.refs_3_, ...), custom_call_target="tpu_custom_call" | custom-call | flops 16777216 | bytes 32768 | tf_op jit(solution)/shard_map/own/pallas_call | solution.py:205
  46.5 0.7 %fusion.3 = f32[16,1024]{1,0:T(8,128)} fusion(f32[16,1024]{1,0:T(8,128)S(1)} %collective-permute-done.8, f32[16,1024]{1,0:T(8,128)S(1)} %collective-permute-done.7, f32[16,1024]{1,0:T(8,128)S(1)} %collective-permute-done.6, f32[16,2048]{1,0:T(8,128)S(1)} %collective-permute-done.5, f32[16,2048]{1,0:T(8,128)S(1)} %get-tuple-element.39, ...), kind=kLoop, calls=%fused_computation.7 | loop fusion | flops 131072 | bytes 593920 | tf_op jit(solution)/shard_map/add | solution.py:273
  (19 shorter events, 0.1 us)
Async XLA Ops:
  1.0 4.5 %copy-start = (f32[32]{0:T(128)S(1)}, f32[32]{0:T(128)}, u32[]{:S(2)}) copy-start(f32[32]{0:T(128)} %param.6) | copy-start | bytes 388
  1.0 6.7 %collective-permute-start = (f32[48,1024]{1,0:T(8,128)S(1)}, f32[48,1024]{1,0:T(8,128)S(1)}, u32[]{:S(2)}, u32[]{:S(2)}) collective-permute-start(f32[48,1024]{1,0:T(8,128)S(1)} %pad_select_fusion.x_ref.refs_1_.refs_4_.refs_2_), channel_id=1, source_target_pairs={{0,1},{1,0},{2,3},{3,2},{4,5},{5,4},{6,7},{7,6},{8,9},{9,8},{10,11... | collective-permute-start | bytes 589832 | tf_op jit(solution)/shard_map/ppermute | solution.py:234
  4.4 6.5 %collective-permute-start.1 = (f32[48,1024]{1,0:T(8,128)S(1)}, f32[48,1024]{1,0:T(8,128)S(1)}, u32[]{:S(2)}, u32[]{:S(2)}) collective-permute-start(f32[48,1024]{1,0:T(8,128)S(1)} %pad_select_fusion.x_ref.refs_1_.refs_4_.refs_2_), channel_id=1, source_target_pairs={{0,2},{1,3},{2,0},{3,1},{4,6},{5,7},{6,4},{7,5},{8,10},{9,11},{10,... | collective-permute-start | bytes 589832 | tf_op jit(solution)/shard_map/ppermute | solution.py:234
  4.4 12.5 %collective-permute-start.3 = (f32[48,1024]{1,0:T(8,128)S(1)}, f32[48,1024]{1,0:T(8,128)S(1)}, u32[]{:S(2)}, u32[]{:S(2)}) collective-permute-start(f32[48,1024]{1,0:T(8,128)S(1)} %pad_select_fusion.x_ref.refs_1_.refs_4_.refs_2_), channel_id=1, source_target_pairs={{0,8},{4,12},{8,16},{12,20},{16,24},{20,28},{24,32},{28,36},{32,40... | collective-permute-start | bytes 589832 | tf_op jit(solution)/shard_map/ppermute | solution.py:229
  10.8 6.2 %collective-permute-start.2 = (f32[48,1024]{1,0:T(8,128)S(1)}, f32[48,1024]{1,0:T(8,128)S(1)}, u32[]{:S(2)}, u32[]{:S(2)}) collective-permute-start(f32[48,1024]{1,0:T(8,128)S(1)} %collective-permute-done.1.x_ref.refs_5_.refs_3_.refs_2_), channel_id=1, source_target_pairs={{0,1},{1,0},{2,3},{3,2},{4,5},{5,4},{6,7},{7,6},{8,9},{9,8},{10,11... | collective-permute-start | bytes 589832 | tf_op jit(solution)/shard_map/ppermute | solution.py:234
  11.7 14.3 %collective-permute-start.4 = (f32[48,1024]{1,0:T(8,128)S(1)}, f32[48,1024]{1,0:T(8,128)S(1)}, u32[]{:S(2)}, u32[]{:S(2)}) collective-permute-start(f32[48,1024]{1,0:T(8,128)S(1)} %pad_select_fusion.x_ref.refs_1_.refs_4_.refs_2_), channel_id=1, source_target_pairs={{0,4},{4,8},{8,12},{12,16},{16,20},{20,24},{24,28},{28,32},{32,36}... | collective-permute-start | bytes 589832 | tf_op jit(solution)/shard_map/ppermute | solution.py:229
  35.5 5.8 %collective-permute-start.5 = (f32[16,2048]{1,0:T(8,128)S(1)}, f32[16,2048]{1,0:T(8,128)S(1)}, u32[]{:S(2)}, u32[]{:S(2)}) collective-permute-start(f32[16,2048]{1,0:T(8,128)S(1)} %get-tuple-element.40), channel_id=1, source_target_pairs={{0,1},{1,0},{2,3},{3,2},{4,5},{5,4},{6,7},{7,6},{8,9},{9,8},{10,11... | collective-permute-start | bytes 393224 | tf_op jit(solution)/shard_map/ppermute | solution.py:234
  36.5 10.0 %collective-permute-start.8 = (f32[16,1024]{1,0:T(8,128)S(1)}, f32[16,1024]{1,0:T(8,128)S(1)}, u32[]{:S(2)}, u32[]{:S(2)}) collective-permute-start(f32[16,1024]{1,0:T(8,128)S(1)} %get-tuple-element.30), channel_id=1, source_target_pairs={{0,248},{4,252},{8,0},{12,4},{16,8},{20,12},{24,16},{28,20},{32,24... | collective-permute-start | bytes 196616 | tf_op jit(solution)/shard_map/ppermute | solution.py:229
  40.1 6.4 %collective-permute-start.7 = (f32[16,1024]{1,0:T(8,128)S(1)}, f32[16,1024]{1,0:T(8,128)S(1)}, u32[]{:S(2)}, u32[]{:S(2)}) collective-permute-start(f32[16,1024]{1,0:T(8,128)S(1)} %add.48), channel_id=1, source_target_pairs={{0,252},{4,0},{8,4},{12,8},{16,12},{20,16},{24,20},{28,24},{32,28}... | collective-permute-start | bytes 196616 | tf_op jit(solution)/shard_map/ppermute | solution.py:229
  41.3 5.2 %copy-start.1 = (f32[16,1024]{1,0:T(8,128)S(1)}, f32[16,1024]{1,0:T(8,128)}, u32[]{:S(2)}) copy-start(f32[16,1024]{1,0:T(8,128)} %param.5) | copy-start | bytes 196612
  41.3 5.2 %copy-start.2 = (f32[1024]{0:T(1024)S(1)}, f32[1024]{0:T(1024)}, u32[]{:S(2)}) copy-start(f32[1024]{0:T(1024)} %param.7) | copy-start | bytes 12292
  41.3 5.2 %collective-permute-start.6 = (f32[16,1024]{1,0:T(8,128)S(1)}, f32[16,1024]{1,0:T(8,128)S(1)}, u32[]{:S(2)}, u32[]{:S(2)}) collective-permute-start(f32[16,1024]{1,0:T(8,128)S(1)} %slice_add_fusion.4), channel_id=1, source_target_pairs={{0,2},{1,3},{2,0},{3,1},{4,6},{5,7},{6,4},{7,5},{8,10},{9,11},{10,... | collective-permute-start | bytes 196616 | tf_op jit(solution)/shard_map/ppermute | solution.py:234

commit v6 on v5

--- a/solution.py
+++ b/solution.py
@@ -260,16 +260,14 @@
     fwd2, ret2 = tiles([at0, at_far, at_cross, at_near], [own, far, cross, near], b2, two)
     back2 = shifted(ret2, -2)
     one = after(one, ret2)
-    b1 = prep(one, inv, False)
-    fwd_other, ret_other = tiles([at_cross, at_near], [cross, near], b1, one)
-    give_near = swapped(fwd_other + fwd2[:, 2 * width :], 1)
-    fwd_pair, ret_pair = tiles([at0, after(at_far, ret_other)], [own, far], b1, one)
-    back1 = shifted(ret_other + ret_pair, -1)
-    rows = fwd_pair + fwd2[:, : 2 * width]
-    rows_far = rows[:, width:] + give_near[:, :width]
+    fwd1, ret1 = tiles([at0, at_far, at_cross, at_near], [own, far, cross, near], prep(one, inv, False), one)
+    back1 = shifted(ret1, -1)
+    fwd = fwd1 + fwd2
+    give_near = swapped(fwd[:, 2 * width :], 1)
+    rows_far = fwd[:, width : 2 * width] + give_near[:, :width]
     give_far = swapped(rows_far, 2)
     total = total + tiles([at_far, after(at_cross, rows_far)], [far, cross], b0)
-    total = total + rows[:, :width] + give_near[:, width:]
+    total = total + fwd[:, :width] + give_near[:, width:]
     return total + give_far + back1 + back2 + noise[None, :] * vectors
 
 

time: 47.3 us -> 46.5 us (0.983)
  Pallas kernels: 26.9 us -> 26.4 us
    pallas_call x6 -> x5, Pallas kernels: 25.4 us -> 25 us  [tiles(): pl.pallas_call(functools.partial(tile_kernel, both, low, len(ats)), out_s...]
where the time goes in v6:
time: 46.5 us; the launch traced here: 46.4 us
  Pallas kernels  26.4 us (57%)
  starting transfers between devices  13.8 us (30%)
  waiting for transfers between devices  4.25 us (9%)
  other arithmetic  1.76 us (4%)
    pallas_call x5, Pallas kernels, tiles(): pl.pallas_call(functools.partial(tile_kernel, both, low, len(ats)), out_s...  25 us
    ppermute x4, starting transfers between devices, shifted(): lax.ppermute(value, 'blk', [(s, (s + steps) % count) for s in range(count)])  7.32 us
    ppermute x5, starting transfers between devices, swapped(): return lax.ppermute(value, 'split', [(s, s ^ mask) for s in range(count)])  6.45 us
    ppermute x4, waiting for transfers between devices, shifted(): lax.ppermute(value, 'blk', [(s, (s + steps) % count) for s in range(count)])  3.42 us
    pallas_call x5, Pallas kernels, prep(): pl.pallas_call(rows_kernel if rows else cols_kernel, out_shape=jax.ShapeD...  1.15 us
    select_n x1, other arithmetic, body(): jnp.where(row < DIMS, jnp.pad(points, ((0, RHS), (0, 0))), jnp.pad(vector...  1.03 us
  transfers between devices with their start and end apart: 9, of which 2 were waited for; matrix products, arithmetic and copies ran while one was open for 0% of the time, Pallas kernels for 37%

profile of v6, /device:TPU:1, one launch (start us, length us, event | category | flops | bytes accessed | tf_op | source)
XLA Modules:
  0.0 46.4 jit_solution(7209547829582782450)
XLA Ops:
  0.0 1.0 %pad_select_fusion.x_ref.refs_1_.refs_4_ = f32[48,1024]{1,0:T(8,128)S(1)} fusion(f32[16,1024]{1,0:T(8,128)} %param.5, f32[32,1024]{1,0:T(8,128)} %param.4, pred[48]{0:T(512)(128)(4,1)S(1)} %iota_compare_fusion), kind=kLoop, calls=%fused_computation | loop fusion | flops 49152 | bytes 393264 | tf_op jit(solution)/shard_map/jit(_where)/select_n | solution.py:243
  1.0 3.3 %collective-permute-start = (f32[48,1024]{1,0:T(8,128)S(1)}, f32[48,1024]{1,0:T(8,128)S(1)}, u32[]{:S(2)}, u32[]{:S(2)}) collective-permute-start(f32[48,1024]{1,0:T(8,128)S(1)} %pad_select_fusion.x_ref.refs_1_.refs_4_), channel_id=1, source_target_pairs={{0,1},{1,0},{2,3},{3,2},{4,5},{5,4},{6,7},{7,6},{8,9},{9,8},{10,11... | collective-permute-start | bytes 589832 | tf_op jit(solution)/shard_map/ppermute | solution.py:234
  4.4 1.1 %collective-permute-start.3 = (f32[48,1024]{1,0:T(8,128)S(1)}, f32[48,1024]{1,0:T(8,128)S(1)}, u32[]{:S(2)}, u32[]{:S(2)}) collective-permute-start(f32[48,1024]{1,0:T(8,128)S(1)} %pad_select_fusion.x_ref.refs_1_.refs_4_), channel_id=1, source_target_pairs={{0,8},{4,12},{8,16},{12,20},{16,24},{20,28},{24,32},{28,36},{32,40... | collective-permute-start | bytes 589832 | tf_op jit(solution)/shard_map/ppermute | solution.py:229
  5.5 0.3 first.1
  5.8 1.9 %own.3 = f32[16,1024]{1,0:T(8,128)S(1)} custom-call(bf16[1024,256]{1,0:T(8,128)(2,1)S(1)} %get-tuple-element.19.refs_0_, f32[48,1024]{1,0:T(8,128)S(1)} %pad_select_fusion.x_ref.refs_1_.refs_4_, bf16[256,1024]{1,0:T(8,128)(2,1)S(1)} %get-tuple-element.20.refs_2_.refs_4_), custom_call_target="tpu_custom_call" | custom-call | flops 8388608 | bytes 16384 | tf_op jit(solution)/shard_map/own/pallas_call | solution.py:205
  7.8 0.3 rows.3.refs_0_.refs_3_
  8.1 1.9 %own.4 = f32[16,1024]{1,0:T(8,128)S(1)} custom-call(bf16[1024,256]{1,0:T(8,128)(2,1)S(1)} %rows.3.refs_0_.refs_3_, f32[48,1024]{1,0:T(8,128)S(1)} %collective-permute-done.x_ref.refs_1_.refs_7_, bf16[256,1024]{1,0:T(8,128)(2,1)S(1)} %get-tuple-element.20.refs_2_.refs_4_), custom_call_target="tpu_custom_call" | custom-call | flops 8388608 | bytes 16384 | tf_op jit(solution)/shard_map/own/pallas_call | solution.py:205
  10.0 0.8 %collective-permute-done.1.x_ref.refs_5_.refs_2_ = f32[48,1024]{1,0:T(8,128)S(1)} collective-permute-done((f32[48,1024]{1,0:T(8,128)S(1)}, f32[48,1024]{1,0:T(8,128)S(1)}, u32[]{:S(2)}, u32[]{:S(2)}) %collective-permute-start.1) | collective-permute-done | bytes 196640 | tf_op jit(solution)/shard_map/ppermute | solution.py:234
  10.8 0.9 %collective-permute-start.2 = (f32[48,1024]{1,0:T(8,128)S(1)}, f32[48,1024]{1,0:T(8,128)S(1)}, u32[]{:S(2)}, u32[]{:S(2)}) collective-permute-start(f32[48,1024]{1,0:T(8,128)S(1)} %collective-permute-done.1.x_ref.refs_5_.refs_2_), channel_id=1, source_target_pairs={{0,1},{1,0},{2,3},{3,2},{4,5},{5,4},{6,7},{7,6},{8,9},{9,8},{10,11... | collective-permute-start | bytes 589832 | tf_op jit(solution)/shard_map/ppermute | solution.py:234
  11.7 1.5 %collective-permute-start.4 = (f32[48,1024]{1,0:T(8,128)S(1)}, f32[48,1024]{1,0:T(8,128)S(1)}, u32[]{:S(2)}, u32[]{:S(2)}) collective-permute-start(f32[48,1024]{1,0:T(8,128)S(1)} %pad_select_fusion.x_ref.refs_1_.refs_4_), channel_id=1, source_target_pairs={{0,4},{4,8},{8,12},{12,16},{16,20},{20,24},{24,28},{28,32},{32,36}... | collective-permute-start | bytes 589832 | tf_op jit(solution)/shard_map/ppermute | solution.py:229
  13.2 0.3 rows.4.refs_1_.refs_0_
  13.5 3.4 %collective-permute-done.3.x_ref.refs_9_ = f32[48,1024]{1,0:T(8,128)S(1)} collective-permute-done((f32[48,1024]{1,0:T(8,128)S(1)}, f32[48,1024]{1,0:T(8,128)S(1)}, u32[]{:S(2)}, u32[]{:S(2)}) %collective-permute-start.3) | collective-permute-done | bytes 196640 | tf_op jit(solution)/shard_map/ppermute | solution.py:229
  16.9 0.2 cols.2.refs_8_
  17.1 0.3 rows.5.refs_2_.refs_1_
  17.3 8.6 %both.2 = (f32[16,4096]{1,0:T(8,128)S(1)}, f32[16,1024]{1,0:T(8,128)S(1)}) custom-call(bf16[1024,256]{1,0:T(8,128)(2,1)S(1)} %get-tuple-element.19.refs_0_, bf16[1024,256]{1,0:T(8,128)(2,1)S(1)} %rows.4.refs_1_.refs_0_, bf16[1024,256]{1,0:T(8,128)(2,1)S(1)} %rows.5.refs_2_.refs_1_, bf16[1024,256]{1,0:T(8,128)(2,1)S(1)} %rows.3.refs_0_.refs_3_, ...), custom_call_target="tpu_custom_call" | custom-call | flops 33554432 | bytes 65536 | tf_op jit(solution)/shard_map/both/pallas_call | solution.py:205
  26.0 0.2 cols.3.refs_8_
  26.2 8.9 %both.3 = (f32[16,4096]{1,0:T(8,128)S(1)}, f32[16,1024]{1,0:T(8,128)S(1)}) custom-call(bf16[1024,256]{1,0:T(8,128)(2,1)S(1)} %get-tuple-element.19.refs_0_, bf16[1024,256]{1,0:T(8,128)(2,1)S(1)} %rows.4.refs_1_.refs_0_, bf16[1024,256]{1,0:T(8,128)(2,1)S(1)} %rows.5.refs_2_.refs_1_, bf16[1024,256]{1,0:T(8,128)(2,1)S(1)} %rows.3.refs_0_.refs_3_, ...), custom_call_target="tpu_custom_call" | custom-call | flops 33554432 | bytes 65536 | tf_op jit(solution)/shard_map/both/pallas_call | solution.py:205
  35.1 1.0 %collective-permute-start.5 = (f32[16,2048]{1,0:T(8,128)S(1)}, f32[16,2048]{1,0:T(8,128)S(1)}, u32[]{:S(2)}, u32[]{:S(2)}) collective-permute-start(f32[16,2048]{1,0:T(8,128)S(1)} %slice.21), channel_id=1, source_target_pairs={{0,1},{1,0},{2,3},{3,2},{4,5},{5,4},{6,7},{7,6},{8,9},{9,8},{10,11... | collective-permute-start | bytes 393224 | tf_op jit(solution)/shard_map/ppermute | solution.py:234
  36.0 3.6 %collective-permute-start.8 = (f32[16,1024]{1,0:T(8,128)S(1)}, f32[16,1024]{1,0:T(8,128)S(1)}, u32[]{:S(2)}, u32[]{:S(2)}) collective-permute-start(f32[16,1024]{1,0:T(8,128)S(1)} %get-tuple-element.27), channel_id=1, source_target_pairs={{0,248},{4,252},{8,0},{12,4},{16,8},{20,12},{24,16},{28,20},{32,24... | collective-permute-start | bytes 196616 | tf_op jit(solution)/shard_map/ppermute | solution.py:229
  39.6 1.1 %collective-permute-start.7 = (f32[16,1024]{1,0:T(8,128)S(1)}, f32[16,1024]{1,0:T(8,128)S(1)}, u32[]{:S(2)}, u32[]{:S(2)}) collective-permute-start(f32[16,1024]{1,0:T(8,128)S(1)} %get-tuple-element.32), channel_id=1, source_target_pairs={{0,252},{4,0},{8,4},{12,8},{16,12},{20,16},{24,20},{28,24},{32,28}... | collective-permute-start | bytes 196616 | tf_op jit(solution)/shard_map/ppermute | solution.py:229
  40.8 1.3 %collective-permute-start.6 = (f32[16,1024]{1,0:T(8,128)S(1)}, f32[16,1024]{1,0:T(8,128)S(1)}, u32[]{:S(2)}, u32[]{:S(2)}) collective-permute-start(f32[16,1024]{1,0:T(8,128)S(1)} %slice_add_fusion.2), channel_id=1, source_target_pairs={{0,2},{1,3},{2,0},{3,1},{4,6},{5,7},{6,4},{7,5},{8,10},{9,11},{10,... | collective-permute-start | bytes 196616 | tf_op jit(solution)/shard_map/ppermute | solution.py:234
  42.1 3.6 %own.5 = f32[16,1024]{1,0:T(8,128)S(1)} custom-call(bf16[1024,256]{1,0:T(8,128)(2,1)S(1)} %rows.4.refs_1_.refs_0_, bf16[1024,256]{1,0:T(8,128)(2,1)S(1)} %rows.5.refs_2_.refs_1_, f32[48,1024]{1,0:T(8,128)S(1)} %collective-permute-done.1.x_ref.refs_5_.refs_2_, f32[48,1024]{1,0:T(8,128)S(1)} %collective-permute-done.2.x_ref.refs_6_.refs_3_, ...), custom_call_target="tpu_custom_call" | custom-call | flops 16777216 | bytes 32768 | tf_op jit(solution)/shard_map/own/pallas_call | solution.py:205
  45.7 0.0 collective-permute-done.7
  45.7 0.7 %fusion.3 = f32[16,1024]{1,0:T(8,128)} fusion(f32[16,1024]{1,0:T(8,128)S(1)} %collective-permute-done.8, f32[16,1024]{1,0:T(8,128)S(1)} %collective-permute-done.7, f32[16,1024]{1,0:T(8,128)S(1)} %collective-permute-done.6, f32[16,2048]{1,0:T(8,128)S(1)} %collective-permute-done.5, f32[16,4096]{1,0:T(8,128)S(1)} %add.35, f32[16,1024]{1,0:T(8,128)S(1)} %copy-done.1, ...), kind=kLoop, calls=%fused_computation.5 | loop fusion | flops 131072 | bytes 593920 | tf_op jit(solution)/shard_map/add | solution.py:271
  (18 shorter events, 0.1 us)
Async XLA Ops:
  1.0 4.5 %copy-start = (f32[32]{0:T(128)S(1)}, f32[32]{0:T(128)}, u32[]{:S(2)}) copy-start(f32[32]{0:T(128)} %param.6) | copy-start | bytes 388
  1.0 6.7 %collective-permute-start = (f32[48,1024]{1,0:T(8,128)S(1)}, f32[48,1024]{1,0:T(8,128)S(1)}, u32[]{:S(2)}, u32[]{:S(2)}) collective-permute-start(f32[48,1024]{1,0:T(8,128)S(1)} %pad_select_fusion.x_ref.refs_1_.refs_4_), channel_id=1, source_target_pairs={{0,1},{1,0},{2,3},{3,2},{4,5},{5,4},{6,7},{7,6},{8,9},{9,8},{10,11... | collective-permute-start | bytes 589832 | tf_op jit(solution)/shard_map/ppermute | solution.py:234
  4.4 6.5 %collective-permute-start.1 = (f32[48,1024]{1,0:T(8,128)S(1)}, f32[48,1024]{1,0:T(8,128)S(1)}, u32[]{:S(2)}, u32[]{:S(2)}) collective-permute-start(f32[48,1024]{1,0:T(8,128)S(1)} %pad_select_fusion.x_ref.refs_1_.refs_4_), channel_id=1, source_target_pairs={{0,2},{1,3},{2,0},{3,1},{4,6},{5,7},{6,4},{7,5},{8,10},{9,11},{10,... | collective-permute-start | bytes 589832 | tf_op jit(solution)/shard_map/ppermute | solution.py:234
  4.4 12.5 %collective-permute-start.3 = (f32[48,1024]{1,0:T(8,128)S(1)}, f32[48,1024]{1,0:T(8,128)S(1)}, u32[]{:S(2)}, u32[]{:S(2)}) collective-permute-start(f32[48,1024]{1,0:T(8,128)S(1)} %pad_select_fusion.x_ref.refs_1_.refs_4_), channel_id=1, source_target_pairs={{0,8},{4,12},{8,16},{12,20},{16,24},{20,28},{24,32},{28,36},{32,40... | collective-permute-start | bytes 589832 | tf_op jit(solution)/shard_map/ppermute | solution.py:229
  10.8 6.2 %collective-permute-start.2 = (f32[48,1024]{1,0:T(8,128)S(1)}, f32[48,1024]{1,0:T(8,128)S(1)}, u32[]{:S(2)}, u32[]{:S(2)}) collective-permute-start(f32[48,1024]{1,0:T(8,128)S(1)} %collective-permute-done.1.x_ref.refs_5_.refs_2_), channel_id=1, source_target_pairs={{0,1},{1,0},{2,3},{3,2},{4,5},{5,4},{6,7},{7,6},{8,9},{9,8},{10,11... | collective-permute-start | bytes 589832 | tf_op jit(solution)/shard_map/ppermute | solution.py:234
  11.7 14.3 %collective-permute-start.4 = (f32[48,1024]{1,0:T(8,128)S(1)}, f32[48,1024]{1,0:T(8,128)S(1)}, u32[]{:S(2)}, u32[]{:S(2)}) collective-permute-start(f32[48,1024]{1,0:T(8,128)S(1)} %pad_select_fusion.x_ref.refs_1_.refs_4_), channel_id=1, source_target_pairs={{0,4},{4,8},{8,12},{12,16},{16,20},{20,24},{24,28},{28,32},{32,36}... | collective-permute-start | bytes 589832 | tf_op jit(solution)/shard_map/ppermute | solution.py:229
  35.1 5.7 %collective-permute-start.5 = (f32[16,2048]{1,0:T(8,128)S(1)}, f32[16,2048]{1,0:T(8,128)S(1)}, u32[]{:S(2)}, u32[]{:S(2)}) collective-permute-start(f32[16,2048]{1,0:T(8,128)S(1)} %slice.21), channel_id=1, source_target_pairs={{0,1},{1,0},{2,3},{3,2},{4,5},{5,4},{6,7},{7,6},{8,9},{9,8},{10,11... | collective-permute-start | bytes 393224 | tf_op jit(solution)/shard_map/ppermute | solution.py:234
  36.0 9.6 %collective-permute-start.8 = (f32[16,1024]{1,0:T(8,128)S(1)}, f32[16,1024]{1,0:T(8,128)S(1)}, u32[]{:S(2)}, u32[]{:S(2)}) collective-permute-start(f32[16,1024]{1,0:T(8,128)S(1)} %get-tuple-element.27), channel_id=1, source_target_pairs={{0,248},{4,252},{8,0},{12,4},{16,8},{20,12},{24,16},{28,20},{32,24... | collective-permute-start | bytes 196616 | tf_op jit(solution)/shard_map/ppermute | solution.py:229
  39.6 6.1 %collective-permute-start.7 = (f32[16,1024]{1,0:T(8,128)S(1)}, f32[16,1024]{1,0:T(8,128)S(1)}, u32[]{:S(2)}, u32[]{:S(2)}) collective-permute-start(f32[16,1024]{1,0:T(8,128)S(1)} %get-tuple-element.32), channel_id=1, source_target_pairs={{0,252},{4,0},{8,4},{12,8},{16,12},{20,16},{24,20},{28,24},{32,28}... | collective-permute-start | bytes 196616 | tf_op jit(solution)/shard_map/ppermute | solution.py:229
  40.8 4.9 %copy-start.1 = (f32[16,1024]{1,0:T(8,128)S(1)}, f32[16,1024]{1,0:T(8,128)}, u32[]{:S(2)}) copy-start(f32[16,1024]{1,0:T(8,128)} %param.5) | copy-start | bytes 196612
  40.8 4.9 %copy-start.2 = (f32[1024]{0:T(1024)S(1)}, f32[1024]{0:T(1024)}, u32[]{:S(2)}) copy-start(f32[1024]{0:T(1024)} %param.7) | copy-start | bytes 12292
  40.8 4.9 %collective-permute-start.6 = (f32[16,1024]{1,0:T(8,128)S(1)}, f32[16,1024]{1,0:T(8,128)S(1)}, u32[]{:S(2)}, u32[]{:S(2)}) collective-permute-start(f32[16,1024]{1,0:T(8,128)S(1)} %slice_add_fusion.2), channel_id=1, source_target_pairs={{0,2},{1,3},{2,0},{3,1},{4,6},{5,7},{6,4},{7,5},{8,10},{9,11},{10,... | collective-permute-start | bytes 196616 | tf_op jit(solution)/shard_map/ppermute | solution.py:234

commit v7 on v6

--- a/solution.py
+++ b/solution.py
@@ -58,6 +58,11 @@
     return jnp.concatenate([hi, hi, mid, hi, mid, lo, norm_rows(sq, 3), pad], axis=0)
 
 
+def put_columns(b_ref, b):
+    for k in range(b_ref.shape[0]):
+        b_ref[k] = b[:, k * 128 : (k + 1) * 128]
+
+
 def halves(v, kind):
     hi = v.astype(kind)
     return jnp.concatenate([hi, (v - hi.astype(F32)).astype(kind)], axis=0)
@@ -96,7 +101,7 @@
     inv_col_ref[...] = jnp.broadcast_to(inv, inv_col_ref.shape)
     x = scaled(x_ref, inv)
     at_ref[...] = features(x, True).T
-    b_ref[...] = features(x, False)
+    put_columns(b_ref, features(x, False))
 
 
 def rows_kernel(x_ref, inv_ref, at_ref):
@@ -104,7 +109,7 @@
 
 
 def cols_kernel(x_ref, inv_ref, b_ref):
-    b_ref[...] = features(scaled(x_ref, inv_ref[:, :1]), False)
+    put_columns(b_ref, features(scaled(x_ref, inv_ref[:, :1]), False))
 
 
 def tile_kernel(both, low, count, *refs):
@@ -115,7 +120,7 @@
         bwd_ref = rest[0]
     vr_ref, vr_low_ref, acc_ref, even_ref, odd_ref, slot_ref = rest[6 if both else 1 :]
     part = ats[0].shape[0]
-    across, per_part = b_ref.shape[1] // TILE, part // (TILE * GROUP)
+    across, per_part = b_ref.shape[0] * 128 // TILE, part // (TILE * GROUP)
     slot_ref[0] = 0
     slot = slot_ref[0]
     if both:
@@ -131,7 +136,8 @@
     def distances(ref, group, j):
         first = group % per_part * TILE * GROUP
         rows = ats[group // per_part][first : first + TILE * GROUP, :]
-        ref[0] = jnp.maximum(dot(rows, b_ref[:, j * TILE : (j + 1) * TILE], 1, 0), 1e-30)
+        cols = jnp.concatenate([b_ref[2 * j], b_ref[2 * j + 1]], axis=1)
+        ref[0] = jnp.maximum(dot(rows, cols, 1, 0), 1e-30)
 
     def products(hi, lo, i, j):
         rows, cols = slice(i * TILE, (i + 1) * TILE), slice(j * TILE, (j + 1) * TILE)
@@ -167,7 +173,7 @@
         first_kernel,
         out_shape=(
             jax.ShapeDtypeStruct((n, DEPTH), BF16),
-            jax.ShapeDtypeStruct((DEPTH, n), BF16),
+            jax.ShapeDtypeStruct((n // 128, DEPTH, 128), BF16),
             jax.ShapeDtypeStruct((DIMS, 128), F32),
         ),
         in_specs=[VMEM, VMEM],
@@ -182,7 +188,7 @@
     n = x.shape[1]
     return pl.pallas_call(
         rows_kernel if rows else cols_kernel,
-        out_shape=jax.ShapeDtypeStruct((n, DEPTH) if rows else (DEPTH, n), BF16),
+        out_shape=jax.ShapeDtypeStruct((n, DEPTH) if rows else (n // 128, DEPTH, 128), BF16),
         in_specs=[VMEM, VMEM],
         out_specs=VMEM,
         compiler_params=PARAMS,
@@ -192,7 +198,7 @@
 
 
 def tiles(ats, vs, b, x=None):
-    n, width = len(ats) * ats[0].shape[0], b.shape[1]
+    n, width = len(ats) * ats[0].shape[0], b.shape[0] * 128
     both = x is not None
     low = F8 if both else BF16
     bwd = jax.ShapeDtypeStruct((RHS, width), F32)

time: 46.5 us -> 46 us (0.989)
  Pallas kernels: 26.4 us -> 25.9 us
    pallas_call x5, Pallas kernels: 25 us -> 24.5 us  [tiles(): pl.pallas_call(functools.partial(tile_kernel, both, low, len(ats)), out_s...]
where the time goes in v7:
time: 46 us; the launch traced here: 45.9 us
  Pallas kernels  25.9 us (56%)
  starting transfers between devices  13.7 us (30%)
  waiting for transfers between devices  4.4 us (10%)
  other arithmetic  1.76 us (4%)
    pallas_call x5, Pallas kernels, tiles(): pl.pallas_call(functools.partial(tile_kernel, both, low, len(ats)), out_s...  24.5 us
    ppermute x4, starting transfers between devices, shifted(): lax.ppermute(value, 'blk', [(s, (s + steps) % count) for s in range(count)])  7.27 us
    ppermute x5, starting transfers between devices, swapped(): return lax.ppermute(value, 'split', [(s, s ^ mask) for s in range(count)])  6.42 us
    ppermute x4, waiting for transfers between devices, shifted(): lax.ppermute(value, 'blk', [(s, (s + steps) % count) for s in range(count)])  3.49 us
    pallas_call x5, Pallas kernels, prep(): pl.pallas_call(rows_kernel if rows else cols_kernel, out_shape=jax.ShapeD...  1.09 us
    select_n x1, other arithmetic, body(): jnp.where(row < DIMS, jnp.pad(points, ((0, RHS), (0, 0))), jnp.pad(vector...  1.03 us
  transfers between devices with their start and end apart: 9, of which 2 were waited for; matrix products, arithmetic and copies ran while one was open for 0% of the time, Pallas kernels for 37%

profile of v7, /device:TPU:1, one launch (start us, length us, event | category | flops | bytes accessed | tf_op | source)
XLA Modules:
  0.0 45.9 jit_solution(4441805103372171428)
XLA Ops:
  0.0 1.0 %pad_select_fusion.x_ref.refs_1_.refs_4_ = f32[48,1024]{1,0:T(8,128)S(1)} fusion(f32[16,1024]{1,0:T(8,128)} %param.5, f32[32,1024]{1,0:T(8,128)} %param.4, pred[48]{0:T(512)(128)(4,1)S(1)} %iota_compare_fusion), kind=kLoop, calls=%fused_computation | loop fusion | flops 49152 | bytes 393264 | tf_op jit(solution)/shard_map/jit(_where)/select_n | solution.py:249
  1.0 3.3 %collective-permute-start = (f32[48,1024]{1,0:T(8,128)S(1)}, f32[48,1024]{1,0:T(8,128)S(1)}, u32[]{:S(2)}, u32[]{:S(2)}) collective-permute-start(f32[48,1024]{1,0:T(8,128)S(1)} %pad_select_fusion.x_ref.refs_1_.refs_4_), channel_id=1, source_target_pairs={{0,1},{1,0},{2,3},{3,2},{4,5},{5,4},{6,7},{7,6},{8,9},{9,8},{10,11... | collective-permute-start | bytes 589832 | tf_op jit(solution)/shard_map/ppermute | solution.py:240
  4.4 1.1 %collective-permute-start.3 = (f32[48,1024]{1,0:T(8,128)S(1)}, f32[48,1024]{1,0:T(8,128)S(1)}, u32[]{:S(2)}, u32[]{:S(2)}) collective-permute-start(f32[48,1024]{1,0:T(8,128)S(1)} %pad_select_fusion.x_ref.refs_1_.refs_4_), channel_id=1, source_target_pairs={{0,8},{4,12},{8,16},{12,20},{16,24},{20,28},{24,32},{28,36},{32,40... | collective-permute-start | bytes 589832 | tf_op jit(solution)/shard_map/ppermute | solution.py:235
  5.5 0.3 first.1
  5.8 1.9 %own.3 = f32[16,1024]{1,0:T(8,128)S(1)} custom-call(bf16[1024,256]{1,0:T(8,128)(2,1)S(1)} %get-tuple-element.19.refs_0_, f32[48,1024]{1,0:T(8,128)S(1)} %pad_select_fusion.x_ref.refs_1_.refs_4_, bf16[8,256,128]{2,1,0:T(8,128)(2,1)S(1)} %get-tuple-element.20.refs_2_.refs_4_), custom_call_target="tpu_custom_call" | custom-call | flops 8388608 | bytes 16384 | tf_op jit(solution)/shard_map/own/pallas_call | solution.py:211
  7.7 0.3 rows.3.refs_0_.refs_3_
  8.0 1.9 %own.4 = f32[16,1024]{1,0:T(8,128)S(1)} custom-call(bf16[1024,256]{1,0:T(8,128)(2,1)S(1)} %rows.3.refs_0_.refs_3_, f32[48,1024]{1,0:T(8,128)S(1)} %collective-permute-done.x_ref.refs_1_.refs_7_, bf16[8,256,128]{2,1,0:T(8,128)(2,1)S(1)} %get-tuple-element.20.refs_2_.refs_4_), custom_call_target="tpu_custom_call" | custom-call | flops 8388608 | bytes 16384 | tf_op jit(solution)/shard_map/own/pallas_call | solution.py:211
  9.9 0.9 %collective-permute-done.1.x_ref.refs_5_.refs_2_ = f32[48,1024]{1,0:T(8,128)S(1)} collective-permute-done((f32[48,1024]{1,0:T(8,128)S(1)}, f32[48,1024]{1,0:T(8,128)S(1)}, u32[]{:S(2)}, u32[]{:S(2)}) %collective-permute-start.1) | collective-permute-done | bytes 196640 | tf_op jit(solution)/shard_map/ppermute | solution.py:240
  10.8 0.9 %collective-permute-start.2 = (f32[48,1024]{1,0:T(8,128)S(1)}, f32[48,1024]{1,0:T(8,128)S(1)}, u32[]{:S(2)}, u32[]{:S(2)}) collective-permute-start(f32[48,1024]{1,0:T(8,128)S(1)} %collective-permute-done.1.x_ref.refs_5_.refs_2_), channel_id=1, source_target_pairs={{0,1},{1,0},{2,3},{3,2},{4,5},{5,4},{6,7},{7,6},{8,9},{9,8},{10,11... | collective-permute-start | bytes 589832 | tf_op jit(solution)/shard_map/ppermute | solution.py:240
  11.7 1.4 %collective-permute-start.4 = (f32[48,1024]{1,0:T(8,128)S(1)}, f32[48,1024]{1,0:T(8,128)S(1)}, u32[]{:S(2)}, u32[]{:S(2)}) collective-permute-start(f32[48,1024]{1,0:T(8,128)S(1)} %pad_select_fusion.x_ref.refs_1_.refs_4_), channel_id=1, source_target_pairs={{0,4},{4,8},{8,12},{12,16},{16,20},{20,24},{24,28},{28,32},{32,36}... | collective-permute-start | bytes 589832 | tf_op jit(solution)/shard_map/ppermute | solution.py:235
  13.1 0.3 rows.4.refs_1_.refs_0_
  13.4 3.5 %collective-permute-done.3.x_ref.refs_9_ = f32[48,1024]{1,0:T(8,128)S(1)} collective-permute-done((f32[48,1024]{1,0:T(8,128)S(1)}, f32[48,1024]{1,0:T(8,128)S(1)}, u32[]{:S(2)}, u32[]{:S(2)}) %collective-permute-start.3) | collective-permute-done | bytes 196640 | tf_op jit(solution)/shard_map/ppermute | solution.py:235
  16.9 0.1 cols.2.refs_8_
  17.0 0.3 rows.5.refs_2_.refs_1_
  17.3 8.5 %both.2 = (f32[16,4096]{1,0:T(8,128)S(1)}, f32[16,1024]{1,0:T(8,128)S(1)}) custom-call(bf16[1024,256]{1,0:T(8,128)(2,1)S(1)} %get-tuple-element.19.refs_0_, bf16[1024,256]{1,0:T(8,128)(2,1)S(1)} %rows.4.refs_1_.refs_0_, bf16[1024,256]{1,0:T(8,128)(2,1)S(1)} %rows.5.refs_2_.refs_1_, bf16[1024,256]{1,0:T(8,128)(2,1)S(1)} %rows.3.refs_0_.refs_3_, ...), custom_call_target="tpu_custom_call" | custom-call | flops 33554432 | bytes 65536 | tf_op jit(solution)/shard_map/both/pallas_call | solution.py:211
  25.8 0.1 cols.3.refs_8_
  26.0 8.7 %both.3 = (f32[16,4096]{1,0:T(8,128)S(1)}, f32[16,1024]{1,0:T(8,128)S(1)}) custom-call(bf16[1024,256]{1,0:T(8,128)(2,1)S(1)} %get-tuple-element.19.refs_0_, bf16[1024,256]{1,0:T(8,128)(2,1)S(1)} %rows.4.refs_1_.refs_0_, bf16[1024,256]{1,0:T(8,128)(2,1)S(1)} %rows.5.refs_2_.refs_1_, bf16[1024,256]{1,0:T(8,128)(2,1)S(1)} %rows.3.refs_0_.refs_3_, ...), custom_call_target="tpu_custom_call" | custom-call | flops 33554432 | bytes 65536 | tf_op jit(solution)/shard_map/both/pallas_call | solution.py:211
  34.7 1.0 %collective-permute-start.5 = (f32[16,2048]{1,0:T(8,128)S(1)}, f32[16,2048]{1,0:T(8,128)S(1)}, u32[]{:S(2)}, u32[]{:S(2)}) collective-permute-start(f32[16,2048]{1,0:T(8,128)S(1)} %slice.21), channel_id=1, source_target_pairs={{0,1},{1,0},{2,3},{3,2},{4,5},{5,4},{6,7},{7,6},{8,9},{9,8},{10,11... | collective-permute-start | bytes 393224 | tf_op jit(solution)/shard_map/ppermute | solution.py:240
  35.7 3.6 %collective-permute-start.8 = (f32[16,1024]{1,0:T(8,128)S(1)}, f32[16,1024]{1,0:T(8,128)S(1)}, u32[]{:S(2)}, u32[]{:S(2)}) collective-permute-start(f32[16,1024]{1,0:T(8,128)S(1)} %get-tuple-element.27), channel_id=1, source_target_pairs={{0,248},{4,252},{8,0},{12,4},{16,8},{20,12},{24,16},{28,20},{32,24... | collective-permute-start | bytes 196616 | tf_op jit(solution)/shard_map/ppermute | solution.py:235
  39.2 1.2 %collective-permute-start.7 = (f32[16,1024]{1,0:T(8,128)S(1)}, f32[16,1024]{1,0:T(8,128)S(1)}, u32[]{:S(2)}, u32[]{:S(2)}) collective-permute-start(f32[16,1024]{1,0:T(8,128)S(1)} %get-tuple-element.32), channel_id=1, source_target_pairs={{0,252},{4,0},{8,4},{12,8},{16,12},{20,16},{24,20},{28,24},{32,28}... | collective-permute-start | bytes 196616 | tf_op jit(solution)/shard_map/ppermute | solution.py:235
  40.4 1.3 %collective-permute-start.6 = (f32[16,1024]{1,0:T(8,128)S(1)}, f32[16,1024]{1,0:T(8,128)S(1)}, u32[]{:S(2)}, u32[]{:S(2)}) collective-permute-start(f32[16,1024]{1,0:T(8,128)S(1)} %slice_add_fusion.2), channel_id=1, source_target_pairs={{0,2},{1,3},{2,0},{3,1},{4,6},{5,7},{6,4},{7,5},{8,10},{9,11},{10,... | collective-permute-start | bytes 196616 | tf_op jit(solution)/shard_map/ppermute | solution.py:240
  41.7 3.5 %own.5 = f32[16,1024]{1,0:T(8,128)S(1)} custom-call(bf16[1024,256]{1,0:T(8,128)(2,1)S(1)} %rows.4.refs_1_.refs_0_, bf16[1024,256]{1,0:T(8,128)(2,1)S(1)} %rows.5.refs_2_.refs_1_, f32[48,1024]{1,0:T(8,128)S(1)} %collective-permute-done.1.x_ref.refs_5_.refs_2_, f32[48,1024]{1,0:T(8,128)S(1)} %collective-permute-done.2.x_ref.refs_6_.refs_3_, ...), custom_call_target="tpu_custom_call" | custom-call | flops 16777216 | bytes 32768 | tf_op jit(solution)/shard_map/own/pallas_call | solution.py:211
  45.2 0.0 collective-permute-done.7
  45.3 0.7 %fusion.3 = f32[16,1024]{1,0:T(8,128)} fusion(f32[16,1024]{1,0:T(8,128)S(1)} %collective-permute-done.8, f32[16,1024]{1,0:T(8,128)S(1)} %collective-permute-done.7, f32[16,1024]{1,0:T(8,128)S(1)} %collective-permute-done.6, f32[16,2048]{1,0:T(8,128)S(1)} %collective-permute-done.5, f32[16,4096]{1,0:T(8,128)S(1)} %add.35, f32[16,1024]{1,0:T(8,128)S(1)} %copy-done.1, ...), kind=kLoop, calls=%fused_computation.5 | loop fusion | flops 131072 | bytes 593920 | tf_op jit(solution)/shard_map/add | solution.py:277
  (18 shorter events, 0.1 us)
Async XLA Ops:
  1.0 4.5 %copy-start = (f32[32]{0:T(128)S(1)}, f32[32]{0:T(128)}, u32[]{:S(2)}) copy-start(f32[32]{0:T(128)} %param.6) | copy-start | bytes 388
  1.0 6.7 %collective-permute-start = (f32[48,1024]{1,0:T(8,128)S(1)}, f32[48,1024]{1,0:T(8,128)S(1)}, u32[]{:S(2)}, u32[]{:S(2)}) collective-permute-start(f32[48,1024]{1,0:T(8,128)S(1)} %pad_select_fusion.x_ref.refs_1_.refs_4_), channel_id=1, source_target_pairs={{0,1},{1,0},{2,3},{3,2},{4,5},{5,4},{6,7},{7,6},{8,9},{9,8},{10,11... | collective-permute-start | bytes 589832 | tf_op jit(solution)/shard_map/ppermute | solution.py:240
  4.4 6.5 %collective-permute-start.1 = (f32[48,1024]{1,0:T(8,128)S(1)}, f32[48,1024]{1,0:T(8,128)S(1)}, u32[]{:S(2)}, u32[]{:S(2)}) collective-permute-start(f32[48,1024]{1,0:T(8,128)S(1)} %pad_select_fusion.x_ref.refs_1_.refs_4_), channel_id=1, source_target_pairs={{0,2},{1,3},{2,0},{3,1},{4,6},{5,7},{6,4},{7,5},{8,10},{9,11},{10,... | collective-permute-start | bytes 589832 | tf_op jit(solution)/shard_map/ppermute | solution.py:240
  4.4 12.5 %collective-permute-start.3 = (f32[48,1024]{1,0:T(8,128)S(1)}, f32[48,1024]{1,0:T(8,128)S(1)}, u32[]{:S(2)}, u32[]{:S(2)}) collective-permute-start(f32[48,1024]{1,0:T(8,128)S(1)} %pad_select_fusion.x_ref.refs_1_.refs_4_), channel_id=1, source_target_pairs={{0,8},{4,12},{8,16},{12,20},{16,24},{20,28},{24,32},{28,36},{32,40... | collective-permute-start | bytes 589832 | tf_op jit(solution)/shard_map/ppermute | solution.py:235
  10.8 6.2 %collective-permute-start.2 = (f32[48,1024]{1,0:T(8,128)S(1)}, f32[48,1024]{1,0:T(8,128)S(1)}, u32[]{:S(2)}, u32[]{:S(2)}) collective-permute-start(f32[48,1024]{1,0:T(8,128)S(1)} %collective-permute-done.1.x_ref.refs_5_.refs_2_), channel_id=1, source_target_pairs={{0,1},{1,0},{2,3},{3,2},{4,5},{5,4},{6,7},{7,6},{8,9},{9,8},{10,11... | collective-permute-start | bytes 589832 | tf_op jit(solution)/shard_map/ppermute | solution.py:240
  11.7 14.1 %collective-permute-start.4 = (f32[48,1024]{1,0:T(8,128)S(1)}, f32[48,1024]{1,0:T(8,128)S(1)}, u32[]{:S(2)}, u32[]{:S(2)}) collective-permute-start(f32[48,1024]{1,0:T(8,128)S(1)} %pad_select_fusion.x_ref.refs_1_.refs_4_), channel_id=1, source_target_pairs={{0,4},{4,8},{8,12},{12,16},{16,20},{20,24},{24,28},{28,32},{32,36}... | collective-permute-start | bytes 589832 | tf_op jit(solution)/shard_map/ppermute | solution.py:235
  34.7 5.7 %collective-permute-start.5 = (f32[16,2048]{1,0:T(8,128)S(1)}, f32[16,2048]{1,0:T(8,128)S(1)}, u32[]{:S(2)}, u32[]{:S(2)}) collective-permute-start(f32[16,2048]{1,0:T(8,128)S(1)} %slice.21), channel_id=1, source_target_pairs={{0,1},{1,0},{2,3},{3,2},{4,5},{5,4},{6,7},{7,6},{8,9},{9,8},{10,11... | collective-permute-start | bytes 393224 | tf_op jit(solution)/shard_map/ppermute | solution.py:240
  35.7 9.5 %collective-permute-start.8 = (f32[16,1024]{1,0:T(8,128)S(1)}, f32[16,1024]{1,0:T(8,128)S(1)}, u32[]{:S(2)}, u32[]{:S(2)}) collective-permute-start(f32[16,1024]{1,0:T(8,128)S(1)} %get-tuple-element.27), channel_id=1, source_target_pairs={{0,248},{4,252},{8,0},{12,4},{16,8},{20,12},{24,16},{28,20},{32,24... | collective-permute-start | bytes 196616 | tf_op jit(solution)/shard_map/ppermute | solution.py:235
  39.2 6.0 %collective-permute-start.7 = (f32[16,1024]{1,0:T(8,128)S(1)}, f32[16,1024]{1,0:T(8,128)S(1)}, u32[]{:S(2)}, u32[]{:S(2)}) collective-permute-start(f32[16,1024]{1,0:T(8,128)S(1)} %get-tuple-element.32), channel_id=1, source_target_pairs={{0,252},{4,0},{8,4},{12,8},{16,12},{20,16},{24,20},{28,24},{32,28}... | collective-permute-start | bytes 196616 | tf_op jit(solution)/shard_map/ppermute | solution.py:235
  40.4 4.8 %copy-start.1 = (f32[16,1024]{1,0:T(8,128)S(1)}, f32[16,1024]{1,0:T(8,128)}, u32[]{:S(2)}) copy-start(f32[16,1024]{1,0:T(8,128)} %param.5) | copy-start | bytes 196612
  40.4 4.8 %copy-start.2 = (f32[1024]{0:T(1024)S(1)}, f32[1024]{0:T(1024)}, u32[]{:S(2)}) copy-start(f32[1024]{0:T(1024)} %param.7) | copy-start | bytes 12292
  40.4 4.8 %collective-permute-start.6 = (f32[16,1024]{1,0:T(8,128)S(1)}, f32[16,1024]{1,0:T(8,128)S(1)}, u32[]{:S(2)}, u32[]{:S(2)}) collective-permute-start(f32[16,1024]{1,0:T(8,128)S(1)} %slice_add_fusion.2), channel_id=1, source_target_pairs={{0,2},{1,3},{2,0},{3,1},{4,6},{5,7},{6,4},{7,5},{8,10},{9,11},{10,... | collective-permute-start | bytes 196616 | tf_op jit(solution)/shard_map/ppermute | solution.py:240

commit v8 on v7

--- a/solution.py
+++ b/solution.py
@@ -63,6 +63,10 @@
         b_ref[k] = b[:, k * 128 : (k + 1) * 128]
 
 
+def two_slabs(ref, k):
+    return jnp.concatenate([ref[2 * k], ref[2 * k + 1]], axis=1)
+
+
 def halves(v, kind):
     hi = v.astype(kind)
     return jnp.concatenate([hi, (v - hi.astype(F32)).astype(kind)], axis=0)
@@ -125,25 +129,24 @@
     slot = slot_ref[0]
     if both:
         vc, undo_c = leveled(x_ref[DIMS:, :], low)
-        vc_ref[...] = halves(vc, BF16)
-        vc_low_ref[...] = halves(vc, low)
+        put_columns(vc_ref, halves(vc, BF16))
+        put_columns(vc_low_ref, halves(vc, low))
         facc_ref[...] = jnp.zeros_like(facc_ref)
     vr, undo_r = leveled(jnp.concatenate([v[DIMS:, :] for v in vs], axis=1), low)
-    vr_ref[...] = halves(vr, BF16)
-    vr_low_ref[...] = halves(vr, low)
+    put_columns(vr_ref, halves(vr, BF16))
+    put_columns(vr_low_ref, halves(vr, low))
     acc_ref[...] = jnp.zeros_like(acc_ref)
 
     def distances(ref, group, j):
         first = group % per_part * TILE * GROUP
         rows = ats[group // per_part][first : first + TILE * GROUP, :]
-        cols = jnp.concatenate([b_ref[2 * j], b_ref[2 * j + 1]], axis=1)
-        ref[0] = jnp.maximum(dot(rows, cols, 1, 0), 1e-30)
+        ref[0] = jnp.maximum(dot(rows, two_slabs(b_ref, j), 1, 0), 1e-30)
 
     def products(hi, lo, i, j):
         rows, cols = slice(i * TILE, (i + 1) * TILE), slice(j * TILE, (j + 1) * TILE)
-        acc_ref[:, cols] += dot(vr_ref[:, rows], hi, 1, 0) + dot(vr_low_ref[:, rows], lo, 1, 0)
+        acc_ref[:, cols] += dot(two_slabs(vr_ref, i), hi, 1, 0) + dot(two_slabs(vr_low_ref, i), lo, 1, 0)
         if both:
-            facc_ref[:, rows] += dot(vc_ref[:, cols], hi, 1, 1) + dot(vc_low_ref[:, cols], lo, 1, 1)
+            facc_ref[:, rows] += dot(two_slabs(vc_ref, j), hi, 1, 1) + dot(two_slabs(vc_low_ref, j), lo, 1, 1)
 
     behind = None
     groups = [(i, j) for i in range(count * per_part) for j in range(across)]
@@ -204,8 +207,8 @@
     bwd = jax.ShapeDtypeStruct((RHS, width), F32)
     fwd = jax.ShapeDtypeStruct((RHS, n), F32)
     more = [
-        pltpu.VMEM((2 * RHS, width), BF16),
-        pltpu.VMEM((2 * RHS, width), low),
+        pltpu.VMEM((width // 128, 2 * RHS, 128), BF16),
+        pltpu.VMEM((width // 128, 2 * RHS, 128), low),
         pltpu.VMEM((2 * RHS, n), F32),
     ]
     return pl.pallas_call(
@@ -215,8 +218,8 @@
         out_specs=(VMEM, VMEM) if both else VMEM,
         scratch_shapes=(more if both else [])
         + [
-            pltpu.VMEM((2 * RHS, n), BF16),
-            pltpu.VMEM((2 * RHS, n), low),
+            pltpu.VMEM((n // 128, 2 * RHS, 128), BF16),
+            pltpu.VMEM((n // 128, 2 * RHS, 128), low),
             pltpu.VMEM((2 * RHS, width), F32),
             pltpu.VMEM((1, TILE * GROUP, TILE), F32),
             pltpu.VMEM((1, TILE * GROUP, TILE), F32),

time: 46 us -> 46.1 us (level)
  no operation moved by 1% of the time
where the time goes in v8:
time: 46.1 us; the launch traced here: 46 us
  Pallas kernels  25.9 us (56%)
  starting transfers between devices  13.7 us (30%)
  waiting for transfers between devices  4.39 us (10%)
  other arithmetic  1.76 us (4%)
    pallas_call x5, Pallas kernels, tiles(): pl.pallas_call(functools.partial(tile_kernel, both, low, len(ats)), out_s...  24.6 us
    ppermute x4, starting transfers between devices, shifted(): lax.ppermute(value, 'blk', [(s, (s + steps) % count) for s in range(count)])  7.28 us
    ppermute x5, starting transfers between devices, swapped(): return lax.ppermute(value, 'split', [(s, s ^ mask) for s in range(count)])  6.42 us
    ppermute x4, waiting for transfers between devices, shifted(): lax.ppermute(value, 'blk', [(s, (s + steps) % count) for s in range(count)])  3.49 us
    pallas_call x5, Pallas kernels, prep(): pl.pallas_call(rows_kernel if rows else cols_kernel, out_shape=jax.ShapeD...  1.09 us
    select_n x1, other arithmetic, body(): jnp.where(row < DIMS, jnp.pad(points, ((0, RHS), (0, 0))), jnp.pad(vector...  1.03 us
  transfers between devices with their start and end apart: 9, of which 2 were waited for; matrix products, arithmetic and copies ran while one was open for 0% of the time, Pallas kernels for 37%

profile of v8, /device:TPU:1, one launch (start us, length us, event | category | flops | bytes accessed | tf_op | source)
XLA Modules:
  0.0 46.0 jit_solution(2723152460466621565)
XLA Ops:
  0.0 1.0 %pad_select_fusion.x_ref.refs_1_.refs_4_ = f32[48,1024]{1,0:T(8,128)S(1)} fusion(f32[16,1024]{1,0:T(8,128)} %param.5, f32[32,1024]{1,0:T(8,128)} %param.4, pred[48]{0:T(512)(128)(4,1)S(1)} %iota_compare_fusion), kind=kLoop, calls=%fused_computation | loop fusion | flops 49152 | bytes 393264 | tf_op jit(solution)/shard_map/jit(_where)/select_n | solution.py:252
  1.0 3.3 %collective-permute-start = (f32[48,1024]{1,0:T(8,128)S(1)}, f32[48,1024]{1,0:T(8,128)S(1)}, u32[]{:S(2)}, u32[]{:S(2)}) collective-permute-start(f32[48,1024]{1,0:T(8,128)S(1)} %pad_select_fusion.x_ref.refs_1_.refs_4_), channel_id=1, source_target_pairs={{0,1},{1,0},{2,3},{3,2},{4,5},{5,4},{6,7},{7,6},{8,9},{9,8},{10,11... | collective-permute-start | bytes 589832 | tf_op jit(solution)/shard_map/ppermute | solution.py:243
  4.4 1.1 %collective-permute-start.3 = (f32[48,1024]{1,0:T(8,128)S(1)}, f32[48,1024]{1,0:T(8,128)S(1)}, u32[]{:S(2)}, u32[]{:S(2)}) collective-permute-start(f32[48,1024]{1,0:T(8,128)S(1)} %pad_select_fusion.x_ref.refs_1_.refs_4_), channel_id=1, source_target_pairs={{0,8},{4,12},{8,16},{12,20},{16,24},{20,28},{24,32},{28,36},{32,40... | collective-permute-start | bytes 589832 | tf_op jit(solution)/shard_map/ppermute | solution.py:238
  5.5 0.3 first.1
  5.8 1.9 %own.3 = f32[16,1024]{1,0:T(8,128)S(1)} custom-call(bf16[1024,256]{1,0:T(8,128)(2,1)S(1)} %get-tuple-element.19.refs_0_, f32[48,1024]{1,0:T(8,128)S(1)} %pad_select_fusion.x_ref.refs_1_.refs_4_, bf16[8,256,128]{2,1,0:T(8,128)(2,1)S(1)} %get-tuple-element.20.refs_2_.refs_4_), custom_call_target="tpu_custom_call" | custom-call | flops 8388608 | bytes 16384 | tf_op jit(solution)/shard_map/own/pallas_call | solution.py:214
  7.7 0.3 rows.3.refs_0_.refs_3_
  8.0 1.9 %own.4 = f32[16,1024]{1,0:T(8,128)S(1)} custom-call(bf16[1024,256]{1,0:T(8,128)(2,1)S(1)} %rows.3.refs_0_.refs_3_, f32[48,1024]{1,0:T(8,128)S(1)} %collective-permute-done.x_ref.refs_1_.refs_7_, bf16[8,256,128]{2,1,0:T(8,128)(2,1)S(1)} %get-tuple-element.20.refs_2_.refs_4_), custom_call_target="tpu_custom_call" | custom-call | flops 8388608 | bytes 16384 | tf_op jit(solution)/shard_map/own/pallas_call | solution.py:214
  9.9 0.9 %collective-permute-done.1.x_ref.refs_5_.refs_2_ = f32[48,1024]{1,0:T(8,128)S(1)} collective-permute-done((f32[48,1024]{1,0:T(8,128)S(1)}, f32[48,1024]{1,0:T(8,128)S(1)}, u32[]{:S(2)}, u32[]{:S(2)}) %collective-permute-start.1) | collective-permute-done | bytes 196640 | tf_op jit(solution)/shard_map/ppermute | solution.py:243
  10.8 0.9 %collective-permute-start.2 = (f32[48,1024]{1,0:T(8,128)S(1)}, f32[48,1024]{1,0:T(8,128)S(1)}, u32[]{:S(2)}, u32[]{:S(2)}) collective-permute-start(f32[48,1024]{1,0:T(8,128)S(1)} %collective-permute-done.1.x_ref.refs_5_.refs_2_), channel_id=1, source_target_pairs={{0,1},{1,0},{2,3},{3,2},{4,5},{5,4},{6,7},{7,6},{8,9},{9,8},{10,11... | collective-permute-start | bytes 589832 | tf_op jit(solution)/shard_map/ppermute | solution.py:243
  11.7 1.4 %collective-permute-start.4 = (f32[48,1024]{1,0:T(8,128)S(1)}, f32[48,1024]{1,0:T(8,128)S(1)}, u32[]{:S(2)}, u32[]{:S(2)}) collective-permute-start(f32[48,1024]{1,0:T(8,128)S(1)} %pad_select_fusion.x_ref.refs_1_.refs_4_), channel_id=1, source_target_pairs={{0,4},{4,8},{8,12},{12,16},{16,20},{20,24},{24,28},{28,32},{32,36}... | collective-permute-start | bytes 589832 | tf_op jit(solution)/shard_map/ppermute | solution.py:238
  13.1 0.3 rows.4.refs_1_.refs_0_
  13.4 3.5 %collective-permute-done.3.x_ref.refs_9_ = f32[48,1024]{1,0:T(8,128)S(1)} collective-permute-done((f32[48,1024]{1,0:T(8,128)S(1)}, f32[48,1024]{1,0:T(8,128)S(1)}, u32[]{:S(2)}, u32[]{:S(2)}) %collective-permute-start.3) | collective-permute-done | bytes 196640 | tf_op jit(solution)/shard_map/ppermute | solution.py:238
  16.9 0.1 cols.2.refs_8_
  17.0 0.3 rows.5.refs_2_.refs_1_
  17.3 8.5 %both.2 = (f32[16,4096]{1,0:T(8,128)S(1)}, f32[16,1024]{1,0:T(8,128)S(1)}) custom-call(bf16[1024,256]{1,0:T(8,128)(2,1)S(1)} %get-tuple-element.19.refs_0_, bf16[1024,256]{1,0:T(8,128)(2,1)S(1)} %rows.4.refs_1_.refs_0_, bf16[1024,256]{1,0:T(8,128)(2,1)S(1)} %rows.5.refs_2_.refs_1_, bf16[1024,256]{1,0:T(8,128)(2,1)S(1)} %rows.3.refs_0_.refs_3_, ...), custom_call_target="tpu_custom_call" | custom-call | flops 33554432 | bytes 65536 | tf_op jit(solution)/shard_map/both/pallas_call | solution.py:214
  25.8 0.1 cols.3.refs_8_
  26.0 8.7 %both.3 = (f32[16,4096]{1,0:T(8,128)S(1)}, f32[16,1024]{1,0:T(8,128)S(1)}) custom-call(bf16[1024,256]{1,0:T(8,128)(2,1)S(1)} %get-tuple-element.19.refs_0_, bf16[1024,256]{1,0:T(8,128)(2,1)S(1)} %rows.4.refs_1_.refs_0_, bf16[1024,256]{1,0:T(8,128)(2,1)S(1)} %rows.5.refs_2_.refs_1_, bf16[1024,256]{1,0:T(8,128)(2,1)S(1)} %rows.3.refs_0_.refs_3_, ...), custom_call_target="tpu_custom_call" | custom-call | flops 33554432 | bytes 65536 | tf_op jit(solution)/shard_map/both/pallas_call | solution.py:214
  34.7 1.0 %collective-permute-start.5 = (f32[16,2048]{1,0:T(8,128)S(1)}, f32[16,2048]{1,0:T(8,128)S(1)}, u32[]{:S(2)}, u32[]{:S(2)}) collective-permute-start(f32[16,2048]{1,0:T(8,128)S(1)} %slice.21), channel_id=1, source_target_pairs={{0,1},{1,0},{2,3},{3,2},{4,5},{5,4},{6,7},{7,6},{8,9},{9,8},{10,11... | collective-permute-start | bytes 393224 | tf_op jit(solution)/shard_map/ppermute | solution.py:243
  35.7 3.6 %collective-permute-start.8 = (f32[16,1024]{1,0:T(8,128)S(1)}, f32[16,1024]{1,0:T(8,128)S(1)}, u32[]{:S(2)}, u32[]{:S(2)}) collective-permute-start(f32[16,1024]{1,0:T(8,128)S(1)} %get-tuple-element.27), channel_id=1, source_target_pairs={{0,248},{4,252},{8,0},{12,4},{16,8},{20,12},{24,16},{28,20},{32,24... | collective-permute-start | bytes 196616 | tf_op jit(solution)/shard_map/ppermute | solution.py:238
  39.3 1.2 %collective-permute-start.7 = (f32[16,1024]{1,0:T(8,128)S(1)}, f32[16,1024]{1,0:T(8,128)S(1)}, u32[]{:S(2)}, u32[]{:S(2)}) collective-permute-start(f32[16,1024]{1,0:T(8,128)S(1)} %get-tuple-element.32), channel_id=1, source_target_pairs={{0,252},{4,0},{8,4},{12,8},{16,12},{20,16},{24,20},{28,24},{32,28}... | collective-permute-start | bytes 196616 | tf_op jit(solution)/shard_map/ppermute | solution.py:238
  40.5 1.3 %collective-permute-start.6 = (f32[16,1024]{1,0:T(8,128)S(1)}, f32[16,1024]{1,0:T(8,128)S(1)}, u32[]{:S(2)}, u32[]{:S(2)}) collective-permute-start(f32[16,1024]{1,0:T(8,128)S(1)} %slice_add_fusion.2), channel_id=1, source_target_pairs={{0,2},{1,3},{2,0},{3,1},{4,6},{5,7},{6,4},{7,5},{8,10},{9,11},{10,... | collective-permute-start | bytes 196616 | tf_op jit(solution)/shard_map/ppermute | solution.py:243
  41.7 3.5 %own.5 = f32[16,1024]{1,0:T(8,128)S(1)} custom-call(bf16[1024,256]{1,0:T(8,128)(2,1)S(1)} %rows.4.refs_1_.refs_0_, bf16[1024,256]{1,0:T(8,128)(2,1)S(1)} %rows.5.refs_2_.refs_1_, f32[48,1024]{1,0:T(8,128)S(1)} %collective-permute-done.1.x_ref.refs_5_.refs_2_, f32[48,1024]{1,0:T(8,128)S(1)} %collective-permute-done.2.x_ref.refs_6_.refs_3_, ...), custom_call_target="tpu_custom_call" | custom-call | flops 16777216 | bytes 32768 | tf_op jit(solution)/shard_map/own/pallas_call | solution.py:214
  45.2 0.0 collective-permute-done.7
  45.3 0.7 %fusion.3 = f32[16,1024]{1,0:T(8,128)} fusion(f32[16,1024]{1,0:T(8,128)S(1)} %collective-permute-done.8, f32[16,1024]{1,0:T(8,128)S(1)} %collective-permute-done.7, f32[16,1024]{1,0:T(8,128)S(1)} %collective-permute-done.6, f32[16,2048]{1,0:T(8,128)S(1)} %collective-permute-done.5, f32[16,4096]{1,0:T(8,128)S(1)} %add.35, f32[16,1024]{1,0:T(8,128)S(1)} %copy-done.1, ...), kind=kLoop, calls=%fused_computation.5 | loop fusion | flops 131072 | bytes 593920 | tf_op jit(solution)/shard_map/add | solution.py:280
  (18 shorter events, 0.1 us)
Async XLA Ops:
  1.0 4.5 %copy-start = (f32[32]{0:T(128)S(1)}, f32[32]{0:T(128)}, u32[]{:S(2)}) copy-start(f32[32]{0:T(128)} %param.6) | copy-start | bytes 388
  1.0 6.7 %collective-permute-start = (f32[48,1024]{1,0:T(8,128)S(1)}, f32[48,1024]{1,0:T(8,128)S(1)}, u32[]{:S(2)}, u32[]{:S(2)}) collective-permute-start(f32[48,1024]{1,0:T(8,128)S(1)} %pad_select_fusion.x_ref.refs_1_.refs_4_), channel_id=1, source_target_pairs={{0,1},{1,0},{2,3},{3,2},{4,5},{5,4},{6,7},{7,6},{8,9},{9,8},{10,11... | collective-permute-start | bytes 589832 | tf_op jit(solution)/shard_map/ppermute | solution.py:243
  4.4 6.5 %collective-permute-start.1 = (f32[48,1024]{1,0:T(8,128)S(1)}, f32[48,1024]{1,0:T(8,128)S(1)}, u32[]{:S(2)}, u32[]{:S(2)}) collective-permute-start(f32[48,1024]{1,0:T(8,128)S(1)} %pad_select_fusion.x_ref.refs_1_.refs_4_), channel_id=1, source_target_pairs={{0,2},{1,3},{2,0},{3,1},{4,6},{5,7},{6,4},{7,5},{8,10},{9,11},{10,... | collective-permute-start | bytes 589832 | tf_op jit(solution)/shard_map/ppermute | solution.py:243
  4.4 12.5 %collective-permute-start.3 = (f32[48,1024]{1,0:T(8,128)S(1)}, f32[48,1024]{1,0:T(8,128)S(1)}, u32[]{:S(2)}, u32[]{:S(2)}) collective-permute-start(f32[48,1024]{1,0:T(8,128)S(1)} %pad_select_fusion.x_ref.refs_1_.refs_4_), channel_id=1, source_target_pairs={{0,8},{4,12},{8,16},{12,20},{16,24},{20,28},{24,32},{28,36},{32,40... | collective-permute-start | bytes 589832 | tf_op jit(solution)/shard_map/ppermute | solution.py:238
  10.8 6.2 %collective-permute-start.2 = (f32[48,1024]{1,0:T(8,128)S(1)}, f32[48,1024]{1,0:T(8,128)S(1)}, u32[]{:S(2)}, u32[]{:S(2)}) collective-permute-start(f32[48,1024]{1,0:T(8,128)S(1)} %collective-permute-done.1.x_ref.refs_5_.refs_2_), channel_id=1, source_target_pairs={{0,1},{1,0},{2,3},{3,2},{4,5},{5,4},{6,7},{7,6},{8,9},{9,8},{10,11... | collective-permute-start | bytes 589832 | tf_op jit(solution)/shard_map/ppermute | solution.py:243
  11.7 14.1 %collective-permute-start.4 = (f32[48,1024]{1,0:T(8,128)S(1)}, f32[48,1024]{1,0:T(8,128)S(1)}, u32[]{:S(2)}, u32[]{:S(2)}) collective-permute-start(f32[48,1024]{1,0:T(8,128)S(1)} %pad_select_fusion.x_ref.refs_1_.refs_4_), channel_id=1, source_target_pairs={{0,4},{4,8},{8,12},{12,16},{16,20},{20,24},{24,28},{28,32},{32,36}... | collective-permute-start | bytes 589832 | tf_op jit(solution)/shard_map/ppermute | solution.py:238
  34.7 5.7 %collective-permute-start.5 = (f32[16,2048]{1,0:T(8,128)S(1)}, f32[16,2048]{1,0:T(8,128)S(1)}, u32[]{:S(2)}, u32[]{:S(2)}) collective-permute-start(f32[16,2048]{1,0:T(8,128)S(1)} %slice.21), channel_id=1, source_target_pairs={{0,1},{1,0},{2,3},{3,2},{4,5},{5,4},{6,7},{7,6},{8,9},{9,8},{10,11... | collective-permute-start | bytes 393224 | tf_op jit(solution)/shard_map/ppermute | solution.py:243
  35.7 9.6 %collective-permute-start.8 = (f32[16,1024]{1,0:T(8,128)S(1)}, f32[16,1024]{1,0:T(8,128)S(1)}, u32[]{:S(2)}, u32[]{:S(2)}) collective-permute-start(f32[16,1024]{1,0:T(8,128)S(1)} %get-tuple-element.27), channel_id=1, source_target_pairs={{0,248},{4,252},{8,0},{12,4},{16,8},{20,12},{24,16},{28,20},{32,24... | collective-permute-start | bytes 196616 | tf_op jit(solution)/shard_map/ppermute | solution.py:238
  39.3 6.0 %collective-permute-start.7 = (f32[16,1024]{1,0:T(8,128)S(1)}, f32[16,1024]{1,0:T(8,128)S(1)}, u32[]{:S(2)}, u32[]{:S(2)}) collective-permute-start(f32[16,1024]{1,0:T(8,128)S(1)} %get-tuple-element.32), channel_id=1, source_target_pairs={{0,252},{4,0},{8,4},{12,8},{16,12},{20,16},{24,20},{28,24},{32,28}... | collective-permute-start | bytes 196616 | tf_op jit(solution)/shard_map/ppermute | solution.py:238
  40.4 4.9 %copy-start.1 = (f32[16,1024]{1,0:T(8,128)S(1)}, f32[16,1024]{1,0:T(8,128)}, u32[]{:S(2)}) copy-start(f32[16,1024]{1,0:T(8,128)} %param.5) | copy-start | bytes 196612
  40.4 4.8 %copy-start.2 = (f32[1024]{0:T(1024)S(1)}, f32[1024]{0:T(1024)}, u32[]{:S(2)}) copy-start(f32[1024]{0:T(1024)} %param.7) | copy-start | bytes 12292
  40.5 4.8 %collective-permute-start.6 = (f32[16,1024]{1,0:T(8,128)S(1)}, f32[16,1024]{1,0:T(8,128)S(1)}, u32[]{:S(2)}, u32[]{:S(2)}) collective-permute-start(f32[16,1024]{1,0:T(8,128)S(1)} %slice_add_fusion.2), channel_id=1, source_target_pairs={{0,2},{1,3},{2,0},{3,1},{4,6},{5,7},{6,4},{7,5},{8,10},{9,11},{10,... | collective-permute-start | bytes 196616 | tf_op jit(solution)/shard_map/ppermute | solution.py:243
